TPU v7x, 32 devices: a whole 2x2x4 slice. The times are simulated.
32 devices in a mesh: obj: 4 (over z), dp: 2 (over core), tensor: 4 (over y, x).
Axes of the slice: x: 2, y: 2, z: 4, core: 2. Of those that a mesh axis runs over, the one named last changes fastest.
Arguments:
- tokens: bfloat16 [16, 1024, 2048], P(('obj', 'dp')), may hold values from -6 to 6
- cotangent: bfloat16 [16, 1024, 2048], P(('obj', 'dp')), may hold values from -6 to 6
- segment_ids: int32 [16, 1024], P(('obj', 'dp')), may hold values from 0 to 3, never falling along the last dimension, each value on 1 to 512 neighbouring positions
- mlm_mask: int32 [16, 1024], replicated, may hold values 0 or 1
- glm_prefix: int32 [16], replicated, may hold values from 256 to 512
- glm_span: int32 [16], replicated, may hold values from 128 to 256
- qkv_weight: bfloat16 [2048, 6144], P(None, 'tensor'), may hold values from -0.125 to 0.125
- out_weight: bfloat16 [2048, 2048], P('tensor'), may hold values from -6 to 6
- gate_weight: bfloat16 [2048, 5632], P(None, 'tensor'), may hold values from -0.125 to 0.125
- up_weight: bfloat16 [2048, 5632], P(None, 'tensor'), may hold values from -0.125 to 0.125
- down_weight: bfloat16 [5632, 2048], P('tensor'), may hold values from -0.625 to 0.625
- norm1_gain: float32 [2048], replicated, may hold values from 0.5 to 1.5
- norm1_bias: float32 [2048], replicated, may hold values from -1.8 to 1.8
- norm2_gain: float32 [2048], replicated, may hold values from 0.5 to 1.5
- norm2_bias: float32 [2048], replicated, may hold values from -1.8 to 1.8
Outputs:
- activations: bfloat16 [16, 1024, 2048], P(('obj', 'dp'))
- input_grad: bfloat16 [16, 1024, 2048], P(('obj', 'dp'))
- qkv_grad: float32 [2048, 6144], P(None, 'tensor')
- out_grad: float32 [2048, 2048], P('tensor')
- gate_grad: float32 [2048, 5632], P(None, 'tensor')
- up_grad: float32 [2048, 5632], P(None, 'tensor')
- down_grad: float32 [5632, 2048], P('tensor')
- norm1_gain_grad: float32 [2048], replicated
- norm1_bias_grad: float32 [2048], replicated
- norm2_gain_grad: float32 [2048], replicated
- norm2_bias_grad: float32 [2048], replicated
Inputs may be any that keep to these rules, and one draw needn't show every extreme that they name: `segment_ids`: each row's segment numbers never fall; a segment holds 1 to 512 positions.
All inputs are finite; a program needn't handle non-finite values.
Results may differ from a plain program's by a relative error of at most 0.025.
Values may be sent and summed in bfloat16 or wider, within the bound.
No kernel may reach another device: no remote copies, remote signals or barrier semaphores. Data moves between devices by JAX's collectives and lax.ppermute only.
A program may use at most 320 MiB of HBM per device.

v0:
```python
import math

import jax
import jax.numpy as jnp
from jax import lax
from jax.sharding import PartitionSpec as P

HEAD_DIM = 128


deep_alpha = math.sqrt(48.0)
norm_eps = 1e-05
mask_fill = -1e30


def rotary_tables(seq_length, head_width):
    half_width = head_width // 2
    frequency = jnp.exp(
        jnp.arange(half_width, dtype=jnp.float32) * (-2.0 * math.log(10000.0) / head_width)
    )
    angles = jnp.arange(seq_length, dtype=jnp.float32)[:, None] * frequency[None, :]
    angles = jnp.concatenate([angles, angles], axis=1)
    return (jnp.cos(angles), jnp.sin(angles))


def rotate(tensor_in, cosine_table, sine_table):
    half_width = tensor_in.shape[-1] // 2
    turned = jnp.concatenate([-tensor_in[..., half_width:], tensor_in[..., :half_width]], axis=-1)
    return tensor_in * cosine_table + turned * sine_table


def rotate_back(gradient, cosine_table, sine_table):
    half_width = gradient.shape[-1] // 2
    sined = gradient * sine_table
    return gradient * cosine_table + jnp.concatenate(
        [sined[..., half_width:], -sined[..., :half_width]], axis=-1
    )


def visible(segment_row, prefix_len, span_len, masked_lm):
    positions = jnp.arange(segment_row.shape[0], dtype=jnp.int32)
    query_pos = positions[:, None]
    key_pos = positions[None, :]
    same_segment = segment_row[:, None] == segment_row[None, :]
    open_keys = (
        masked_lm
        | (key_pos < prefix_len)
        | (key_pos <= query_pos) & (key_pos < prefix_len + span_len)
        | (key_pos == query_pos)
    )
    return same_segment & open_keys


def gelu_gated(gate_in, up_in):
    return jax.nn.gelu(gate_in, approximate=False) * up_in


def norm_stats(resid):
    row_mean = jnp.mean(resid, axis=-1, keepdims=True)
    centered = resid - row_mean
    variance = jnp.mean(centered * centered, axis=-1, keepdims=True)
    inv_scale = lax.rsqrt(variance + norm_eps)
    return (centered * inv_scale, inv_scale)


def norm_back(gradient, normed, inv_scale, gain_vec):
    scaled = gradient * gain_vec
    inner = jnp.mean(scaled, axis=-1, keepdims=True) + normed * jnp.mean(
        scaled * normed, axis=-1, keepdims=True
    )
    return inv_scale * (scaled - inner)


def gain_terms(gradient, normed, token_weight):
    weighted = gradient * token_weight[:, None]
    return (jnp.sum(weighted * normed, axis=0), jnp.sum(weighted, axis=0))


def weighted_outer(left_side, right_side, row_weight):
    per_row = jnp.einsum("rta,rtb->rab", left_side, right_side, preferred_element_type=jnp.float32)
    return jnp.sum(row_weight[:, None, None] * per_row, axis=0)


def to_heads(flat_rows, seq_here, heads_here):
    parts = flat_rows.reshape(seq_here, -1, heads_here, HEAD_DIM).transpose(0, 2, 1, 3)
    return parts.reshape(seq_here * heads_here, -1, HEAD_DIM)


def from_heads(stacked, seq_here, heads_here):
    seq_length = stacked.shape[1]
    parts = stacked.reshape(seq_here, heads_here, seq_length, HEAD_DIM).transpose(0, 2, 1, 3)
    return parts.reshape(seq_here * seq_length, heads_here * HEAD_DIM)


def attend(query_block, key_block, value_block, allowed_block, score_scale):
    raw_scores = jnp.dot(query_block, key_block.T, preferred_element_type=jnp.float32)
    scores = jnp.where(allowed_block, raw_scores * score_scale, mask_fill)
    row_max = jnp.max(scores, axis=1, keepdims=True)
    exponent = jnp.exp(scores - row_max)
    row_total = jnp.sum(exponent, axis=1, keepdims=True)
    soft_weights = (exponent / row_total).astype(jnp.bfloat16)
    attended = jnp.dot(soft_weights, value_block, preferred_element_type=jnp.float32)
    return (attended, (row_max + jnp.log(row_total))[:, 0])


def attend_back(
    query_block, key_block, value_block, grad_block, log_total, allowed_block, score_scale
):
    raw_scores = jnp.dot(query_block, key_block.T, preferred_element_type=jnp.float32)
    scores = jnp.where(allowed_block, raw_scores * score_scale, mask_fill)
    soft_weights = jnp.exp(scores - log_total[:, None])
    value_grad = jnp.dot(
        soft_weights.astype(jnp.bfloat16).T, grad_block, preferred_element_type=jnp.float32
    )
    weight_grad = jnp.dot(grad_block, value_block.T, preferred_element_type=jnp.float32)
    score_grad = soft_weights * (
        weight_grad - jnp.sum(soft_weights * weight_grad, axis=1, keepdims=True)
    )
    raw_grad = (score_grad * score_scale).astype(jnp.bfloat16)
    query_grad = jnp.dot(raw_grad, key_block, preferred_element_type=jnp.float32)
    key_grad = jnp.dot(raw_grad.T, query_block, preferred_element_type=jnp.float32)
    return (query_grad, key_grad, value_grad)


def body(
    tokens,
    cotangent,
    segment_ids,
    mlm_mask,
    glm_prefix,
    glm_span,
    qkv_weight,
    out_weight,
    gate_weight,
    up_weight,
    down_weight,
    norm1_gain,
    norm1_bias,
    norm2_gain,
    norm2_bias,
):
    seq_here, seq_length, model_width = tokens.shape
    token_count = seq_here * seq_length
    data_ways = lax.axis_size("dp")
    objective_ways = lax.axis_size("obj")
    heads_here = qkv_weight.shape[1] // (3 * HEAD_DIM)
    score_scale = 1.0 / math.sqrt(HEAD_DIM)
    rows_all = mlm_mask.shape[0]
    masked_limit = seq_here * data_ways * (objective_ways // 2)
    row_ids = jnp.arange(rows_all, dtype=jnp.int32)
    counts = jnp.where(row_ids < masked_limit, jnp.sum(mlm_mask, axis=1), glm_span).astype(
        jnp.float32
    )
    weight_all = counts * rows_all / jnp.sum(counts)
    first_row = (lax.axis_index("obj") * data_ways + lax.axis_index("dp")) * seq_here
    row_weight = lax.dynamic_slice_in_dim(weight_all, first_row, seq_here)
    prefix_here = lax.dynamic_slice_in_dim(glm_prefix, first_row, seq_here)
    span_here = lax.dynamic_slice_in_dim(glm_span, first_row, seq_here)
    masked_lm = first_row < masked_limit
    allowed = jax.vmap(visible, in_axes=(0, 0, 0, None))(
        segment_ids, prefix_here, span_here, masked_lm
    )
    token_weight = jnp.repeat(row_weight, seq_length)
    cosine_table, sine_table = rotary_tables(seq_length, HEAD_DIM)
    cosine_tok = jnp.tile(cosine_table, (seq_here, 1))[:, None, :]
    sine_tok = jnp.tile(sine_table, (seq_here, 1))[:, None, :]
    flat_tokens = tokens.reshape(token_count, model_width)
    tokens_float = flat_tokens.astype(jnp.float32)
    cotangent_float = cotangent.reshape(token_count, model_width).astype(jnp.float32)
    head_rows = jnp.arange(seq_here * heads_here, dtype=jnp.int32) // heads_here

    def by_rows(array):
        return array.reshape(seq_here, seq_length, -1)

    def project_heads():
        projected_rows = jnp.dot(flat_tokens, qkv_weight, preferred_element_type=jnp.float32)
        projected_rows = projected_rows.reshape(token_count, heads_here, 3, HEAD_DIM)
        queries = rotate(projected_rows[:, :, 0], cosine_tok, sine_tok).astype(jnp.bfloat16)
        keys = rotate(projected_rows[:, :, 1], cosine_tok, sine_tok).astype(jnp.bfloat16)
        values = projected_rows[:, :, 2].astype(jnp.bfloat16)
        width_here = heads_here * HEAD_DIM
        return (
            to_heads(queries.reshape(token_count, width_here), seq_here, heads_here),
            to_heads(keys.reshape(token_count, width_here), seq_here, heads_here),
            to_heads(values.reshape(token_count, width_here), seq_here, heads_here),
        )

    def gated_inputs(hidden_low):
        gate_in = jnp.dot(hidden_low, gate_weight, preferred_element_type=jnp.float32)
        up_in = jnp.dot(hidden_low, up_weight, preferred_element_type=jnp.float32)
        return (gate_in, up_in)

    queries, keys, values = project_heads()

    def forward_pair(pieces):
        query_block, key_block, value_block, row_index = pieces
        return attend(query_block, key_block, value_block, allowed[row_index], score_scale)

    attended, log_totals = lax.map(forward_pair, (queries, keys, values, head_rows))
    attended_low = from_heads(attended.astype(jnp.bfloat16), seq_here, heads_here)
    attn_partial = jnp.dot(attended_low, out_weight, preferred_element_type=jnp.float32)
    attn_branch = lax.psum(attn_partial.astype(jnp.bfloat16), "tensor").astype(jnp.float32)
    resid_one = deep_alpha * tokens_float + attn_branch
    normed_one, scale_one = norm_stats(resid_one)
    hidden = normed_one * norm1_gain + norm1_bias
    hidden_low = hidden.astype(jnp.bfloat16)
    gate_in, up_in = gated_inputs(hidden_low)
    activated_low = gelu_gated(gate_in, up_in).astype(jnp.bfloat16)
    ffn_partial = jnp.dot(activated_low, down_weight, preferred_element_type=jnp.float32)
    ffn_branch = lax.psum(ffn_partial.astype(jnp.bfloat16), "tensor").astype(jnp.float32)
    resid_two = deep_alpha * hidden + ffn_branch
    normed_two, scale_two = norm_stats(resid_two)
    activations = (normed_two * norm2_gain + norm2_bias).astype(jnp.bfloat16)
    resid_two_grad = norm_back(cotangent_float, normed_two, scale_two, norm2_gain)
    gain_two_grad, bias_two_grad = gain_terms(cotangent_float, normed_two, token_weight)
    ffn_grad_low = resid_two_grad.astype(jnp.bfloat16)
    gate_in, up_in = gated_inputs(hidden_low)
    activated, pullback = jax.vjp(gelu_gated, gate_in, up_in)
    activated_grad = jnp.dot(ffn_grad_low, down_weight.T, preferred_element_type=jnp.float32)
    gate_grad, up_grad = pullback(activated_grad)
    gate_low = gate_grad.astype(jnp.bfloat16)
    up_low = up_grad.astype(jnp.bfloat16)
    activated_low = activated.astype(jnp.bfloat16)
    down_update = weighted_outer(by_rows(activated_low), by_rows(ffn_grad_low), row_weight)
    gate_update = weighted_outer(by_rows(hidden_low), by_rows(gate_low), row_weight)
    up_update = weighted_outer(by_rows(hidden_low), by_rows(up_low), row_weight)
    gate_low, up_low, ffn_updates = (gate_low, up_low, (gate_update, up_update, down_update))
    hidden_partial = jnp.dot(gate_low, gate_weight.T, preferred_element_type=jnp.float32) + jnp.dot(
        up_low, up_weight.T, preferred_element_type=jnp.float32
    )
    hidden_grad = deep_alpha * resid_two_grad + lax.psum(
        hidden_partial.astype(jnp.bfloat16), "tensor"
    ).astype(jnp.float32)
    resid_one_grad = norm_back(hidden_grad, normed_one, scale_one, norm1_gain)
    gain_one_grad, bias_one_grad = gain_terms(hidden_grad, normed_one, token_weight)
    attn_grad_low = resid_one_grad.astype(jnp.bfloat16)
    again_queries, again_keys, again_values = project_heads()
    out_grad = jnp.dot(attn_grad_low, out_weight.T, preferred_element_type=jnp.float32).astype(
        jnp.bfloat16
    )
    out_grad_heads = to_heads(out_grad, seq_here, heads_here)

    def backward_pair(pieces):
        query_block, key_block, value_block, grad_block, log_total, row_index = pieces
        return attend_back(
            query_block,
            key_block,
            value_block,
            grad_block,
            log_total,
            allowed[row_index],
            score_scale,
        )

    query_grad, key_grad, value_grad = lax.map(
        backward_pair,
        (again_queries, again_keys, again_values, out_grad_heads, log_totals, head_rows),
    )
    head_shape = (token_count, heads_here, HEAD_DIM)
    query_back = rotate_back(
        from_heads(query_grad, seq_here, heads_here).reshape(head_shape), cosine_tok, sine_tok
    )
    key_back = rotate_back(
        from_heads(key_grad, seq_here, heads_here).reshape(head_shape), cosine_tok, sine_tok
    )
    value_back = from_heads(value_grad, seq_here, heads_here).reshape(head_shape)
    qkv_grad_low = jnp.stack([query_back, key_back, value_back], axis=2).astype(jnp.bfloat16)
    qkv_grad_low = qkv_grad_low.reshape(token_count, 3 * heads_here * HEAD_DIM)
    qkv_update = weighted_outer(by_rows(flat_tokens), by_rows(qkv_grad_low), row_weight)
    out_update = weighted_outer(by_rows(attended_low), by_rows(attn_grad_low), row_weight)
    qkv_grad_low, attn_updates = (qkv_grad_low, (qkv_update, out_update))
    input_partial = jnp.dot(qkv_grad_low, qkv_weight.T, preferred_element_type=jnp.float32)
    input_grad = deep_alpha * resid_one_grad + lax.psum(
        input_partial.astype(jnp.bfloat16), "tensor"
    ).astype(jnp.float32)
    input_low = (token_weight[:, None] * input_grad).astype(jnp.bfloat16)
    summed = (
        lax.psum(attn_updates[0].astype(jnp.bfloat16), ("obj", "dp")).astype(jnp.float32),
        lax.psum(attn_updates[1].astype(jnp.bfloat16), ("obj", "dp")).astype(jnp.float32),
        lax.psum(ffn_updates[0].astype(jnp.bfloat16), ("obj", "dp")).astype(jnp.float32),
        lax.psum(ffn_updates[1].astype(jnp.bfloat16), ("obj", "dp")).astype(jnp.float32),
        lax.psum(ffn_updates[2].astype(jnp.bfloat16), ("obj", "dp")).astype(jnp.float32),
        lax.psum(gain_one_grad.astype(jnp.bfloat16), ("obj", "dp")).astype(jnp.float32),
        lax.psum(bias_one_grad.astype(jnp.bfloat16), ("obj", "dp")).astype(jnp.float32),
        lax.psum(gain_two_grad.astype(jnp.bfloat16), ("obj", "dp")).astype(jnp.float32),
        lax.psum(bias_two_grad.astype(jnp.bfloat16), ("obj", "dp")).astype(jnp.float32),
    )
    return (
        activations.reshape(seq_here, seq_length, model_width),
        input_low.reshape(seq_here, seq_length, model_width),
        summed[0],
        summed[1],
        summed[2],
        summed[3],
        summed[4],
        summed[5],
        summed[6],
        summed[7],
        summed[8],
    )


def solution(mesh):
    in_specs = (
        P(("obj", "dp"), None, None),
        P(("obj", "dp"), None, None),
        P(("obj", "dp"), None),
        P(),
        P(),
        P(),
        P(None, "tensor"),
        P("tensor", None),
        P(None, "tensor"),
        P(None, "tensor"),
        P("tensor", None),
        P(),
        P(),
        P(),
        P(),
    )
    out_specs = (
        P(("obj", "dp"), None, None),
        P(("obj", "dp"), None, None),
        P(None, "tensor"),
        P("tensor", None),
        P(None, "tensor"),
        P(None, "tensor"),
        P("tensor", None),
        P(),
        P(),
        P(),
        P(),
    )
    return jax.shard_map(body, mesh=mesh, in_specs=in_specs, out_specs=out_specs, check_vma=False)
```

profile of v0, /device:TPU:0, one launch (start us, length us, event | category | flops | bytes accessed | tf_op | source)
XLA Modules:
  0.0 1953.0 jit_solution(18110451210896071651)
XLA Ops:
  17.5 19.0 fusion.81
  133.7 101.2 %while.28 = (s32[]{:T(128)}, bf16[8,1024,128]{2,1,0:T(8,128)(2,1)}, f32[8,1024]{1,0:T(8,128)}, s32[8]{0:T(128)S(1)}, pred[2,1024,1024]{1,2,0:T(32,128)(4,1)}, /*...) while((s32[]{:T(128)}, bf16[8,1024,128]{2,1,0:T(8,128)(2,1)}, ...), condition=%wide.region_3.4_spmd.clone, body=%wide.region_0.3_spmd.sunk.clone | while | flops 545258496 | bytes 31762600 | solution.py:199
  255.9 165.2 %all-reduce.8.cloned.1.call-done = bf16[2048,2048]{1,0:T(8,128)(2,1)} async-done(((bf16[2048,2048]{1,0:T(8,128)(2,1)}), bf16[2048,2048]{1,0:T(8,128)(2,1)}) %all-reduce.8.cloned.1.call-update) | async-done | bytes 8388624 | tf_op jit(solution)/shard_map/psum | solution.py:202
  446.2 15.9 fusion.82
  462.1 39.4 %multiply_convert_fusion.3 = (bf16[2048,1408]{1,0:T(8,128)(2,1)}, f32[2048,1408]{1,0:T(8,128)}, f32[2048,1408]{1,0:T(8,128)}) fusion(f32[2048,1408]{1,0:T(8,128)} %fusion.82, bf16[2048,2048]{1,0:T(8,128)(2,1)S(1)} %fusion.50, bf16[2048,1408]{1,0:T(8,128)(2,1)S(1)} %bitcast.330), kind=kOutput, calls=%fused_computation.87 | convolution fusion | flops 12001476608 | bytes 54525952 | tf_op jit(solution)/shard_map/dot_general | solution.py:190
  501.6 17.0 convolution_convert_fusion.1
  529.8 161.8 %all-reduce.10.cloned.1.call-done = bf16[2048,2048]{1,0:T(8,128)(2,1)} async-done(((bf16[2048,2048]{1,0:T(8,128)(2,1)}), bf16[2048,2048]{1,0:T(8,128)(2,1)}) %all-reduce.10.cloned.1.call-update) | async-done | bytes 8388624 | tf_op jit(solution)/shard_map/psum | solution.py:210
  691.6 16.8 fusion.76
  727.4 21.0 %fusion.74 = (bf16[2048,2048]{1,0:T(8,128)(2,1)}, f32[2048,2048]{1,0:T(8,128)}, bf16[2048,2048]{1,0:T(8,128)(2,1)}) fusion(f32[2048]{0:T(1024)S(1)} %broadcast_multiply_fusion.2, f32[2048,2048]{1,0:T(8,128)} %get-tuple-element.189, f32[2048]{0:T(1024)S(1)} %broadcast_multiply_fusion.3, f32[2048]{0:T(1024)S(1)} %bitcast.324, f32[2048]{0:T(1024)S(1)} %copy-done.26, ...), kind=kLoop, calls=%fused_computation.168 | loop fusion | flops 50331648 | bytes 58769408 | tf_op jit(solution)/shard_map/convert_element_type | solution.py:216
  748.4 27.5 %multiply_convert_fusion.2 = (bf16[2048,1408]{1,0:T(8,128)(2,1)}, bf16[2048,1408]{1,0:T(8,128)(2,1)}) fusion(f32[2048,1408]{1,0:T(8,128)} %get-tuple-element.191, f32[2048,1408]{1,0:T(8,128)} %fusion.82, f32[2048,1408]{1,0:T(8,128)} %get-tuple-element.225, bf16[2048,2048]{1,0:T(8,128)(2,1)} %get-tuple-element.186, bf16[1408,2048]{1,0:T(8,128)(2,1)} %param.29), kind=kOutput, calls=%fused_computation.85 | convolution fusion | flops 11863064576 | bytes 60293120 | tf_op jit(solution)/shard_map/dot_general | solution.py:219
  775.9 19.3 fusion.83
  795.2 21.6 %add_convert_fusion = bf16[2048,2048]{1,0:T(8,128)(2,1)} fusion(f32[2048,2048]{1,0:T(8,128)} %fusion.83, bf16[2048,1408]{1,0:T(8,128)(2,1)} %get-tuple-element.198, bf16[2048,1408]{1,0:T(8,128)(2,1)} %param.28), kind=kOutput, calls=%fused_computation.70 | convolution fusion | flops 11819548672 | bytes 36700160 | tf_op jit(solution)/shard_map/dot_general | solution.py:228
  823.7 21.8 %multiply_reduce_fusion.3 = bf16[2048,1408]{1,0:T(8,128)(2,1)} fusion(bf16[2,1024,2048]{2,1,0:T(8,128)(2,1)} %bitcast.298, bf16[2,1024,1408]{2,1,0:T(8,128)(2,1)} %bitcast.333, f32[2]{0:T(128)S(1)} %dynamic_slice.50), kind=kOutput, calls=%fused_computation.50 | convolution fusion | flops 11819810816 | bytes 19922952 | tf_op jit(solution)/shard_map/rta,rtb->rab/dot_general | solution.py:80
  845.5 144.3 %all-reduce.12.cloned.1.call-done = bf16[2048,2048]{1,0:T(8,128)(2,1)} async-done(((bf16[2048,2048]{1,0:T(8,128)(2,1)}), bf16[2048,2048]{1,0:T(8,128)(2,1)}) %all-reduce.12.cloned.1.call-update) | async-done | bytes 8388624 | tf_op jit(solution)/shard_map/psum | solution.py:231
  989.8 18.5 multiply_reduce_fusion.5
  1008.4 20.3 %fusion.73 = (bf16[2048,2048]{1,0:T(8,128)(2,1)}, f32[2048,2048]{1,0:T(8,128)}) fusion(f32[2048]{0:T(1024)S(1)} %broadcast_multiply_fusion, f32[2048]{0:T(1024)S(1)} %copy-done.17, bf16[2048,2048]{1,0:T(8,128)(2,1)} %all-reduce.8.cloned.1.call-done, bf16[2,1024,2048]{2,1,0:T(8,128)(2,1)} %param.19, f32[2048]{0:T(1024)S(1)} %broadcast_multiply_fusion.1, ...), kind=kLoop, calls=%fused_computation.167 | loop fusion | flops 62914560 | bytes 67149824 | tf_op jit(solution)/shard_map/convert_element_type | solution.py:236
  1044.9 130.9 %while.29 = (s32[]{:T(128)}, f32[8,1024,128]{2,1,0:T(8,128)}, f32[8,1024,128]{2,1,0:T(8,128)}, bf16[8,1024,128]{2,1,0:T(8,128)(2,1)}, s32[8]{0:T(128)S(1)}, /*in...) while((s32[]{:T(128)}, f32[8,1024,128]{2,1,0:T(8,128)}, ...), condition=%wide.region_19.20_spmd.clone, body=%wide.region_17.19_spmd.sunk.clone | while | flops 1352662016 | bytes 35939488 | solution.py:255
  1214.4 19.5 %convolution_convert_fusion = bf16[2048,2048]{1,0:T(8,128)(2,1)} fusion(bf16[2048,1536]{0,1:T(8,128)(2,1)} %bitcast.293, bf16[2048,1536]{1,0:T(8,128)(2,1)} %param.25), kind=kOutput, calls=%fused_computation.104 | convolution fusion | flops 12889096192 | bytes 20971520 | tf_op jit(solution)/shard_map/dot_general | solution.py:272
  1234.5 21.2 %multiply_reduce_fusion.2 = bf16[1408,2048]{1,0:T(8,128)(2,1)} fusion(bf16[2,1024,1408]{2,1,0:T(8,128)(2,1)} %bitcast.331, bf16[2,1024,2048]{2,1,0:T(8,128)(2,1)} %bitcast.307, f32[2]{0:T(128)S(1)} %copy-done.37), kind=kOutput, calls=%fused_computation.49 | convolution fusion | flops 11819810816 | bytes 19922952 | tf_op jit(solution)/shard_map/rta,rtb->rab/dot_general | solution.py:80
  1255.7 22.5 %multiply_reduce_fusion.4 = bf16[2048,1408]{1,0:T(8,128)(2,1)} fusion(bf16[2,1024,2048]{2,1,0:T(8,128)(2,1)} %bitcast.299, bf16[2,1024,1408]{2,1,0:T(8,128)(2,1)} %bitcast.332, f32[2]{0:T(128)S(1)} %copy-done.37), kind=kOutput, calls=%fused_computation.51 | convolution fusion | flops 11819810816 | bytes 19922952 | tf_op jit(solution)/shard_map/rta,rtb->rab/dot_general | solution.py:80
  1300.2 25.6 %multiply_reduce_fusion.1 = bf16[1536,2048]{1,0:T(8,128)(2,1)} fusion(bf16[2,1024,2048]{2,1,0:T(8,128)(2,1)} %param.19, f32[2]{0:T(128)S(1)} %copy-done.37, bf16[2,1024,1536]{1,0,2:T(2,128)(2,1)} %convert_element_type.192), kind=kOutput, calls=%fused_computation.48 | convolution fusion | flops 12894339072 | bytes 20971528 | tf_op jit(solution)/shard_map/rta,rtb->rab/dot_general | solution.py:80
  1326.6 28.9 %all-reduce = (bf16[2048]{0:T(1024)(128)(2,1)S(1)}, bf16[2048]{0:T(1024)(128)(2,1)S(1)}, bf16[2048]{0:T(1024)(128)(2,1)S(1)}, bf16[2048]{0:T(1024)(128)(2,1)S(1)}) all-reduce(bf16[2048]{0:T(1024)(128)(2,1)S(1)} %copy-done.33, bf16[2048]{0:T(1024)(128)(2,1)S(1)} %copy-done.34, ...), channel_id=1, replica_groups=mesh['obj'=4,'dp'=2,'tensor'=4] {'obj','dp'}, use_global_device_ids=true, to_apply=%region_32.33 | all-reduce | flops 8192 | bytes 32768 | tf_op jit(solution)/shard_map/psum | solution.py:283
  1357.9 49.0 %all-reduce.14.cloned.1.call-done = bf16[2048,2048]{1,0:T(8,128)(2,1)} async-done(((bf16[2048,2048]{1,0:T(8,128)(2,1)}), bf16[2048,2048]{1,0:T(8,128)(2,1)}) %all-reduce.14.cloned.1.call-update) | async-done | bytes 8388624 | tf_op jit(solution)/shard_map/psum | solution.py:273
  1418.9 495.6 %all-reduce.16.cloned.1.call-done = (bf16[2048,1536]{0,1:T(8,128)(2,1)}, bf16[512,2048]{1,0:T(8,128)(2,1)}, bf16[2048,1408]{1,0:T(8,128)(2,1)}, bf16[2048,1408]{1,0:T(8,128)(2,1)}, bf16[1408,2048]{1,0:T(8,128)(2,1)}) async-done(((bf16[2048,1536]{0,1:T(8,128)(2,1)}, bf16[512,2048]{1,0:T(8,128)(2,1)}, bf16[2048,1408]{1,0:T(8,128)(2,1)}, bf16[2048,1408]{1,0:T(8,128)(2,1)}, bf16[1408,2048]{1,0:T(8,128)(2,1)}), ...) | async-done | bytes 25690128 | tf_op jit(solution)/shard_map/psum | solution.py:278
  (331 shorter events, 515.4 us)
Async XLA Ops:
  7.2 232.2 %copy-start = (bf16[512,2048]{1,0:T(8,128)(2,1)S(1)}, bf16[512,2048]{1,0:T(8,128)(2,1)}, u32[]{:S(2)}) copy-start(bf16[512,2048]{1,0:T(8,128)(2,1)} %param.26) | copy-start | bytes 6291460
  7.2 413.9 %all-reduce.8.cloned.1.call-start = ((), (), s32[]{:S(2)}) async-start(), calls=%async_computation | async-start | bytes 16777216 | tf_op jit(solution)/shard_map/psum | solution.py:202
  108.3 19.9 %copy-start.38 = (s32[16]{0:T(128)S(1)}, s32[16]{0:T(128)}, u32[]{:S(2)}) copy-start(s32[16]{0:T(128)} %param.24) | copy-start | bytes 196
  108.3 19.9 %copy-start.40 = (s32[16]{0:T(128)S(1)}, s32[16]{0:T(128)}, u32[]{:S(2)}) copy-start(s32[16]{0:T(128)} %param.23) | copy-start | bytes 196
  108.3 20.1 %copy-start.28 = (s32[2,1024]{1,0:T(2,128)S(1)}, s32[2,1024]{1,0:T(2,128)}, u32[]{:S(2)}) copy-start(s32[2,1024]{1,0:T(2,128)} %param.21) | copy-start | bytes 24580
  246.2 445.4 %all-reduce.10.cloned.1.call-start = ((), (), s32[]{:S(2)}) async-start(), calls=%async_computation.1 | async-start | bytes 16777216 | tf_op jit(solution)/shard_map/psum | solution.py:210
  438.8 23.2 %slice-start.10 = ((s8[5767168]{0:T(1024)(128)(4,1)}), s8[4194304]{0:T(1024)(128)(4,1)S(1)}, s32[]{:S(2)}) async-start(s8[5767168]{0:T(1024)(128)(4,1)} %bitcast.329), calls=%async_computation.15 | async-start | bytes 8388608
  446.2 55.3 %slice-start.6 = ((s8[5767168]{0:T(1024)(128)(4,1)}), s8[4194304]{0:T(1024)(128)(4,1)S(1)}, s32[]{:S(2)}) async-start(s8[5767168]{0:T(1024)(128)(4,1)} %bitcast.325), calls=%async_computation.11 | async-start | bytes 8388608
  462.1 39.5 %slice-start.7 = ((s8[5767168]{0:T(1024)(128)(4,1)}), s8[1572864]{0:T(1024)(128)(4,1)S(1)}, s32[]{:S(2)}) async-start(s8[5767168]{0:T(1024)(128)(4,1)} %bitcast.325), calls=%async_computation.12 | async-start | bytes 3145728
  518.6 173.0 %copy-start.16 = (f32[2048]{0:T(1024)S(1)}, f32[2048]{0:T(1024)}, u32[]{:S(2)}) copy-start(f32[2048]{0:T(1024)} %copy-done.15) | copy-start | bytes 24580
  518.6 173.0 %copy-start.19 = (f32[2048]{0:T(1024)S(1)}, f32[2048]{0:T(1024)}, u32[]{:S(2)}) copy-start(f32[2048]{0:T(1024)} %copy-done.18) | copy-start | bytes 24580
  518.6 173.0 %copy-start.24 = (f32[2048]{0:T(1024)S(1)}, f32[2048]{0:T(1024)}, u32[]{:S(2)}) copy-start(f32[2048]{0:T(1024)} %param.30) | copy-start | bytes 24580
  518.6 173.0 %copy-start.30 = (f32[2048]{0:T(1024)S(1)}, f32[2048]{0:T(1024)}, u32[]{:S(2)}) copy-start(f32[2048]{0:T(1024)} %param.31) | copy-start | bytes 24580
  518.6 471.2 %all-reduce.12.cloned.1.call-start = ((), (), s32[]{:S(2)}) async-start(), calls=%async_computation.2 | async-start | bytes 16777216 | tf_op jit(solution)/shard_map/psum | solution.py:231
  520.9 302.8 %copy-start.36 = (f32[2]{0:T(128)}, f32[2]{0:T(128)S(1)}, u32[]{:S(2)}) copy-start(f32[2]{0:T(128)S(1)} %dynamic_slice.50) | copy-start | bytes 28
  520.9 468.9 %copy-start.21 = (f32[1,8,2,128]{3,1,2,0:T(8,128)}, f32[1,8,2,128]{3,1,2,0:T(8,128)S(1)}, u32[]{:S(2)}) copy-start(f32[1,8,2,128]{3,1,2,0:T(8,128)S(1)} %copy.115) | copy-start | bytes 24580
  816.9 590.1 %all-reduce.14.cloned.1.call-start = ((), (), s32[]{:S(2)}) async-start(), calls=%async_computation.3 | async-start | bytes 16777216 | tf_op jit(solution)/shard_map/psum | solution.py:273
  823.7 166.1 %copy-start.17 = (f32[2048]{0:T(1024)S(1)}, f32[2048]{0:T(1024)}, u32[]{:S(2)}) copy-start(f32[2048]{0:T(1024)} %copy-done.15) | copy-start | bytes 24580
  823.7 166.1 %copy-start.20 = (f32[2048]{0:T(1024)S(1)}, f32[2048]{0:T(1024)}, u32[]{:S(2)}) copy-start(f32[2048]{0:T(1024)} %copy-done.18) | copy-start | bytes 24580
  823.7 166.1 %copy-start.25 = (f32[2048]{0:T(1024)S(1)}, f32[2048]{0:T(1024)}, u32[]{:S(2)}) copy-start(f32[2048]{0:T(1024)} %param.30) | copy-start | bytes 24580
  989.8 18.5 slice-start
  989.8 18.5 slice-start.1
  1234.0 680.5 %all-reduce.16.cloned.1.call-start = ((), (), s32[]{:S(2)}) async-start(), calls=%async_computation.4 | async-start | bytes 51380224 | tf_op jit(solution)/shard_map/psum | solution.py:278
  1325.9 81.0 %copy-start.22 = (f32[1,8,2,128]{3,1,2,0:T(8,128)S(1)}, f32[1,8,2,128]{3,1,2,0:T(8,128)}, u32[]{:S(2)}) copy-start(f32[1,8,2,128]{3,1,2,0:T(8,128)} %copy-done.21) | copy-start | bytes 24580
  (43 other events, 267.8 us)
Sparse Core Ops, SparseCore 0:
  246.3 174.7 all-reduce.7
  518.8 172.7 all-reduce.9
  817.0 172.7 all-reduce.11
  1234.1 172.7 all-reduce.13
  1410.5 503.9 all-reduce.15
where the time goes:
time: 1970 us; the launch traced here: 1950 us
  waiting for transfers between devices  1020 us (52%)
  matrix products  440 us (22%)
  other arithmetic  233 us (12%)
  local copies, waits for them, and re-layouts  179 us (9%)
  loops' own time  31.3 us (2%)
  blocking collectives  28.9 us (1%)
    psum x1, waiting for transfers between devices, body(): lax.psum(attn_updates[0].astype(jnp.bfloat16), ('obj', 'dp'))  496 us
    psum x1, waiting for transfers between devices, body(): lax.psum(attn_partial.astype(jnp.bfloat16), 'tensor').astype(jnp.float32)  165 us
    psum x1, waiting for transfers between devices, body(): lax.psum(ffn_partial.astype(jnp.bfloat16), 'tensor').astype(jnp.float32)  162 us
    psum x1, waiting for transfers between devices, body(): lax.psum(hidden_partial.astype(jnp.bfloat16), 'tensor').astype(jnp.float32)  144 us
    dot_general x5, matrix products, weighted_outer(): jnp.einsum('rta,rtb->rab', left_side, right_side, preferred_element_type=...  102 us
    psum x1, waiting for transfers between devices, body(): lax.psum(input_partial.astype(jnp.bfloat16), 'tensor').astype(jnp.float32)  49 us
    dot_general x1, matrix products, gated_inputs(): up_in = jnp.dot(hidden_low, up_weight, preferred_element_type=jnp.float32)  39.4 us
  transfers between devices with their start and end apart: 5, of which 5 were waited for; matrix products, arithmetic and copies ran while one was open for 7% of the time, Pallas kernels for 0%

commit v1 on v0

v1 whole, which is shorter than its diff:
```python
import functools
import math

import jax
import jax.numpy as jnp
from jax import lax
from jax.experimental import pallas as pl
from jax.experimental.pallas import tpu as pltpu
from jax.sharding import PartitionSpec as P

HEAD_DIM = 128
deep_alpha = math.sqrt(48.0)
norm_eps = 1e-05
mask_fill = -1e30
score_scale = 1.0 / math.sqrt(HEAD_DIM)
MIB = 1024 * 1024
BF = jnp.bfloat16
F32 = jnp.float32
ANY = pl.ANY


def mm(a, b):
    return lax.dot_general(a, b, (((1,), (0,)), ((), ())), preferred_element_type=F32)


def mm_nt(a, b):
    return lax.dot_general(a, b, (((1,), (1,)), ((), ())), preferred_element_type=F32)


def mm_tn(a, b):
    return lax.dot_general(a, b, (((0,), (0,)), ((), ())), preferred_element_type=F32)


def params(mib, grid_rank=1):
    return pltpu.CompilerParams(
        vmem_limit_bytes=mib * MIB, dimension_semantics=("arbitrary",) * grid_rank
    )


def cost(flops, nbytes, trans=0):
    return pl.CostEstimate(flops=int(flops), bytes_accessed=int(nbytes), transcendentals=int(trans))


def const_spec(shape):
    zeros = (0,) * len(shape)
    return pl.BlockSpec(shape, lambda *_: zeros, pipeline_mode=pl.Buffered(1))


def rotary_tables(seq_length):
    half_width = HEAD_DIM // 2
    frequency = jnp.exp(
        jnp.arange(half_width, dtype=F32) * (-2.0 * math.log(10000.0) / HEAD_DIM)
    )
    angles = jnp.arange(seq_length, dtype=F32)[:, None] * frequency[None, :]
    sine = jnp.sin(angles)
    cosine = jnp.cos(angles)
    return jnp.concatenate([cosine, cosine], axis=1), jnp.concatenate([-sine, sine], axis=1)


def fill_bias(info_ref, segc_ref, segr_ref, bias_ref, tile):
    length = bias_ref.shape[0]
    prefix, limit = info_ref[1], info_ref[2]

    def one(step, carry):
        rows = pl.ds(pl.multiple_of(step * tile, tile), tile)
        key_pos = lax.broadcasted_iota(jnp.int32, (tile, length), 0) + step * tile
        query_pos = lax.broadcasted_iota(jnp.int32, (tile, length), 1)
        same = segc_ref[rows, :] == segr_ref[...]
        open_keys = (
            (key_pos < prefix)
            | ((key_pos <= query_pos) & (key_pos < limit))
            | (key_pos == query_pos)
        )
        bias_ref[rows, :] = jnp.where(same & open_keys, 0.0, mask_fill)
        return carry

    lax.fori_loop(0, length // tile, one, 0)


def attn_fwd_kernel(
    info_ref, x_ref, w_ref, cos_ref, sin_ref, segc_ref, segr_ref, qkv_ref, ol_ref, lse_ref, bias_ref, tile
):
    length = x_ref.shape[0]

    @pl.when(pl.program_id(0) == 0)
    def _():
        fill_bias(info_ref, segc_ref, segr_ref, bias_ref, tile)

    for step in range(length // tile):
        rows = pl.ds(step * tile, tile)
        proj = mm(x_ref[rows, :], w_ref[...])
        cosine, sine = cos_ref[rows, :], sin_ref[rows, :]
        for part in range(2):
            piece = proj[:, part * HEAD_DIM : (part + 1) * HEAD_DIM]
            turned = piece * cosine + pltpu.roll(piece, HEAD_DIM // 2, 1) * sine
            qkv_ref[rows, part * HEAD_DIM : (part + 1) * HEAD_DIM] = turned.astype(BF)
        qkv_ref[rows, 2 * HEAD_DIM :] = proj[:, 2 * HEAD_DIM :].astype(BF)
    keys = qkv_ref[:, HEAD_DIM : 2 * HEAD_DIM]
    values_t = qkv_ref[:, 2 * HEAD_DIM :].astype(F32).T.astype(BF)
    for step in range(length // tile):
        rows = pl.ds(step * tile, tile)
        queries = qkv_ref[rows, :HEAD_DIM]
        scores = mm_nt(keys, queries) * score_scale + bias_ref[:, rows]
        top = jnp.max(scores, axis=0, keepdims=True)
        exponent = jnp.exp(scores - top)
        total = jnp.sum(exponent, axis=0, keepdims=True)
        attended = mm(values_t, exponent.astype(BF)) * (1.0 / total)
        ol_ref[rows, :] = attended.T.astype(BF)
        lse_ref[:, rows] = top + jnp.log(total)


def attn_fwd(info, row, tokens, qkv_weight, cosine, sine, segc, segr):
    _, length, width = tokens.shape
    heads = qkv_weight.shape[1] // (3 * HEAD_DIM)
    tile = min(256, length)
    grid_spec = pltpu.PrefetchScalarGridSpec(
        num_scalar_prefetch=1,
        grid=(heads,),
        in_specs=[
            pl.BlockSpec((None, length, width), lambda h, *_: (row, 0, 0), pipeline_mode=pl.Buffered(1)),
            pl.BlockSpec((width, 3 * HEAD_DIM), lambda h, *_: (0, h)),
            const_spec((length, HEAD_DIM)),
            const_spec((length, HEAD_DIM)),
            const_spec((length, 1)),
            const_spec((1, length)),
        ],
        out_specs=[
            pl.BlockSpec((length, 3 * HEAD_DIM), lambda h, *_: (0, h)),
            pl.BlockSpec((length, HEAD_DIM), lambda h, *_: (0, h)),
            pl.BlockSpec((None, 1, length), lambda h, *_: (h, 0, 0)),
        ],
        scratch_shapes=[pltpu.VMEM((length, length), F32)],
    )
    return pl.pallas_call(
        functools.partial(attn_fwd_kernel, tile=tile),
        grid_spec=grid_spec,
        out_shape=[
            jax.ShapeDtypeStruct((length, heads * 3 * HEAD_DIM), BF),
            jax.ShapeDtypeStruct((length, heads * HEAD_DIM), BF),
            jax.ShapeDtypeStruct((heads, 1, length), F32),
        ],
        compiler_params=params(48),
        cost_estimate=cost(
            heads * (2 * length * width * 384 + 8 * length * length * HEAD_DIM),
            2 * length * width + 2 * width * heads * 384 + 8 * length * heads * 128,
        ),
        name="attn_fwd",
    )(info, tokens, qkv_weight, cosine, sine, segc, segr)


def attn_bwd_kernel(
    info_ref, qkv_ref, dol_ref, lse_ref, cos_ref, sin_ref, segc_ref, segr_ref, dqkv_ref,
    bias_ref, dol_nat, dk_ref, dv_ref, tile
):
    length = qkv_ref.shape[0]
    ways, block, _ = dol_ref.shape
    me = info_ref[0]

    @pl.when(pl.program_id(0) == 0)
    def _():
        fill_bias(info_ref, segc_ref, segr_ref, bias_ref, tile)

    for at in range(ways):
        dol_nat[pl.ds(at * block, block), :] = dol_ref[me ^ at]
    keys = qkv_ref[:, HEAD_DIM : 2 * HEAD_DIM]
    values = qkv_ref[:, 2 * HEAD_DIM :]
    keys_t = keys.astype(F32).T.astype(BF)
    for step in range(length // tile):
        rows = pl.ds(step * tile, tile)
        queries = qkv_ref[rows, :HEAD_DIM]
        dol = dol_nat[rows, :]
        scores = mm_nt(keys, queries) * score_scale + bias_ref[:, rows]
        probs = jnp.exp(scores - lse_ref[:, rows])
        dp = mm_nt(values, dol)
        inner = jnp.sum(probs * dp, axis=0, keepdims=True)
        draw = (probs * (dp - inner) * score_scale).astype(BF)
        dv = mm(probs.astype(BF), dol)
        dk = mm(draw, queries)
        if step == 0:
            dv_ref[...] = dv
            dk_ref[...] = dk
        else:
            dv_ref[...] += dv
            dk_ref[...] += dk
        dq = mm(keys_t, draw).T
        turned = dq * cos_ref[rows, :] - pltpu.roll(dq, HEAD_DIM // 2, 1) * sin_ref[rows, :]
        dqkv_ref[rows, :HEAD_DIM] = turned.astype(BF)
    dk = dk_ref[...]
    turned = dk * cos_ref[...] - pltpu.roll(dk, HEAD_DIM // 2, 1) * sin_ref[...]
    dqkv_ref[:, HEAD_DIM : 2 * HEAD_DIM] = turned.astype(BF)
    dqkv_ref[:, 2 * HEAD_DIM :] = dv_ref[...].astype(BF)


def attn_bwd(info, qkv, dol, lse, cosine, sine, segc, segr):
    length = qkv.shape[0]
    heads = qkv.shape[1] // (3 * HEAD_DIM)
    ways, block, _ = dol.shape
    tile = min(256, length)
    grid_spec = pltpu.PrefetchScalarGridSpec(
        num_scalar_prefetch=1,
        grid=(heads,),
        in_specs=[
            pl.BlockSpec((length, 3 * HEAD_DIM), lambda h, *_: (0, h)),
            pl.BlockSpec((ways, block, HEAD_DIM), lambda h, *_: (0, 0, h)),
            pl.BlockSpec((None, 1, length), lambda h, *_: (h, 0, 0)),
            const_spec((length, HEAD_DIM)),
            const_spec((length, HEAD_DIM)),
            const_spec((length, 1)),
            const_spec((1, length)),
        ],
        out_specs=pl.BlockSpec((length, 3 * HEAD_DIM), lambda h, *_: (0, h)),
        scratch_shapes=[
            pltpu.VMEM((length, length), F32),
            pltpu.VMEM((length, HEAD_DIM), BF),
            pltpu.VMEM((length, HEAD_DIM), F32),
            pltpu.VMEM((length, HEAD_DIM), F32),
        ],
    )
    return pl.pallas_call(
        functools.partial(attn_bwd_kernel, tile=tile),
        grid_spec=grid_spec,
        out_shape=jax.ShapeDtypeStruct(qkv.shape, BF),
        compiler_params=params(48),
        cost_estimate=cost(heads * 20 * length * length * HEAD_DIM, 16 * length * heads * 128),
        name="attn_bwd",
    )(info, qkv, dol, lse, cosine, sine, segc, segr)


def out_norm_kernel(info_ref, *refs, ways):
    ol_refs, ow_refs = refs[:ways], refs[ways : 2 * ways]
    x_ref, gain_ref, bias_ref, hl_ref, n1_ref, rstd_ref = refs[2 * ways :]
    total = x_ref[...].astype(F32) * deep_alpha
    for ol_ref, ow_ref in zip(ol_refs, ow_refs):
        total += mm(ol_ref[...], ow_ref[...])
    centered = total - jnp.mean(total, axis=1, keepdims=True)
    variance = jnp.mean(centered * centered, axis=1, keepdims=True)
    inv = lax.rsqrt(variance + norm_eps)
    normed = centered * inv
    hl_ref[...] = (normed * gain_ref[...] + bias_ref[...]).astype(BF)

    @pl.when(pl.program_id(0) == info_ref[0])
    def _():
        n1_ref[...] = normed
        rstd_ref[...] = jnp.broadcast_to(inv, rstd_ref.shape)


def out_norm(info, row, ol_pieces, ow_pieces, tokens, gain, bias):
    _, length, width = tokens.shape
    ways = len(ol_pieces)
    block = length // ways
    head_width = ol_pieces[0].shape[1]
    grid_spec = pltpu.PrefetchScalarGridSpec(
        num_scalar_prefetch=1,
        grid=(ways,),
        in_specs=[pl.BlockSpec((block, head_width), lambda i, *_: (i, 0))] * ways
        + [const_spec((head_width, width))] * ways
        + [
            pl.BlockSpec((None, block, width), lambda i, *_: (row, i, 0)),
            const_spec((1, width)),
            const_spec((1, width)),
        ],
        out_specs=[
            pl.BlockSpec((block, width), lambda i, info: (i ^ info[0], 0)),
            pl.BlockSpec((block, width), lambda i, *_: (0, 0)),
            pl.BlockSpec((block, HEAD_DIM), lambda i, *_: (0, 0)),
        ],
    )
    return pl.pallas_call(
        functools.partial(out_norm_kernel, ways=ways),
        grid_spec=grid_spec,
        out_shape=[
            jax.ShapeDtypeStruct((length, width), BF),
            jax.ShapeDtypeStruct((block, width), F32),
            jax.ShapeDtypeStruct((block, HEAD_DIM), F32),
        ],
        compiler_params=params(48),
        cost_estimate=cost(2 * length * width * width, 2 * width * width + 6 * length * width),
        name="out_norm",
    )(info, *ol_pieces, *ow_pieces, tokens, gain, bias)


def piece_shapes(ways, block, width):
    if ways == 4:
        sizes = [block] + [block // 2] * 6
    else:
        sizes = [block] * ways
    return [jax.ShapeDtypeStruct((size, width), BF) for size in sizes]


def store_pieces(at, part, refs, ways):
    if ways == 4:
        half = part.shape[0] // 2

        @pl.when(at == 0)
        def _():
            refs[0][...] = part

        for r in range(1, 4):

            @pl.when(at == r)
            def _(r=r):
                refs[2 * r - 1][...] = part[:half]
                refs[2 * r][...] = part[half:]
    else:
        for r in range(ways):

            @pl.when(at == r)
            def _(r=r):
                refs[r][...] = part


def piece_specs(shapes):
    return [pl.BlockSpec(s.shape, lambda *_: (0, 0)) for s in shapes]


def ffn_fwd_kernel(hl_ref, wg_ref, wu_ref, wd_ref, al_ref, ga_ref, gb_ref, *refs, ways):
    hidden = hl_ref[...]
    gate = mm(hidden, wg_ref[...])
    up = mm(hidden, wu_ref[...])
    cdf = 0.5 + 0.5 * lax.erf(gate * (1.0 / math.sqrt(2.0)))
    pdf = jnp.exp(gate * gate * -0.5) * (1.0 / math.sqrt(2.0 * math.pi))
    act = gate * cdf
    ga_ref[...] = (up * (cdf + gate * pdf)).astype(BF)
    gb_ref[...] = act.astype(BF)
    low = (act * up).astype(BF)
    al_ref[...] = low
    store_pieces(pl.program_id(0), mm(low, wd_ref[...]).astype(BF), refs, ways)


def ffn_fwd(hidden, gate_weight, up_weight, down_weight, ways):
    length, width = hidden.shape
    units = gate_weight.shape[1]
    block = length // ways
    tiled = lambda w: pl.BlockSpec((block, w), lambda i: (i, 0))
    shapes = piece_shapes(ways, block, width)
    out = pl.pallas_call(
        functools.partial(ffn_fwd_kernel, ways=ways),
        grid=(ways,),
        in_specs=[
            tiled(width),
            const_spec((width, units)),
            const_spec((width, units)),
            const_spec((units, width)),
        ],
        out_specs=[tiled(units)] * 3 + piece_specs(shapes),
        out_shape=[jax.ShapeDtypeStruct((length, units), BF)] * 3 + shapes,
        compiler_params=params(60),
        cost_estimate=cost(6 * length * width * units, 6 * units * width + 6 * length * units),
        name="ffn_fwd",
    )(hidden, gate_weight, up_weight, down_weight)
    return out[:3], out[3:]


def norm_two_kernel(info_ref, share_ref, *refs, n_in, ways):
    in_refs = refs[:n_in]
    cot_ref, gain_ref, bias_ref = refs[n_in : n_in + 3]
    act_ref, dffn_ref, sums_ref, held = refs[-4:]
    at = pl.program_id(0)
    if n_in == 5:
        half = held.shape[0] // 2
        for r in range(3):

            @pl.when(at == r)
            def _(r=r):
                held[...] = in_refs[r][...]

        @pl.when(at == 3)
        def _():
            held[:half] = in_refs[3][...]
            held[half:] = in_refs[4][...]
    else:
        for r in range(ways):

            @pl.when(at == r)
            def _(r=r):
                held[...] = in_refs[r][...]

    resid = held[...].astype(F32)
    centered = resid - jnp.mean(resid, axis=1, keepdims=True)
    variance = jnp.mean(centered * centered, axis=1, keepdims=True)
    inv = lax.rsqrt(variance + norm_eps)
    normed = centered * inv
    gain = gain_ref[...]
    act_ref[...] = (normed * gain + bias_ref[...]).astype(BF)
    dout = cot_ref[...].astype(F32) * share_ref[0]
    scaled = dout * gain
    inner = jnp.mean(scaled, axis=1, keepdims=True) + normed * jnp.mean(
        scaled * normed, axis=1, keepdims=True
    )
    dffn_ref[...] = (inv * (scaled - inner)).astype(BF)
    gain_sum = jnp.sum(dout * normed, axis=0, keepdims=True)
    bias_sum = jnp.sum(dout, axis=0, keepdims=True)

    @pl.when(at == 0)
    def _():
        sums_ref[0:1, :] = gain_sum
        sums_ref[1:2, :] = bias_sum

    @pl.when(at > 0)
    def _():
        sums_ref[0:1, :] += gain_sum
        sums_ref[1:2, :] += bias_sum


def norm_two(info, share, row, pieces, cotangent, gain, bias, before):
    rows, length, width = cotangent.shape
    block = pieces[0].shape[0]
    ways = length // block
    natural = pl.BlockSpec((None, block, width), lambda i, info, share: (row, i ^ info[0], 0))
    grid_spec = pltpu.PrefetchScalarGridSpec(
        num_scalar_prefetch=2,
        grid=(ways,),
        in_specs=[const_spec(p.shape) for p in pieces]
        + [natural, const_spec((1, width)), const_spec((1, width))]
        + ([pl.BlockSpec(memory_space=ANY)] if before is not None else []),
        out_specs=[
            natural,
            pl.BlockSpec((block, width), lambda i, *_: (i, 0)),
            pl.BlockSpec((2, width), lambda i, *_: (0, 0)),
        ],
        scratch_shapes=[pltpu.VMEM((block, width), BF)],
    )
    return pl.pallas_call(
        functools.partial(norm_two_kernel, n_in=len(pieces), ways=ways),
        grid_spec=grid_spec,
        out_shape=[
            jax.ShapeDtypeStruct(cotangent.shape, BF),
            jax.ShapeDtypeStruct((length, width), BF),
            jax.ShapeDtypeStruct((2, width), F32),
        ],
        input_output_aliases={len(pieces) + 5: 0} if before is not None else {},
        compiler_params=params(48),
        cost_estimate=cost(20 * length * width, 8 * length * width),
        name="norm_two",
    )(info, share, *pieces, cotangent, gain, bias, *([before] if before is not None else []))


def ffn_bwd_kernel(dffn_ref, ga_ref, gb_ref, wg_ref, wu_ref, wd_ref, dg_ref, du_ref, *refs, ways):
    dact = mm_nt(dffn_ref[...], wd_ref[...])
    dgate = (dact * ga_ref[...].astype(F32)).astype(BF)
    dup = (dact * gb_ref[...].astype(F32)).astype(BF)
    dg_ref[...] = dgate
    du_ref[...] = dup
    part = mm_nt(dgate, wg_ref[...]) + mm_nt(dup, wu_ref[...])
    store_pieces(pl.program_id(0), part.astype(BF), refs, ways)


def ffn_bwd(dffn, gate_slope, up_slope, gate_weight, up_weight, down_weight, ways):
    length, width = dffn.shape
    units = gate_weight.shape[1]
    block = length // ways
    tiled = lambda w: pl.BlockSpec((block, w), lambda i: (i, 0))
    shapes = piece_shapes(ways, block, width)
    out = pl.pallas_call(
        functools.partial(ffn_bwd_kernel, ways=ways),
        grid=(ways,),
        in_specs=[
            tiled(width),
            tiled(units),
            tiled(units),
            const_spec((width, units)),
            const_spec((width, units)),
            const_spec((units, width)),
        ],
        out_specs=[tiled(units)] * 2 + piece_specs(shapes),
        out_shape=[jax.ShapeDtypeStruct((length, units), BF)] * 2 + shapes,
        compiler_params=params(60),
        cost_estimate=cost(6 * length * width * units, 6 * units * width + 8 * length * units),
        name="ffn_bwd",
    )(dffn, gate_slope, up_slope, gate_weight, up_weight, down_weight)
    return out[0], out[1], out[2:]


def input_back_kernel(info_ref, dqkv_ref, w_ref, *refs, ways):
    part = mm_nt(dqkv_ref[...], w_ref[...])
    store_pieces(pl.program_id(0), part.astype(BF), refs, ways)


def input_back(info, dqkv, qkv_weight, ways):
    length, columns = dqkv.shape
    width = qkv_weight.shape[0]
    block = length // ways
    shapes = piece_shapes(ways, block, width)
    grid_spec = pltpu.PrefetchScalarGridSpec(
        num_scalar_prefetch=1,
        grid=(ways,),
        in_specs=[
            pl.BlockSpec((block, columns), lambda i, info: (i ^ info[0], 0)),
            const_spec((width, columns)),
        ],
        out_specs=piece_specs(shapes),
    )
    return pl.pallas_call(
        functools.partial(input_back_kernel, ways=ways),
        grid_spec=grid_spec,
        out_shape=shapes,
        compiler_params=params(48),
        cost_estimate=cost(2 * length * width * columns, 2 * width * columns + 2 * length * width),
        name="input_back",
    )(info, dqkv, qkv_weight)


def place_kernel(info_ref, *refs, n_in, ways):
    in_refs = refs[:n_in]
    out_ref = refs[-1]
    at = pl.program_id(0)
    if n_in == 5:
        half = out_ref.shape[0] // 2
        for r in range(3):

            @pl.when(at == r)
            def _(r=r):
                out_ref[...] = in_refs[r][...]

        @pl.when(at == 3)
        def _():
            out_ref[:half] = in_refs[3][...]
            out_ref[half:] = in_refs[4][...]
    else:
        for r in range(ways):

            @pl.when(at == r)
            def _(r=r):
                out_ref[...] = in_refs[r][...]


def place(info, row, pieces, shape, before):
    rows, length, width = shape
    block = pieces[0].shape[0]
    ways = length // block
    grid_spec = pltpu.PrefetchScalarGridSpec(
        num_scalar_prefetch=1,
        grid=(ways,),
        in_specs=[const_spec(p.shape) for p in pieces]
        + ([pl.BlockSpec(memory_space=ANY)] if before is not None else []),
        out_specs=pl.BlockSpec((None, block, width), lambda i, info: (row, i ^ info[0], 0)),
    )
    return pl.pallas_call(
        functools.partial(place_kernel, n_in=len(pieces), ways=ways),
        grid_spec=grid_spec,
        out_shape=jax.ShapeDtypeStruct(shape, BF),
        input_output_aliases={len(pieces) + 1: 0} if before is not None else {},
        compiler_params=params(32),
        cost_estimate=cost(0, 4 * length * width),
        name="place",
    )(info, *pieces, *([before] if before is not None else []))


def swap(array, bit, ways):
    return lax.ppermute(array, "tensor", [(i, i ^ bit) for i in range(ways)])


def gather_halves(own_a, own_b):
    xa = swap(own_a, 1, 4)
    yb = swap(own_b, 2, 4)
    xb = swap(own_b, 1, 4)
    ya = swap(own_a, 2, 4)
    ra = swap(xa, 2, 4)
    rb = swap(yb, 1, 4)
    return [(xa, xb), (ya, yb), (ra, rb)]


def gather_rel(own, ways):
    blocks = [own]
    bit = 1
    while bit < ways:
        blocks = blocks + [swap(b, bit, ways) for b in blocks]
        bit *= 2
    return blocks


def gather_tokens(own, ways):
    if ways == 4:
        half = own.shape[0] // 2
        (xa, xb), (ya, yb), (ra, rb) = gather_halves(own[:half], own[half:])
        return [own, jnp.concatenate([xa, xb]), jnp.concatenate([ya, yb]), ra, rb]
    return gather_rel(own, ways)


def join(pieces):
    return jnp.concatenate(pieces, axis=0)


def add_low(a, b):
    return (a.astype(F32) + b.astype(F32)).astype(BF)


def scatter_sum(pieces, ways):
    if ways == 4:
        own, r1a, r1b, r2a, r2b, r3a, r3b = pieces
        in3a = swap(r3a, 1, 4)
        in3b = swap(r3b, 2, 4)
        in1a = swap(r1a, 1, 4)
        in2b = swap(r2b, 2, 4)
        in2a = swap(add_low(r2a, in3a), 2, 4)
        in1b = swap(add_low(r1b, in3b), 1, 4)
        half = r1a.shape[0]
        top = own[:half].astype(F32) + in1a.astype(F32) + in2a.astype(F32)
        low = own[half:].astype(F32) + in1b.astype(F32) + in2b.astype(F32)
        return jnp.concatenate([top, low], axis=0)
    blocks = list(pieces)
    bit = ways // 2
    while bit >= 1:
        keep, send = blocks[:bit], blocks[bit:]
        blocks = [add_low(k, swap(s, bit, ways)) for k, s in zip(keep, send)]
        bit //= 2
    return blocks[0].astype(F32)


def sum_over_obj(array, ways):
    if ways != 4:
        return lax.psum(array, "obj")
    at = lax.axis_index("obj")
    one = add_low(array, lax.ppermute(array, "obj", [(0, 1), (3, 2)]))
    two = add_low(one, lax.ppermute(one, "obj", [(1, 2), (2, 1)]))
    back = lax.ppermute(two, "obj", [(1, 0), (2, 3)])
    return jnp.where((at == 0) | (at == 3), back, two)


def sum_gradient(update, data_ways, objective_ways):
    if data_ways != 2:
        return lax.psum(update, ("obj", "dp")).astype(F32)
    core = lax.axis_index("dp")
    half = update.shape[0] // 2
    other = [(0, 1), (1, 0)]
    mine = lax.dynamic_slice_in_dim(update, core * half, half)
    send = lax.dynamic_slice_in_dim(update, (1 - core) * half, half)
    mine = add_low(mine, lax.ppermute(send, "dp", other))
    mine = sum_over_obj(mine, objective_ways)
    theirs = lax.ppermute(mine, "dp", other)
    first = jnp.where(core == 0, mine, theirs)
    second = jnp.where(core == 0, theirs, mine)
    return jnp.concatenate([first, second], axis=0).astype(F32)


def body(
    tokens,
    cotangent,
    segment_ids,
    mlm_mask,
    glm_prefix,
    glm_span,
    qkv_weight,
    out_weight,
    gate_weight,
    up_weight,
    down_weight,
    norm1_gain,
    norm1_bias,
    norm2_gain,
    norm2_bias,
):
    seq_here, length, width = tokens.shape
    ways = lax.axis_size("tensor")
    data_ways = lax.axis_size("dp")
    objective_ways = lax.axis_size("obj")
    me = lax.axis_index("tensor").astype(jnp.int32)
    block = length // ways
    rows_all = mlm_mask.shape[0]
    masked_limit = seq_here * data_ways * (objective_ways // 2)
    row_ids = jnp.arange(rows_all, dtype=jnp.int32)
    counts = jnp.where(row_ids < masked_limit, jnp.sum(mlm_mask, axis=1), glm_span).astype(F32)
    weight_all = counts * rows_all / jnp.sum(counts)
    first_row = (lax.axis_index("obj") * data_ways + lax.axis_index("dp")) * seq_here
    share_here = lax.dynamic_slice_in_dim(weight_all, first_row, seq_here)
    prefix_here = lax.dynamic_slice_in_dim(glm_prefix, first_row, seq_here)
    span_here = lax.dynamic_slice_in_dim(glm_span, first_row, seq_here)
    masked_lm = first_row < masked_limit
    open_here = jnp.where(masked_lm, length, prefix_here)
    info = [jnp.stack([me, open_here[r], prefix_here[r] + span_here[r]]) for r in range(seq_here)]
    share = [share_here[r : r + 1] for r in range(seq_here)]
    cosine, sine = rotary_tables(length)
    segc = [segment_ids[r].reshape(length, 1) for r in range(seq_here)]
    segr = [segment_ids[r].reshape(1, length) for r in range(seq_here)]
    gain1, bias1 = norm1_gain.reshape(1, width), norm1_bias.reshape(1, width)
    gain2, bias2 = norm2_gain.reshape(1, width), norm2_bias.reshape(1, width)
    rows = range(seq_here)

    if ways == 4 and data_ways == 2:
        core = lax.axis_index("dp")
        half = out_weight.shape[0] // 2
        mine = lax.dynamic_slice_in_dim(out_weight, core * half, half)
        pairs = gather_halves(mine[: half // 2], mine[half // 2 :])
        ow_pieces = [out_weight]
        for a, b in pairs:
            got = jnp.concatenate([a, b])
            other = lax.ppermute(got, "dp", [(0, 1), (1, 0)])
            ow_pieces.append(
                jnp.concatenate(
                    [jnp.where(core == 0, got, other), jnp.where(core == 0, other, got)]
                )
            )
    else:
        ow_pieces = gather_rel(out_weight, ways)

    qkv, ol, lse, hl, n1, rstd1 = {}, {}, {}, {}, {}, {}
    al, slope_g, slope_u, dffn, dgate, dup = {}, {}, {}, {}, {}, {}
    r2_pieces, norm2_sums, norm1_sums, dr1, dqkv, dattn = {}, {}, {}, {}, {}, {}

    for r in rows:
        qkv[r], ol[r], lse[r] = attn_fwd(info[r], r, tokens, qkv_weight, cosine, sine, segc[r], segr[r])
    ffn_parts = {}
    for r in rows:
        if ways == 4:
            pairs = gather_halves(ol[r][: length // 2], ol[r][length // 2 :])
            ol_pieces = [ol[r]] + [jnp.concatenate(p) for p in pairs]
        else:
            ol_pieces = gather_rel(ol[r], ways)
        hl[r], n1[r], rstd1[r] = out_norm(info[r], r, ol_pieces, ow_pieces, tokens, gain1, bias1)
        (al[r], slope_g[r], slope_u[r]), ffn_parts[r] = ffn_fwd(
            hl[r], gate_weight, up_weight, down_weight, ways
        )
    for r in rows:
        total = scatter_sum(ffn_parts[r], ways)
        resid = deep_alpha * (n1[r] * gain1 + bias1) + total
        r2_pieces[r] = gather_tokens(resid.astype(BF), ways)

    activations = None
    dh_parts = {}
    for r in rows:
        activations, dffn[r], norm2_sums[r] = norm_two(
            info[r], share[r], r, r2_pieces[r], cotangent, gain2, bias2, activations
        )
        dgate[r], dup[r], dh_parts[r] = ffn_bwd(
            dffn[r], slope_g[r], slope_u[r], gate_weight, up_weight, down_weight, ways
        )

    def update(lefts, rights):
        total = None
        for r in rows:
            one = mm_tn(lefts[r], rights[r])
            total = one if total is None else total + one
        return total.astype(BF)

    def reduced(lefts, rights):
        return sum_gradient(update(lefts, rights), data_ways, objective_ways)

    down_grad = reduced(al, dffn)
    gate_grad = reduced(hl, dgate)
    up_grad = reduced(hl, dup)

    dx_parts = {}
    for r in rows:
        total = scatter_sum(dh_parts[r], ways)
        dh = deep_alpha * dffn[r][:block].astype(F32) + total
        scaled = dh * gain1
        inner = jnp.mean(scaled, axis=1, keepdims=True) + n1[r] * jnp.mean(
            scaled * n1[r], axis=1, keepdims=True
        )
        dr1[r] = rstd1[r][:, :1] * (scaled - inner)
        norm1_sums[r] = jnp.stack([jnp.sum(dh * n1[r], axis=0), jnp.sum(dh, axis=0)])
        dattn[r] = join(gather_tokens(dr1[r].astype(BF), ways))
    for r in rows:
        dol = mm_nt(dattn[r], out_weight).astype(BF).reshape(ways, block, -1)
        dqkv[r] = attn_bwd(info[r], qkv[r], dol, lse[r], cosine, sine, segc[r], segr[r])
        dx_parts[r] = input_back(info[r], dqkv[r], qkv_weight, ways)

    qkv_grad = reduced([tokens[r] for r in rows], dqkv)
    ol_rel = {}
    for r in rows:
        parts = ol[r].reshape(ways, block, -1)
        ol_rel[r] = jnp.stack(
            [lax.dynamic_index_in_dim(parts, me ^ i, 0, keepdims=False) for i in range(ways)]
        ).reshape(length, -1)
    out_grad = reduced(ol_rel, dattn)

    input_grad = None
    for r in rows:
        total = scatter_sum(dx_parts[r], ways)
        dx = (deep_alpha * dr1[r] + total).astype(BF)
        input_grad = place(info[r], r, gather_tokens(dx, ways), tokens.shape, input_grad)

    first = (me == 0).astype(F32)
    sums = jnp.concatenate(
        [sum(norm1_sums[r] for r in rows), sum(norm2_sums[r] for r in rows) * first]
    )
    sums = lax.psum(sums, ("obj", "dp", "tensor"))
    return (
        activations,
        input_grad,
        qkv_grad,
        out_grad,
        gate_grad,
        up_grad,
        down_grad,
        sums[0],
        sums[1],
        sums[2],
        sums[3],
    )


def solution(mesh):
    rows3 = P(("obj", "dp"), None, None)
    in_specs = (
        rows3,
        rows3,
        P(("obj", "dp"), None),
        P(),
        P(),
        P(),
        P(None, "tensor"),
        P("tensor", None),
        P(None, "tensor"),
        P(None, "tensor"),
        P("tensor", None),
        P(),
        P(),
        P(),
        P(),
    )
    out_specs = (
        rows3,
        rows3,
        P(None, "tensor"),
        P("tensor", None),
        P(None, "tensor"),
        P(None, "tensor"),
        P("tensor", None),
        P(),
        P(),
        P(),
        P(),
    )
    return jax.shard_map(body, mesh=mesh, in_specs=in_specs, out_specs=out_specs, check_vma=False)
```

time: 1970 us -> 1430 us (0.73)
  waiting for transfers between devices: 1020 us -> 653 us
  matrix products: 440 us -> 104 us
  Pallas kernels: 0 us -> 305 us
  local copies, waits for them, and re-layouts: 179 us -> 57.9 us
  starting transfers between devices: 9.92 us -> 125 us
  other arithmetic: 233 us -> 122 us
  loops' own time: 31.3 us -> 0 us
  blocking collectives: 28.9 us -> 51.1 us
    psum x5 -> x0, waiting for transfers between devices: 1020 us -> none  [the longest x1 496 us: body(): lax.psum(attn_updates[0].astype(jnp.bfloat16), ('obj', 'dp'))]
    ppermute x0 -> x118, waiting for transfers between devices: none -> 653 us  [the longest x90 303 us: swap(): return lax.ppermute(array, 'tensor', [(i, i ^ bit) for i in range(ways)])]
    dot_general x71 -> x12, matrix products: 440 us -> 104 us  [the longest x10 98.9 us: mm_tn(): lax.dot_general(a, b, (((0,), (0,)), ((), ())), preferred_element_type=F32)]
    pallas_call x0 -> x16, Pallas kernels: none -> 305 us  [the longest x2 61.4 us: ffn_bwd(): pl.pallas_call(functools.partial(ffn_bwd_kernel, ways=ways), grid=(ways,)...]
    ppermute x0 -> x118, starting transfers between devices: none -> 125 us  [the longest x90 93 us: swap(): return lax.ppermute(array, 'tensor', [(i, i ^ bit) for i in range(ways)])]
    reduce_sum x15 -> x1, other arithmetic: 85.6 us -> 3.31 us  [body(): jnp.sum(dh * n1[r], axis=0)]
    another operation x2 -> x0, loops' own time: 31.3 us -> none  [the longest x1 15.7 us: body(): lax.map(forward_pair, (queries, keys, values, head_rows))]
    convert_element_type x21 -> x34, other arithmetic: 98.8 us -> 70 us  [the longest x27 41 us: add_low(): return (a.astype(F32) + b.astype(F32)).astype(BF)]
  transfers between devices with their start and end apart: 5 -> 118, of which waited for: 5 -> 55; matrix products, arithmetic and copies ran while one was open for 7% -> 17% of each run, Pallas kernels for 0% -> 15%
where the time goes in v1:
time: 1430 us; the launch traced here: 1420 us
  waiting for transfers between devices  653 us (46%)
  Pallas kernels  305 us (21%)
  starting transfers between devices  125 us (9%)
  other arithmetic  122 us (9%)
  matrix products  104 us (7%)
  local copies, waits for them, and re-layouts  57.9 us (4%)
  blocking collectives  51.1 us (4%)
    ppermute x90, waiting for transfers between devices, swap(): return lax.ppermute(array, 'tensor', [(i, i ^ bit) for i in range(ways)])  303 us
    ppermute x5, waiting for transfers between devices, sum_over_obj(): back = lax.ppermute(two, 'obj', [(1, 0), (2, 3)])  208 us
    ppermute x5, waiting for transfers between devices, sum_over_obj(): one = add_low(array, lax.ppermute(array, 'obj', [(0, 1), (3, 2)]))  142 us
    dot_general x10, matrix products, mm_tn(): lax.dot_general(a, b, (((0,), (0,)), ((), ())), preferred_element_type=F32)  98.9 us
    ppermute x90, starting transfers between devices, swap(): return lax.ppermute(array, 'tensor', [(i, i ^ bit) for i in range(ways)])  93 us
    pallas_call x2, Pallas kernels, ffn_bwd(): pl.pallas_call(functools.partial(ffn_bwd_kernel, ways=ways), grid=(ways,)...  61.4 us
    pallas_call x2, Pallas kernels, ffn_fwd(): pl.pallas_call(functools.partial(ffn_fwd_kernel, ways=ways), grid=(ways,)...  60.6 us
    pallas_call x2, Pallas kernels, attn_fwd(): pl.pallas_call(functools.partial(attn_fwd_kernel, tile=tile), grid_spec=g...  54.2 us
  transfers between devices with their start and end apart: 118, of which 55 were waited for; matrix products, arithmetic and copies ran while one was open for 17% of the time, Pallas kernels for 15%

profile of v1, /device:TPU:0, one launch (start us, length us, event | category | flops | bytes accessed | tf_op | source)
XLA Modules:
  0.0 1423.2 jit_solution(14701113182056044934)
XLA Ops:
  18.5 27.0 %attn_fwd.3 = (bf16[1024,1536]{1,0:T(8,128)(2,1)S(1)}, bf16[1024,512]{1,0:T(8,128)(2,1)S(1)}, f32[4,1,1024]{2,1,0:T(1,128)S(1)}) custom-call(s32[3]{0:T(128)S(1)} %get-tuple-element.274.info_ref, bf16[2,1024,2048]{2,1,0:T(8,128)(2,1)} %refs_8_.3, bf16[2048,1536]{1,0:T(8,128)(2,1)} %w_ref.7, f32[1024,128]{1,0:T(8,128)S(1)} %get-tuple-element.275.cos_ref, ...), custom_call_target="tpu_custom_call" | custom-call | flops 10737418240 | bytes 14680064 | tf_op jit(solution)/shard_map/attn_fwd/pallas_call | solution.py:134
  53.2 27.2 %attn_fwd.2 = (bf16[1024,1536]{1,0:T(8,128)(2,1)S(1)}, bf16[1024,512]{1,0:T(8,128)(2,1)S(1)}, f32[4,1,1024]{2,1,0:T(1,128)S(1)}) custom-call(s32[3]{0:T(128)S(1)} %get-tuple-element.273.info_ref, bf16[2,1024,2048]{2,1,0:T(8,128)(2,1)} %refs_8_.3, bf16[2048,1536]{1,0:T(8,128)(2,1)} %w_ref.7, f32[1024,128]{1,0:T(8,128)S(1)} %get-tuple-element.275.cos_ref, ...), custom_call_target="tpu_custom_call" | custom-call | flops 10737418240 | bytes 14680064 | tf_op jit(solution)/shard_map/attn_fwd/pallas_call | solution.py:134
  170.8 18.7 %out_norm.2 = (bf16[1024,2048]{1,0:T(8,128)(2,1)}, f32[256,2048]{1,0:T(8,128)}, f32[256,128]{1,0:T(8,128)S(1)}) custom-call(s32[3]{0:T(128)S(1)} %get-tuple-element.273.info_ref, bf16[1024,512]{1,0:T(8,128)(2,1)S(1)} %get-tuple-element.81.refs_0_, bf16[1024,512]{1,0:T(8,128)(2,1)S(1)} %pad_maximum_fusion.3.refs_1_, ...), custom_call_target="tpu_custom_call" | custom-call | flops 8589934592 | bytes 20971520 | tf_op jit(solution)/shard_map/out_norm/pallas_call | solution.py:268
  189.5 30.2 %ffn_fwd.2 = (bf16[1024,1408]{1,0:T(8,128)(2,1)}, bf16[1024,1408]{1,0:T(8,128)(2,1)}, bf16[1024,1408]{1,0:T(8,128)(2,1)}, bf16[256,2048]{1,0:T(8,128)(2,1)}, bf1...) custom-call(bf16[1024,2048]{1,0:T(8,128)(2,1)} %get-tuple-element.83, ...), custom_call_target="tpu_custom_call" | custom-call | flops 17716740096 | bytes 25952256 | tf_op jit(solution)/shard_map/ffn_fwd/pallas_call | solution.py:336
  225.0 18.6 %out_norm.3 = (bf16[1024,2048]{1,0:T(8,128)(2,1)}, f32[256,2048]{1,0:T(8,128)}, f32[256,128]{1,0:T(8,128)S(1)}) custom-call(s32[3]{0:T(128)S(1)} %get-tuple-element.274.info_ref, bf16[1024,512]{1,0:T(8,128)(2,1)S(1)} %get-tuple-element.91.refs_0_, bf16[1024,512]{1,0:T(8,128)(2,1)S(1)} %copy-done, bf16[1024,512]{1,0:T(8,128)(2,1)S(1)} %pad_maximum_fusion.9.refs_2_, ...), custom_call_target="tpu_custom_call" | custom-call | flops 8589934592 | bytes 20971520 | tf_op jit(solution)/shard_map/out_norm/pallas_call | solution.py:268
  243.7 30.4 %ffn_fwd.3 = (bf16[1024,1408]{1,0:T(8,128)(2,1)}, bf16[1024,1408]{1,0:T(8,128)(2,1)}, bf16[1024,1408]{1,0:T(8,128)(2,1)}, bf16[256,2048]{1,0:T(8,128)(2,1)}, bf1...) custom-call(bf16[1024,2048]{1,0:T(8,128)(2,1)} %get-tuple-element.93, ...), custom_call_target="tpu_custom_call" | custom-call | flops 17716740096 | bytes 25952256 | tf_op jit(solution)/shard_map/ffn_fwd/pallas_call | solution.py:336
  393.8 11.9 norm_two.3
  405.7 30.9 %ffn_bwd.2 = (bf16[1024,1408]{1,0:T(8,128)(2,1)}, bf16[1024,1408]{1,0:T(8,128)(2,1)}, bf16[256,2048]{1,0:T(8,128)(2,1)}, bf16[128,2048]{1,0:T(8,128)(2,1)}, bf16...) custom-call(bf16[1024,2048]{1,0:T(8,128)(2,1)} %get-tuple-element.10, ...), custom_call_target="tpu_custom_call" | custom-call | flops 17716740096 | bytes 28835840 | tf_op jit(solution)/shard_map/ffn_bwd/pallas_call | solution.py:454
  440.6 30.5 %ffn_bwd.3 = (bf16[1024,1408]{1,0:T(8,128)(2,1)}, bf16[1024,1408]{1,0:T(8,128)(2,1)}, bf16[256,2048]{1,0:T(8,128)(2,1)}, bf16[128,2048]{1,0:T(8,128)(2,1)}, bf16...) custom-call(bf16[1024,2048]{1,0:T(8,128)(2,1)} %get-tuple-element.12, ...), custom_call_target="tpu_custom_call" | custom-call | flops 17716740096 | bytes 28835840 | tf_op jit(solution)/shard_map/ffn_bwd/pallas_call | solution.py:454
  472.1 12.1 fusion.36
  512.7 12.6 add_convert_fusion.3
  589.8 51.1 %psum.7 = f32[4,2048]{1,0:T(4,128)S(1)} all-reduce(f32[4,2048]{1,0:T(4,128)S(1)} %pad_maximum_fusion.21), channel_id=1, replica_groups=mesh['obj'=4,'dp'=2,'tensor'=4] {'obj','dp','tensor'}, use_global_device_ids=true, to_apply=%region_10.11 | all-reduce | flops 8192 | bytes 65536 | tf_op jit(solution)/shard_map/psum | solution.py:777
  714.0 19.7 %attn_bwd.2.dqkv_ref = bf16[1024,1536]{1,0:T(8,128)(2,1)S(1)} custom-call(s32[3]{0:T(128)S(1)} %get-tuple-element.273.info_ref, bf16[1024,1536]{1,0:T(8,128)(2,1)} %copy-done.22, bf16[4,256,512]{2,1,0:T(8,128)(2,1)S(1)} %bitcast.68, f32[4,1,1024]{2,1,0:T(1,128)S(1)} %get-tuple-element.115.lse_ref, f32[1024,128]{1,0:T(8,128)S(1)} %copy-done.3, ...), custom_call_target="tpu_custom_call" | custom-call | flops 10737418240 | bytes 8388608 | tf_op jit(solution)/shard_map/attn_bwd/pallas_call | solution.py:219
  749.3 19.3 %attn_bwd.3.dqkv_ref = bf16[1024,1536]{1,0:T(8,128)(2,1)S(1)} custom-call(s32[3]{0:T(128)S(1)} %get-tuple-element.274.info_ref, bf16[1024,1536]{1,0:T(8,128)(2,1)} %copy-done.21, bf16[4,256,512]{2,1,0:T(8,128)(2,1)S(1)} %bitcast.67, f32[4,1,1024]{2,1,0:T(1,128)S(1)} %get-tuple-element.135.lse_ref, f32[1024,128]{1,0:T(8,128)S(1)} %copy-done.3, ...), custom_call_target="tpu_custom_call" | custom-call | flops 10737418240 | bytes 8388608 | tf_op jit(solution)/shard_map/attn_bwd/pallas_call | solution.py:219
  768.6 12.8 fusion.2
  781.4 12.8 add_convert_fusion
  924.3 33.5 %collective-permute-done.99 = bf16[256,2048]{1,0:T(8,128)(2,1)} collective-permute-done((bf16[256,2048]{1,0:T(8,128)(2,1)S(1)}, bf16[256,2048]{1,0:T(8,128)(2,1)}, u32[]{:S(2)}, u32[]{:S(2)}) %collective-permute-start.99) | collective-permute-done | bytes 1048608 | tf_op jit(solution)/shard_map/ppermute | solution.py:614
  1001.0 80.4 %collective-permute-done.109 = bf16[1024,1408]{1,0:T(8,128)(2,1)} collective-permute-done((bf16[1024,1408]{1,0:T(8,128)(2,1)S(1)}, bf16[1024,1408]{1,0:T(8,128)(2,1)}, u32[]{:S(2)}, u32[]{:S(2)}) %collective-permute-start.109) | collective-permute-done | bytes 2883616 | tf_op jit(solution)/shard_map/ppermute | solution.py:614
  1120.6 27.8 %collective-permute-done.94 = bf16[1024,1536]{0,1:T(8,128)(2,1)S(1)} collective-permute-done((bf16[1024,1536]{0,1:T(8,128)(2,1)S(1)}, bf16[1024,1536]{0,1:T(8,128)(2,1)S(1)}, u32[]{:S(2)}, u32[]{:S(2)}) %collective-permute-start.94) | collective-permute-done | bytes 3145760 | tf_op jit(solution)/shard_map/ppermute | solution.py:614
  1157.2 39.3 %collective-permute-done.116 = bf16[704,2048]{1,0:T(8,128)(2,1)S(1)} collective-permute-done((bf16[704,2048]{1,0:T(8,128)(2,1)S(1)}, bf16[704,2048]{1,0:T(8,128)(2,1)S(1)}, u32[]{:S(2)}, u32[]{:S(2)}) %collective-permute-start.116) | collective-permute-done | bytes 2883616 | tf_op jit(solution)/shard_map/ppermute | solution.py:616
  1202.6 55.9 %collective-permute-done.111 = bf16[1024,1408]{1,0:T(8,128)(2,1)} collective-permute-done((bf16[1024,1408]{1,0:T(8,128)(2,1)S(1)}, bf16[1024,1408]{1,0:T(8,128)(2,1)}, u32[]{:S(2)}, u32[]{:S(2)}) %collective-permute-start.111) | collective-permute-done | bytes 2883616 | tf_op jit(solution)/shard_map/ppermute | solution.py:616
  1261.0 59.3 %collective-permute-done.106 = bf16[1024,1408]{1,0:T(8,128)(2,1)} collective-permute-done((bf16[1024,1408]{1,0:T(8,128)(2,1)S(1)}, bf16[1024,1408]{1,0:T(8,128)(2,1)}, u32[]{:S(2)}, u32[]{:S(2)}) %collective-permute-start.106) | collective-permute-done | bytes 2883616 | tf_op jit(solution)/shard_map/ppermute | solution.py:616
  1330.7 53.8 %collective-permute-done.96 = bf16[1024,1536]{0,1:T(8,128)(2,1)} collective-permute-done((bf16[1024,1536]{0,1:T(8,128)(2,1)S(1)}, bf16[1024,1536]{0,1:T(8,128)(2,1)}, u32[]{:S(2)}, u32[]{:S(2)}) %collective-permute-start.96) | collective-permute-done | bytes 3145760 | tf_op jit(solution)/shard_map/ppermute | solution.py:616
  1410.4 12.6 copy.33
  (539 shorter events, 689.9 us)
Async XLA Ops:
  2.9 83.1 %collective-permute-start.10 = (bf16[128,2048]{1,0:T(8,128)(2,1)}, bf16[128,2048]{1,0:T(8,128)(2,1)}, u32[]{:S(2)}, u32[]{:S(2)}) collective-permute-start(bf16[128,2048]{1,0:T(8,128)(2,1)} %get-tuple-element.205), channel_id=1, source_target_pairs={{0,2},{1,3},{2,0},{3,1},{4,6},{5,7},{6,4},{7,5},{8,10},{9,11},{10,... | collective-permute-start | bytes 1572872 | tf_op jit(solution)/shard_map/ppermute | solution.py:550
  5.9 83.2 %collective-permute-start.7 = (bf16[128,2048]{1,0:T(8,128)(2,1)}, bf16[128,2048]{1,0:T(8,128)(2,1)}, u32[]{:S(2)}, u32[]{:S(2)}) collective-permute-start(bf16[128,2048]{1,0:T(8,128)(2,1)} %get-tuple-element.205), channel_id=1, source_target_pairs={{0,1},{1,0},{2,3},{3,2},{4,5},{5,4},{6,7},{7,6},{8,9},{9,8},{10,11... | collective-permute-start | bytes 1572872 | tf_op jit(solution)/shard_map/ppermute | solution.py:550
  7.9 81.4 %collective-permute-start.6 = (bf16[128,2048]{1,0:T(8,128)(2,1)}, bf16[128,2048]{1,0:T(8,128)(2,1)}, u32[]{:S(2)}, u32[]{:S(2)}) collective-permute-start(bf16[128,2048]{1,0:T(8,128)(2,1)} %get-tuple-element.206), channel_id=1, source_target_pairs={{0,1},{1,0},{2,3},{3,2},{4,5},{5,4},{6,7},{7,6},{8,9},{9,8},{10,11... | collective-permute-start | bytes 1572872 | tf_op jit(solution)/shard_map/ppermute | solution.py:550
  436.5 120.3 %collective-permute-start.45 = (bf16[128,2048]{1,0:T(8,128)(2,1)}, bf16[128,2048]{1,0:T(8,128)(2,1)S(1)}, u32[]{:S(2)}, u32[]{:S(2)}) collective-permute-start(bf16[128,2048]{1,0:T(8,128)(2,1)} %get-tuple-element.108), channel_id=1, source_target_pairs={{0,1},{1,0},{2,3},{3,2},{4,5},{5,4},{6,7},{7,6},{8,9},{9,8},{10,11... | collective-permute-start | bytes 1572872 | tf_op jit(solution)/shard_map/ppermute | solution.py:550
  437.4 105.8 %collective-permute-start.46 = (bf16[128,2048]{1,0:T(8,128)(2,1)}, bf16[128,2048]{1,0:T(8,128)(2,1)}, u32[]{:S(2)}, u32[]{:S(2)}) collective-permute-start(bf16[128,2048]{1,0:T(8,128)(2,1)} %get-tuple-element.110), channel_id=1, source_target_pairs={{0,1},{1,0},{2,3},{3,2},{4,5},{5,4},{6,7},{7,6},{8,9},{9,8},{10,11... | collective-permute-start | bytes 1572872 | tf_op jit(solution)/shard_map/ppermute | solution.py:550
  438.6 107.2 %collective-permute-start.48 = (bf16[128,2048]{1,0:T(8,128)(2,1)}, bf16[128,2048]{1,0:T(8,128)(2,1)S(1)}, u32[]{:S(2)}, u32[]{:S(2)}) collective-permute-start(bf16[128,2048]{1,0:T(8,128)(2,1)} %get-tuple-element.112), channel_id=1, source_target_pairs={{0,2},{1,3},{2,0},{3,1},{4,6},{5,7},{6,4},{7,5},{8,10},{9,11},{10,... | collective-permute-start | bytes 1572872 | tf_op jit(solution)/shard_map/ppermute | solution.py:550
  440.1 118.1 %collective-permute-start.50 = (bf16[128,2048]{1,0:T(8,128)(2,1)}, bf16[128,2048]{1,0:T(8,128)(2,1)S(1)}, u32[]{:S(2)}, u32[]{:S(2)}) collective-permute-start(bf16[128,2048]{1,0:T(8,128)(2,1)} %get-tuple-element.113), channel_id=1, source_target_pairs={{0,2},{1,3},{2,0},{3,1},{4,6},{5,7},{6,4},{7,5},{8,10},{9,11},{10,... | collective-permute-start | bytes 1572872 | tf_op jit(solution)/shard_map/ppermute | solution.py:550
  558.3 285.6 %collective-permute-start.113 = (bf16[704,2048]{1,0:T(8,128)(2,1)}, bf16[704,2048]{1,0:T(8,128)(2,1)}, u32[]{:S(2)}, u32[]{:S(2)}) collective-permute-start(bf16[704,2048]{1,0:T(8,128)(2,1)} %constant_dynamic-slice_fusion.1), channel_id=1, source_target_pairs={{0,4},{4,0},{1,5},{5,1},{2,6},{6,2},{3,7},{7,3},{8,12},{12,8},{9,1... | collective-permute-start | bytes 8650760 | tf_op jit(solution)/shard_map/ppermute | solution.py:628
  567.8 263.4 %collective-permute-start.103 = (bf16[1024,1408]{1,0:T(8,128)(2,1)}, bf16[1024,1408]{1,0:T(8,128)(2,1)}, u32[]{:S(2)}, u32[]{:S(2)}) collective-permute-start(bf16[1024,1408]{1,0:T(8,128)(2,1)} %constant_dynamic-slice_fusion.3), channel_id=1, source_target_pairs={{0,4},{4,0},{1,5},{5,1},{2,6},{6,2},{3,7},{7,3},{8,12},{12,8},{9,1... | collective-permute-start | bytes 8650760 | tf_op jit(solution)/shard_map/ppermute | solution.py:628
  692.6 194.4 %collective-permute-start.108 = (bf16[1024,1408]{1,0:T(8,128)(2,1)}, bf16[1024,1408]{1,0:T(8,128)(2,1)}, u32[]{:S(2)}, u32[]{:S(2)}) collective-permute-start(bf16[1024,1408]{1,0:T(8,128)(2,1)} %constant_dynamic-slice_fusion.2), channel_id=1, source_target_pairs={{0,4},{4,0},{1,5},{5,1},{2,6},{6,2},{3,7},{7,3},{8,12},{12,8},{9,1... | collective-permute-start | bytes 8650760 | tf_op jit(solution)/shard_map/ppermute | solution.py:628
  870.0 101.7 %collective-permute-start.93 = (bf16[1024,1536]{0,1:T(8,128)(2,1)}, bf16[1024,1536]{0,1:T(8,128)(2,1)}, u32[]{:S(2)}, u32[]{:S(2)}) collective-permute-start(bf16[1024,1536]{0,1:T(8,128)(2,1)} %dynamic-slice_bitcast_fusion), channel_id=1, source_target_pairs={{0,4},{4,0},{1,5},{5,1},{2,6},{6,2},{3,7},{7,3},{8,12},{12,8},{9,1... | collective-permute-start | bytes 9437192 | tf_op jit(solution)/shard_map/ppermute | solution.py:628
  870.0 90.3 %collective-permute-start.114 = (bf16[704,2048]{1,0:T(8,128)(2,1)}, bf16[704,2048]{1,0:T(8,128)(2,1)}, u32[]{:S(2)}, u32[]{:S(2)}) collective-permute-start(bf16[704,2048]{1,0:T(8,128)(2,1)} %add_convert_fusion.8), channel_id=1, source_target_pairs={{0,8},{24,16},{1,9},{25,17},{2,10},{26,18},{3,11},{27,19},{4,12},{... | collective-permute-start | bytes 8650760 | tf_op jit(solution)/shard_map/ppermute | solution.py:614
  877.6 80.2 %collective-permute-start.99 = (bf16[256,2048]{1,0:T(8,128)(2,1)S(1)}, bf16[256,2048]{1,0:T(8,128)(2,1)}, u32[]{:S(2)}, u32[]{:S(2)}) collective-permute-start(bf16[256,2048]{1,0:T(8,128)(2,1)S(1)} %add_convert_fusion.18), channel_id=1, source_target_pairs={{0,8},{24,16},{1,9},{25,17},{2,10},{26,18},{3,11},{27,19},{4,12},{... | collective-permute-start | bytes 3145736 | tf_op jit(solution)/shard_map/ppermute | solution.py:614
  912.3 183.0 %collective-permute-start.104 = (bf16[1024,1408]{1,0:T(8,128)(2,1)S(1)}, bf16[1024,1408]{1,0:T(8,128)(2,1)}, u32[]{:S(2)}, u32[]{:S(2)}) collective-permute-start(bf16[1024,1408]{1,0:T(8,128)(2,1)S(1)} %add_convert_fusion.14), channel_id=1, source_target_pairs={{0,8},{24,16},{1,9},{25,17},{2,10},{26,18},{3,11},{27,19},{4,12},{... | collective-permute-start | bytes 8650760 | tf_op jit(solution)/shard_map/ppermute | solution.py:614
  921.3 160.0 %collective-permute-start.109 = (bf16[1024,1408]{1,0:T(8,128)(2,1)S(1)}, bf16[1024,1408]{1,0:T(8,128)(2,1)}, u32[]{:S(2)}, u32[]{:S(2)}) collective-permute-start(bf16[1024,1408]{1,0:T(8,128)(2,1)S(1)} %add_convert_fusion.11), channel_id=1, source_target_pairs={{0,8},{24,16},{1,9},{25,17},{2,10},{26,18},{3,11},{27,19},{4,12},{... | collective-permute-start | bytes 8650760 | tf_op jit(solution)/shard_map/ppermute | solution.py:614
  971.7 136.4 %collective-permute-start.115 = (bf16[704,2048]{1,0:T(8,128)(2,1)S(1)}, bf16[704,2048]{1,0:T(8,128)(2,1)}, u32[]{:S(2)}, u32[]{:S(2)}) collective-permute-start(bf16[704,2048]{1,0:T(8,128)(2,1)S(1)} %add_convert_fusion.7), channel_id=1, source_target_pairs={{8,16},{16,8},{9,17},{17,9},{10,18},{18,10},{11,19},{19,11},{12,20... | collective-permute-start | bytes 8650760 | tf_op jit(solution)/shard_map/ppermute | solution.py:615
  983.2 165.2 %collective-permute-start.94 = (bf16[1024,1536]{0,1:T(8,128)(2,1)S(1)}, bf16[1024,1536]{0,1:T(8,128)(2,1)S(1)}, u32[]{:S(2)}, u32[]{:S(2)}) collective-permute-start(bf16[1024,1536]{0,1:T(8,128)(2,1)S(1)} %fusion), channel_id=1, source_target_pairs={{0,8},{24,16},{1,9},{25,17},{2,10},{26,18},{3,11},{27,19},{4,12},{... | collective-permute-start | bytes 9437192 | tf_op jit(solution)/shard_map/ppermute | solution.py:614
  1000.6 84.1 %collective-permute-start.64 = (bf16[128,2048]{1,0:T(8,128)(2,1)S(1)}, bf16[128,2048]{1,0:T(8,128)(2,1)}, u32[]{:S(2)}, u32[]{:S(2)}) collective-permute-start(bf16[128,2048]{1,0:T(8,128)(2,1)S(1)} %get-tuple-element.224), channel_id=1, source_target_pairs={{0,1},{1,0},{2,3},{3,2},{4,5},{5,4},{6,7},{7,6},{8,9},{9,8},{10,11... | collective-permute-start | bytes 1572872 | tf_op jit(solution)/shard_map/ppermute | solution.py:550
  1112.1 84.4 %collective-permute-start.116 = (bf16[704,2048]{1,0:T(8,128)(2,1)S(1)}, bf16[704,2048]{1,0:T(8,128)(2,1)S(1)}, u32[]{:S(2)}, u32[]{:S(2)}) collective-permute-start(bf16[704,2048]{1,0:T(8,128)(2,1)S(1)} %add_convert_fusion.6), channel_id=1, source_target_pairs={{8,0},{16,24},{9,1},{17,25},{10,2},{18,26},{11,3},{19,27},{12,4},{... | collective-permute-start | bytes 8650760 | tf_op jit(solution)/shard_map/ppermute | solution.py:616
  1153.6 104.8 %collective-permute-start.111 = (bf16[1024,1408]{1,0:T(8,128)(2,1)S(1)}, bf16[1024,1408]{1,0:T(8,128)(2,1)}, u32[]{:S(2)}, u32[]{:S(2)}) collective-permute-start(bf16[1024,1408]{1,0:T(8,128)(2,1)S(1)} %add_convert_fusion.9), channel_id=1, source_target_pairs={{8,0},{16,24},{9,1},{17,25},{10,2},{18,26},{11,3},{19,27},{12,4},{... | collective-permute-start | bytes 8650760 | tf_op jit(solution)/shard_map/ppermute | solution.py:616
  1155.8 164.5 %collective-permute-start.106 = (bf16[1024,1408]{1,0:T(8,128)(2,1)S(1)}, bf16[1024,1408]{1,0:T(8,128)(2,1)}, u32[]{:S(2)}, u32[]{:S(2)}) collective-permute-start(bf16[1024,1408]{1,0:T(8,128)(2,1)S(1)} %add_convert_fusion.12), channel_id=1, source_target_pairs={{8,0},{16,24},{9,1},{17,25},{10,2},{18,26},{11,3},{19,27},{12,4},{... | collective-permute-start | bytes 8650760 | tf_op jit(solution)/shard_map/ppermute | solution.py:616
  1196.9 125.7 %collective-permute-start.117 = (bf16[704,2048]{1,0:T(8,128)(2,1)S(1)}, bf16[704,2048]{1,0:T(8,128)(2,1)}, u32[]{:S(2)}, u32[]{:S(2)}) collective-permute-start(bf16[704,2048]{1,0:T(8,128)(2,1)S(1)} %broadcast_select_fusion.3), channel_id=1, source_target_pairs={{0,4},{4,0},{1,5},{5,1},{2,6},{6,2},{3,7},{7,3},{8,12},{12,8},{9,1... | collective-permute-start | bytes 8650760 | tf_op jit(solution)/shard_map/ppermute | solution.py:630
  1201.3 183.2 %collective-permute-start.96 = (bf16[1024,1536]{0,1:T(8,128)(2,1)S(1)}, bf16[1024,1536]{0,1:T(8,128)(2,1)}, u32[]{:S(2)}, u32[]{:S(2)}) collective-permute-start(bf16[1024,1536]{0,1:T(8,128)(2,1)S(1)} %add_convert_fusion.4), channel_id=1, source_target_pairs={{8,0},{16,24},{9,1},{17,25},{10,2},{18,26},{11,3},{19,27},{12,4},{... | collective-permute-start | bytes 9437192 | tf_op jit(solution)/shard_map/ppermute | solution.py:616
  1260.9 126.0 %collective-permute-start.112 = (bf16[1024,1408]{1,0:T(8,128)(2,1)S(1)}, bf16[1024,1408]{1,0:T(8,128)(2,1)}, u32[]{:S(2)}, u32[]{:S(2)}) collective-permute-start(bf16[1024,1408]{1,0:T(8,128)(2,1)S(1)} %broadcast_select_fusion.6), channel_id=1, source_target_pairs={{0,4},{4,0},{1,5},{5,1},{2,6},{6,2},{3,7},{7,3},{8,12},{12,8},{9,1... | collective-permute-start | bytes 8650760 | tf_op jit(solution)/shard_map/ppermute | solution.py:630
  (174 other events, 3860.1 us)

commit v2 on v1

--- a/solution.py
+++ b/solution.py
@@ -3,6 +3,7 @@
 
 import jax
 import jax.numpy as jnp
+import numpy as np
 from jax import lax
 from jax.experimental import pallas as pl
 from jax.experimental.pallas import tpu as pltpu
@@ -633,7 +634,7 @@
     return jnp.concatenate([first, second], axis=0).astype(F32)
 
 
-def body(
+def general_body(
     tokens,
     cotangent,
     segment_ids,
@@ -790,6 +791,1393 @@
     )
 
 
+ORDER = ((1, 0), (3, 0), (2, 1), (3, 1), (1, 1), (2, 0), (0, 0), (0, 1))
+CORES = ((0, 1), (1, 0))
+COST_SHARE = 0.1
+
+
+def plane_case(token_shape, down_shape):
+    return (
+        lax.axis_size("tensor") == 4
+        and lax.axis_size("dp") == 2
+        and lax.axis_size("obj") == 4
+        and token_shape[0] == 2
+        and token_shape[1] % 1024 == 0
+        and token_shape[2] % 1024 == 0
+        and down_shape[0] % 128 == 0
+    )
+
+
+def spec(shape, index):
+    return pl.BlockSpec(shape, index)
+
+
+def call(
+    kernel, name, grid, ins, in_specs, outs, out_specs, scalars=(), after=(), scratch=(), aliases=None,
+    mib=48, flops=0, nbytes=0,
+):
+    ns, ni, na = len(scalars), len(ins), len(after)
+
+    def wrapped(*refs):
+        kernel(*refs[: ns + ni], *refs[ns + ni + na :])
+
+    grid_spec = pltpu.PrefetchScalarGridSpec(
+        num_scalar_prefetch=ns,
+        grid=grid,
+        in_specs=list(in_specs) + [pl.BlockSpec(memory_space=ANY)] * na,
+        out_specs=list(out_specs),
+        scratch_shapes=list(scratch),
+    )
+    return pl.pallas_call(
+        wrapped,
+        grid_spec=grid_spec,
+        out_shape=[jax.ShapeDtypeStruct(s, d) for s, d in outs],
+        input_output_aliases={ns + k: v for k, v in (aliases or {}).items()},
+        compiler_params=params(62, len(grid)),
+        cost_estimate=cost(flops / COST_SHARE, nbytes / COST_SHARE),
+        name=name,
+    )(*scalars, *ins, *after)
+
+
+def constant_tables(length):
+    half = HEAD_DIM // 2
+    frequency = np.exp(np.arange(half, dtype=np.float32) * np.float32(-2.0 * math.log(10000.0) / HEAD_DIM))
+    angles = np.arange(length, dtype=np.float32)[:, None] * frequency[None, :]
+    cosine, sine = np.cos(angles), np.sin(angles)
+    both = lambda a, b: jnp.asarray(np.concatenate([a, b], axis=1).astype(np.float32))
+    return both(cosine, cosine), both(-sine, sine)
+
+
+class Chain:
+    def __init__(self):
+        self.last = ()
+
+    def __call__(self, *args, after=(), **kwargs):
+        out = call(*args, after=tuple(self.last) + tuple(after), **kwargs)
+        self.last = (out[0],)
+        return out
+
+
+def pair_swap(to_x, to_y):
+    return swap(to_x, 1, 4), swap(to_y, 2, 4)
+
+
+def plane_attn_fwd(chain, info, row, tokens, qkv_weight, cosine, sine, segc, segr, after=()):
+    _, length, width = tokens.shape
+    heads = qkv_weight.shape[1] // (3 * HEAD_DIM)
+    return chain(
+        functools.partial(attn_fwd_kernel, tile=256),
+        "attn_fwd",
+        (heads,),
+        (tokens, qkv_weight, cosine, sine, segc, segr),
+        [
+            pl.BlockSpec((None, length, width), lambda h, *_: (row, 0, 0), pipeline_mode=pl.Buffered(1)),
+            spec((width, 3 * HEAD_DIM), lambda h, *_: (0, h)),
+            const_spec((length, HEAD_DIM)),
+            const_spec((length, HEAD_DIM)),
+            const_spec((length, 1)),
+            const_spec((1, length)),
+        ],
+        [((length, heads * 384), BF), ((length, heads * 128), BF), ((heads, 1, length), F32)],
+        [
+            spec((length, 384), lambda h, *_: (0, h)),
+            spec((length, 128), lambda h, *_: (0, h)),
+            spec((None, 1, length), lambda h, *_: (h, 0, 0)),
+        ],
+        scalars=(info,),
+        after=after,
+        scratch=[pltpu.VMEM((length, length), F32)],
+        flops=heads * (2 * length * width * 384 + 8 * length * length * 128),
+        nbytes=2 * length * width + 2 * width * heads * 384 + 8 * length * heads * 128,
+    )
+
+
+def plane_attn_bwd_kernel(
+    info_ref, qkv_ref, own, r1, r2, r3a, r3b, ow_ref, lse_ref, cos_ref, sin_ref, segc_ref, segr_ref, dqkv_ref,
+    bias_ref, dol_nat, dk_ref, dv_ref,
+):
+    length = qkv_ref.shape[0]
+    block = own.shape[0]
+    half = block // 2
+    me = info_ref[0]
+
+    @pl.when(pl.program_id(0) == 0)
+    def _():
+        fill_bias(info_ref, segc_ref, segr_ref, bias_ref, block)
+
+    def natural(r, lower):
+        return pl.multiple_of((me ^ r) * block + lower, half)
+
+    for r, piece in enumerate((own, r1, r2)):
+        dol_nat[pl.ds(natural(r, 0), block), :] = mm_nt(piece[...], ow_ref[...]).astype(BF)
+    for lower, piece in ((0, r3a), (half, r3b)):
+        dol_nat[pl.ds(natural(3, lower), half), :] = mm_nt(piece[...], ow_ref[...]).astype(BF)
+    attn_bwd_head(qkv_ref, dol_nat, lse_ref, cos_ref, sin_ref, dqkv_ref, bias_ref, dk_ref, dv_ref, block)
+
+
+def attn_bwd_head(qkv_ref, dol_nat, lse_ref, cos_ref, sin_ref, dqkv_ref, bias_ref, dk_ref, dv_ref, tile):
+    length = qkv_ref.shape[0]
+    keys = qkv_ref[:, HEAD_DIM : 2 * HEAD_DIM]
+    values = qkv_ref[:, 2 * HEAD_DIM :]
+    keys_t = keys.astype(F32).T.astype(BF)
+    for step in range(length // tile):
+        rows = pl.ds(step * tile, tile)
+        queries = qkv_ref[rows, :HEAD_DIM]
+        dol = dol_nat[rows, :]
+        scores = mm_nt(keys, queries) * score_scale + bias_ref[:, rows]
+        probs = jnp.exp(scores - lse_ref[:, rows])
+        dp = mm_nt(values, dol)
+        inner = jnp.sum(probs * dp, axis=0, keepdims=True)
+        draw = (probs * (dp - inner) * score_scale).astype(BF)
+        dv = mm(probs.astype(BF), dol)
+        dk = mm(draw, queries)
+        if step == 0:
+            dv_ref[...] = dv
+            dk_ref[...] = dk
+        else:
+            dv_ref[...] += dv
+            dk_ref[...] += dk
+        dq = mm(keys_t, draw).T
+        turned = dq * cos_ref[rows, :] - pltpu.roll(dq, HEAD_DIM // 2, 1) * sin_ref[rows, :]
+        dqkv_ref[rows, :HEAD_DIM] = turned.astype(BF)
+    dk = dk_ref[...]
+    turned = dk * cos_ref[...] - pltpu.roll(dk, HEAD_DIM // 2, 1) * sin_ref[...]
+    dqkv_ref[:, HEAD_DIM : 2 * HEAD_DIM] = turned.astype(BF)
+    dqkv_ref[:, 2 * HEAD_DIM :] = dv_ref[...].astype(BF)
+
+
+def plane_attn_bwd(chain, info, qkv, pieces, out_weight, lse, cosine, sine, segc, segr, after=()):
+    length = qkv.shape[0]
+    heads = qkv.shape[1] // 384
+    width = out_weight.shape[1]
+    return chain(
+        plane_attn_bwd_kernel,
+        "attn_bwd",
+        (heads,),
+        (qkv, *pieces, out_weight, lse, cosine, sine, segc, segr),
+        [spec((length, 384), lambda h, *_: (0, h))]
+        + [const_spec(p.shape) for p in pieces]
+        + [
+            spec((128, width), lambda h, *_: (h, 0)),
+            spec((None, 1, length), lambda h, *_: (h, 0, 0)),
+            const_spec((length, HEAD_DIM)),
+            const_spec((length, HEAD_DIM)),
+            const_spec((length, 1)),
+            const_spec((1, length)),
+        ],
+        [(qkv.shape, BF)],
+        [spec((length, 384), lambda h, *_: (0, h))],
+        scalars=(info,),
+        after=after,
+        scratch=[
+            pltpu.VMEM((length, length), F32),
+            pltpu.VMEM((length, HEAD_DIM), BF),
+            pltpu.VMEM((length, HEAD_DIM), F32),
+            pltpu.VMEM((length, HEAD_DIM), F32),
+        ],
+        flops=heads * 24 * length * length * 128,
+        nbytes=16 * length * heads * 128,
+    )[0]
+
+
+def plane_out_norm_kernel(
+    info_ref, order_ref, *refs
+):
+    lows, highs = refs[:4], refs[4:8]
+    ow_ref, mine_ref, other_ref = refs[8:11]
+    xl_ref, xh_ref, gain_ref, bias_ref, hl_ref, n1_ref, rstd_ref, total_ref = refs[11:]
+    half = xl_ref.shape[0]
+    feat = mine_ref.shape[0] // 3
+    total_ref[:half] = xl_ref[...].astype(F32) * deep_alpha
+    total_ref[half:] = xh_ref[...].astype(F32) * deep_alpha
+    ols = [jnp.concatenate([lo[...], hi[...]], axis=0) for lo, hi in zip(lows, highs)]
+
+    def add(first, second):
+        total = mm(ols[0], ow_ref[...])
+        for r in range(1, 4):
+            rows = pl.ds((r - 1) * feat, feat)
+            total += mm(ols[r][:, :feat], first[rows, :])
+            total += mm(ols[r][:, feat:], second[rows, :])
+        total_ref[...] += total
+
+    @pl.when(info_ref[3] == 0)
+    def _():
+        add(mine_ref, other_ref)
+
+    @pl.when(info_ref[3] != 0)
+    def _():
+        add(other_ref, mine_ref)
+
+    total = total_ref[...]
+    centered = total - jnp.mean(total, axis=1, keepdims=True)
+    variance = jnp.mean(centered * centered, axis=1, keepdims=True)
+    inv = lax.rsqrt(variance + norm_eps)
+    normed = centered * inv
+    hl_ref[...] = (normed * gain_ref[...] + bias_ref[...]).astype(BF)
+
+    @pl.when(pl.program_id(0) == 3)
+    def _():
+        n1_ref[...] = normed
+        rstd_ref[...] = jnp.broadcast_to(inv, rstd_ref.shape)
+
+
+def plane_out_norm(chain, info, order, row, ol_pieces, out_weight, mine, other, tokens, gain, bias, after=()):
+    _, length, width = tokens.shape
+    block = length // 4
+    half = block // 2
+    head_width = out_weight.shape[0]
+    low = lambda i, info, order: (order[2 * i], 0)
+    high = lambda i, info, order: (order[2 * i + 1], 0)
+    low3 = lambda i, info, order: (row, order[2 * i], 0)
+    high3 = lambda i, info, order: (row, order[2 * i + 1], 0)
+    return chain(
+        plane_out_norm_kernel,
+        "out_norm",
+        (4,),
+        (*ol_pieces, *ol_pieces, out_weight, mine, other, tokens, tokens, gain, bias),
+        [spec((half, head_width), low)] * 4
+        + [spec((half, head_width), high)] * 4
+        + [const_spec(out_weight.shape), const_spec(mine.shape), const_spec(other.shape)]
+        + [
+            spec((None, half, width), low3),
+            spec((None, half, width), high3),
+            const_spec((1, width)),
+            const_spec((1, width)),
+        ],
+        [((length, width), BF), ((block, width), F32), ((block, HEAD_DIM), F32)],
+        [
+            spec((block, width), lambda i, *_: (i, 0)),
+            spec((block, width), lambda i, *_: (0, 0)),
+            spec((block, HEAD_DIM), lambda i, *_: (0, 0)),
+        ],
+        scalars=(info, order),
+        after=after,
+        scratch=[pltpu.VMEM((block, width), F32)],
+        flops=2 * length * width * width,
+        nbytes=2 * width * width + 6 * length * width,
+    )
+
+
+def split_kernel(x_ref, y_ref, *refs):
+    count = len(refs) // 2 - 1
+    refs[count][...] = x_ref[...]
+    refs[count + 1][...] = y_ref[...]
+
+
+def forward(chain, from_x, from_y, carry=(), after=()):
+    rows, width = from_x.shape
+    shape = (rows // 2, width)
+    any_spec = pl.BlockSpec(memory_space=ANY)
+    out = chain(
+        split_kernel, "split", (1,), (from_x, from_y, *carry),
+        [
+            pl.BlockSpec(shape, lambda i, *_: (0, 0), pipeline_mode=pl.Buffered(1)),
+            pl.BlockSpec(shape, lambda i, *_: (1, 0), pipeline_mode=pl.Buffered(1)),
+        ]
+        + [any_spec] * len(carry),
+        [(shape, BF)] * 2 + [(c.shape, c.dtype) for c in carry],
+        [spec(shape, lambda i, *_: (0, 0))] * 2 + [any_spec] * len(carry),
+        after=after,
+        aliases={2 + k: 2 + k for k in range(len(carry))},
+        nbytes=4 * rows * width,
+    )
+    pair = (swap(out[0], 2, 4), swap(out[1], 1, 4))
+    return (pair, *out[2:]) if carry else pair
+
+
+def ow_join_kernel(x_ref, y_ref, a_ref, b_ref, out_ref):
+    rows = x_ref.shape[0]
+    out_ref[:rows] = x_ref[...]
+    out_ref[rows : 2 * rows] = y_ref[...]
+    out_ref[2 * rows : 2 * rows + rows // 2] = a_ref[...]
+    out_ref[2 * rows + rows // 2 :] = b_ref[...]
+
+
+def ow_join(chain, pieces, after=()):
+    rows, width = pieces[0].shape
+    shape = (3 * rows, width)
+    return chain(
+        ow_join_kernel, "ow_join", (1,), pieces, [const_spec(p.shape) for p in pieces],
+        [(shape, BF)], [spec(shape, lambda i, *_: (0, 0))], after=after,
+    )[0]
+
+
+def join_kernel(a_ref, b_ref, carried, out_ref, carried_out):
+    half = a_ref.shape[0]
+    out_ref[:half] = a_ref[...]
+    out_ref[half:] = b_ref[...]
+
+
+def join_halves(chain, halves, carry, after=()):
+    rows, width = halves[0].shape
+    shape = (2 * rows, width)
+    out = chain(
+        join_kernel, "join_halves", (1,), (*halves, carry),
+        [const_spec(h.shape) for h in halves] + [pl.BlockSpec(memory_space=ANY)],
+        [(shape, BF), (carry.shape, carry.dtype)],
+        [spec(shape, lambda i, *_: (0, 0)), pl.BlockSpec(memory_space=ANY)],
+        after=after, aliases={2: 1}, nbytes=4 * rows * width,
+    )
+    return out
+
+
+def load_once(pairs, sem):
+    copies = [pltpu.make_async_copy(src, dst, sem.at[k]) for k, (src, dst) in enumerate(pairs)]
+
+    @pl.when(pl.program_id(0) == 0)
+    def _():
+        for copy in copies:
+            copy.start()
+
+    def wait(k):
+        @pl.when(pl.program_id(0) == 0)
+        def _():
+            copies[k].wait()
+
+    return wait
+
+
+def store_half(first, part, refs):
+    at = pl.program_id(0)
+    half = part.shape[0] // 2
+    if first is None:
+
+        @pl.when(at == 0)
+        def _():
+            refs[0][...] = part
+
+        @pl.when(at == 1)
+        def _():
+            refs[1][...] = part
+
+        @pl.when(at == 2)
+        def _():
+            refs[2][...] = part[:half]
+            refs[3][...] = part[half:]
+
+        @pl.when(at == 3)
+        def _():
+            refs[4][...] = part
+
+        return
+
+    @pl.when(at == 0)
+    def _():
+        if first:
+            refs[0][...] = part
+        else:
+            refs[0][...] = part[:half]
+            refs[1][...] = part[half:]
+
+    @pl.when(at == 1)
+    def _():
+        refs[-1][...] = part
+
+
+def half_outs(first, block, width):
+    if first is None:
+        sizes = [block, block, block // 2, block // 2, block]
+    else:
+        sizes = [block, block] if first else [block // 2, block // 2, block]
+    return [((s, width), BF) for s in sizes], [spec((s, width), lambda i, *_: (0, 0)) for s in sizes]
+
+
+def plane_ffn_fwd_kernel(hl_ref, wg_hbm, wu_hbm, wd_hbm, *refs, first):
+    refs, (wg, wu, wd, sem) = refs[:-4], refs[-4:]
+    (al_ref, ga_ref, gb_ref), refs = refs[-3:], refs[:-3]
+    wait = load_once(((wg_hbm, wg), (wu_hbm, wu), (wd_hbm, wd)), sem)
+    hidden = hl_ref[...]
+    wait(0)
+    gate = mm(hidden, wg[...])
+    wait(1)
+    up = mm(hidden, wu[...])
+    cdf = 0.5 + 0.5 * lax.erf(gate * (1.0 / math.sqrt(2.0)))
+    pdf = jnp.exp(gate * gate * -0.5) * (1.0 / math.sqrt(2.0 * math.pi))
+    act = gate * cdf
+    ga_ref[...] = (up * (cdf + gate * pdf)).astype(BF)
+    gb_ref[...] = act.astype(BF)
+    low = (act * up).astype(BF)
+    al_ref[...] = low
+    wait(2)
+    store_half(first, mm(low, wd[...]).astype(BF), refs)
+
+
+def plane_ffn_fwd(chain, first, hidden, weights, kept, after=()):
+    length, width = hidden.shape
+    units = weights[0].shape[1]
+    block = length // 4
+    base = 0 if first else 2
+    tiled = lambda w: spec((block, w), lambda i, *_: (i + base, 0))
+    outs, out_specs = half_outs(first, block, width)
+    n = len(outs)
+    any_spec = pl.BlockSpec(memory_space=ANY)
+    kept = () if first else tuple(kept)
+    held, carried = kept[:3], kept[3:]
+    kernel = functools.partial(plane_ffn_fwd_kernel, first=first)
+    if first:
+        body_kernel = kernel
+    else:
+        nk, nc = len(kept), len(carried)
+
+        def body_kernel(hl, wg, wu, wd, *refs):
+            refs = refs[nk:]
+            kernel(hl, wg, wu, wd, *refs[:n], *refs[n + nc :])
+
+    out = chain(
+        body_kernel,
+        "ffn_fwd",
+        (2,),
+        (hidden, *weights, *kept),
+        [tiled(width)] + [any_spec] * (3 + len(kept)),
+        outs + [(c.shape, BF) for c in carried] + [((length, units), BF)] * 3,
+        out_specs + [any_spec] * len(carried) + [tiled(units)] * 3,
+        after=after,
+        aliases={}
+        if first
+        else {
+            **{4 + k: n + len(carried) + k for k in range(3)},
+            **{7 + k: n + k for k in range(len(carried))},
+        },
+        scratch=[
+            pltpu.VMEM(weights[0].shape, BF),
+            pltpu.VMEM(weights[1].shape, BF),
+            pltpu.VMEM(weights[2].shape, BF),
+            pltpu.SemaphoreType.DMA((3,)),
+        ],
+        mib=60,
+        flops=3 * length * width * units,
+        nbytes=6 * units * width + 3 * length * units,
+    )
+    n += len(carried)
+    return out[:n], out[n:]
+
+
+def plane_ffn_bwd_kernel(dffn_ref, ga_ref, gb_ref, wd_hbm, wg_hbm, wu_hbm, *refs, first):
+    refs, (wd, wg, wu, sem) = refs[:-4], refs[-4:]
+    (dg_ref, du_ref), refs = refs[-2:], refs[:-2]
+    wait = load_once(((wd_hbm, wd), (wg_hbm, wg), (wu_hbm, wu)), sem)
+    grad = dffn_ref[...]
+    wait(0)
+    dact = mm_nt(grad, wd[...])
+    dgate = (dact * ga_ref[...].astype(F32)).astype(BF)
+    dup = (dact * gb_ref[...].astype(F32)).astype(BF)
+    dg_ref[...] = dgate
+    du_ref[...] = dup
+    wait(1)
+    part = mm_nt(dgate, wg[...])
+    wait(2)
+    part += mm_nt(dup, wu[...])
+    store_half(first, part.astype(BF), refs)
+
+
+def plane_ffn_bwd(chain, first, dffn, slopes, weights, kept, after=()):
+    length, width = dffn.shape
+    units = weights[0].shape[1]
+    block = length // 4
+    base = 2 if first is False else 0
+    steps = 4 if first is None else 2
+    tiled = lambda w: spec((block, w), lambda i, *_: (i + base, 0))
+    outs, out_specs = half_outs(first, block, width)
+    n = len(outs)
+    any_spec = pl.BlockSpec(memory_space=ANY)
+    kept = tuple(kept)
+    kernel = functools.partial(plane_ffn_bwd_kernel, first=first)
+    carried = kept[2:]
+    if first is not False:
+        body_kernel = kernel
+    else:
+        nk, nc = len(kept), len(carried)
+
+        def body_kernel(d, ga, gb, wd, wg, wu, *refs):
+            refs = refs[nk:]
+            kernel(d, ga, gb, wd, wg, wu, *refs[:n], *refs[n + nc :])
+
+    out = chain(
+        body_kernel,
+        "ffn_bwd",
+        (steps,),
+        (dffn, *slopes, weights[2], weights[0], weights[1], *kept),
+        [tiled(width), tiled(units), tiled(units)] + [any_spec] * (3 + len(kept)),
+        outs + [(c.shape, BF) for c in carried] + [((length, units), BF)] * 2,
+        out_specs + [any_spec] * len(carried) + [tiled(units)] * 2,
+        after=after,
+        aliases={}
+        if first is not False
+        else {
+            **{6 + k: n + len(carried) + k for k in range(2)},
+            **{8 + k: n + k for k in range(len(carried))},
+        },
+        scratch=[
+            pltpu.VMEM(weights[2].shape, BF),
+            pltpu.VMEM(weights[0].shape, BF),
+            pltpu.VMEM(weights[1].shape, BF),
+            pltpu.SemaphoreType.DMA((3,)),
+        ],
+        mib=60,
+        flops=3 * length * width * units * steps // 2,
+        nbytes=6 * units * width + 4 * length * units,
+    )
+    n += len(carried)
+    return out[:n], out[n:]
+
+
+def middle_kernel(x1_ref, y1_ref, r1b_ref, r2a_ref, x2_ref, y2_ref):
+    half = r1b_ref.shape[0]
+    x2_ref[...] = (r1b_ref[...].astype(F32) + y1_ref[half:].astype(F32)).astype(BF)
+    y2_ref[...] = (r2a_ref[...].astype(F32) + x1_ref[half:].astype(F32)).astype(BF)
+
+
+def middle(chain, arrived, r1b, r2a, after=()):
+    x1, y1 = arrived
+    shape = r1b.shape
+    return chain(
+        middle_kernel,
+        "middle_sum",
+        (1,),
+        (x1, y1, r1b, r2a),
+        [const_spec(a.shape) for a in (x1, y1, r1b, r2a)],
+        [(shape, BF)] * 2,
+        [spec(shape, lambda i, *_: (0, 0))] * 2,
+        after=after,
+        mib=32,
+        nbytes=16 * r1b.size,
+    )
+
+
+def own_sum(own, x1, y1, x2, y2):
+    top = pl.program_id(0) < OWN_STEPS // 2
+    direct = jnp.where(top, x1[...].astype(F32), y1[...].astype(F32))
+    relayed = jnp.where(top, y2[...].astype(F32), x2[...].astype(F32))
+    return own[...].astype(F32) + direct + relayed
+
+
+def resid_two_kernel(own, x1, y1, x2, y2, n1_ref, gain_ref, bias_ref, out_ref):
+    total = own_sum(own, x1, y1, x2, y2)
+    out_ref[...] = (deep_alpha * (n1_ref[...] * gain_ref[...] + bias_ref[...]) + total).astype(BF)
+
+
+def norm_one_back_kernel(own, x1, y1, x2, y2, dffn_ref, n1_ref, rstd_ref, gain_ref, low_ref, dr1_ref, sums_ref):
+    total = own_sum(own, x1, y1, x2, y2)
+    dh = deep_alpha * dffn_ref[...].astype(F32) + total
+    normed = n1_ref[...]
+    scaled = dh * gain_ref[...]
+    inner = jnp.mean(scaled, axis=1, keepdims=True) + normed * jnp.mean(scaled * normed, axis=1, keepdims=True)
+    dr1 = rstd_ref[:, :1] * (scaled - inner)
+    dr1_ref[...] = dr1
+    low_ref[...] = dr1.astype(BF)
+    gain_sum = jnp.sum(dh * normed, axis=0, keepdims=True)
+    bias_sum = jnp.sum(dh, axis=0, keepdims=True)
+
+    @pl.when(pl.program_id(0) == 0)
+    def _():
+        sums_ref[0:1, :] = gain_sum
+        sums_ref[1:2, :] = bias_sum
+
+    @pl.when(pl.program_id(0) > 0)
+    def _():
+        sums_ref[0:1, :] += gain_sum
+        sums_ref[1:2, :] += bias_sum
+
+
+def input_grad_kernel(own, x1, y1, x2, y2, dr1_ref, out_ref):
+    out_ref[...] = (deep_alpha * dr1_ref[...] + own_sum(own, x1, y1, x2, y2)).astype(BF)
+
+
+OWN_STEPS = 4
+
+
+def rows_spec(array_shape, tile, base=0):
+    return spec((tile, array_shape[1]), lambda i, *_: (i + base, 0))
+
+
+def own_step(chain, kernel, name, sums, extra, extra_specs, outs, after=()):
+    block, width = sums[0].shape
+    tile = block // OWN_STEPS
+    middle_step = OWN_STEPS // 2
+    first = spec((tile, width), lambda i, *_: (jnp.minimum(i, middle_step - 1), 0))
+    later = spec((tile, width), lambda i, *_: (jnp.maximum(i - middle_step, 0), 0))
+    return chain(
+        kernel,
+        name,
+        (OWN_STEPS,),
+        (*sums, *extra),
+        [rows_spec((block, width), tile), first, later, later, first] + extra_specs,
+        outs,
+        [rows_spec(s, tile) if s[0] == block else spec(s, lambda i, *_: (0, 0)) for s, _ in outs],
+        after=after,
+        mib=40,
+        nbytes=16 * block * width,
+    )
+
+
+def plane_norm_two_kernel(info_ref, order_ref, share_ref, own, r1, r2, r3a, r3b, cot_ref, gain_ref, bias_ref, *refs):
+    act_ref, sums_ref, dffn_ref, held = refs[-4:]
+    at = pl.program_id(0)
+    half = held.shape[0]
+    places = (
+        (r1, 0), (r3a, 0), (r2, half), (r3b, 0), (r1, half), (r2, 0), (own, 0), (own, half),
+    )
+    for k, (ref, start) in enumerate(places):
+
+        @pl.when(at == k)
+        def _(ref=ref, start=start):
+            held[...] = ref[start : start + half]
+
+    resid = held[...].astype(F32)
+    centered = resid - jnp.mean(resid, axis=1, keepdims=True)
+    variance = jnp.mean(centered * centered, axis=1, keepdims=True)
+    inv = lax.rsqrt(variance + norm_eps)
+    normed = centered * inv
+    gain = gain_ref[...]
+    act_ref[...] = (normed * gain + bias_ref[...]).astype(BF)
+    dout = cot_ref[...].astype(F32) * share_ref[0]
+    scaled = dout * gain
+    inner = jnp.mean(scaled, axis=1, keepdims=True) + normed * jnp.mean(scaled * normed, axis=1, keepdims=True)
+    dffn_ref[...] = (inv * (scaled - inner)).astype(BF)
+    gain_sum = jnp.sum(dout * normed, axis=0, keepdims=True)
+    bias_sum = jnp.sum(dout, axis=0, keepdims=True)
+
+    @pl.when(at == 0)
+    def _():
+        sums_ref[0:1, :] = gain_sum
+        sums_ref[1:2, :] = bias_sum
+
+    @pl.when(at > 0)
+    def _():
+        sums_ref[0:1, :] += gain_sum
+        sums_ref[1:2, :] += bias_sum
+
+
+def plane_norm_two(chain, info, order, share, row, pieces, cotangent, gain, bias, before, after=()):
+    rows, length, width = cotangent.shape
+    half = length // 8
+    natural = spec((None, half, width), lambda i, info, order, share: (row, order[i], 0))
+    held = () if before is None else (before,)
+    return chain(
+        plane_norm_two_kernel,
+        "norm_two",
+        (8,),
+        (*pieces, cotangent, gain, bias, *held),
+        [const_spec(p.shape) for p in pieces]
+        + [natural, const_spec((1, width)), const_spec((1, width))]
+        + [pl.BlockSpec(memory_space=ANY)] * len(held),
+        [(cotangent.shape, BF), ((2, width), F32), ((length, width), BF)],
+        [natural, spec((2, width), lambda i, *_: (0, 0)), spec((half, width), lambda i, *_: (i, 0))],
+        scalars=(info, order, share),
+        after=after,
+        aliases={len(pieces) + 3: 0} if held else {},
+        scratch=[pltpu.VMEM((half, width), BF)],
+        flops=20 * length * width,
+        nbytes=8 * length * width,
+    )
+
+
+def plane_input_back_kernel(order_ref, low_ref, high_ref, w_ref, x1_ref, y1_ref, r1b_ref, r2a_ref, own_ref):
+    at = pl.program_id(0)
+    half = low_ref.shape[0]
+    part = mm_nt(jnp.concatenate([low_ref[...], high_ref[...]], axis=0), w_ref[...]).astype(BF)
+
+    @pl.when(at == 0)
+    def _():
+        x1_ref[...] = part
+
+    @pl.when(at == 1)
+    def _():
+        y1_ref[...] = part
+
+    @pl.when(at == 2)
+    def _():
+        r1b_ref[...] = part[:half]
+        r2a_ref[...] = part[half:]
+
+    @pl.when(at == 3)
+    def _():
+        own_ref[...] = part
+
+
+def plane_input_back(chain, order, dqkv, qkv_weight, after=()):
+    length, columns = dqkv.shape
+    width = qkv_weight.shape[0]
+    block = length // 4
+    half = block // 2
+    sizes = [block, block, half, half, block]
+    return chain(
+        plane_input_back_kernel,
+        "input_back",
+        (4,),
+        (dqkv, dqkv, qkv_weight),
+        [
+            spec((half, columns), lambda i, order: (order[2 * i], 0)),
+            spec((half, columns), lambda i, order: (order[2 * i + 1], 0)),
+            const_spec(qkv_weight.shape),
+        ],
+        [((s, width), BF) for s in sizes],
+        [spec((s, width), lambda i, *_: (0, 0)) for s in sizes],
+        scalars=(order,),
+        after=after,
+        flops=2 * length * width * columns,
+        nbytes=2 * width * columns + 4 * length * width,
+    )
+
+
+def plane_place_kernel(order_ref, own, r1, r2, r3a, r3b, *refs):
+    out_ref = refs[-1]
+    at = pl.program_id(0)
+    half = r3a.shape[0]
+    for k, ref in enumerate((own, r1, r2)):
+
+        @pl.when(at == k)
+        def _(ref=ref):
+            out_ref[...] = ref[...]
+
+    @pl.when(at == 3)
+    def _():
+        out_ref[:half] = r3a[...]
+        out_ref[half:] = r3b[...]
+
+
+def plane_place(chain, info, row, pieces, shape, before, after=()):
+    rows, length, width = shape
+    block = length // 4
+    held = () if before is None else (before,)
+    return chain(
+        plane_place_kernel,
+        "place",
+        (4,),
+        (*pieces, *held),
+        [const_spec(p.shape) for p in pieces] + [pl.BlockSpec(memory_space=ANY)] * len(held),
+        [(shape, BF)],
+        [spec((None, block, width), lambda i, info: (row, i ^ info[0], 0))],
+        scalars=(info,),
+        after=after,
+        aliases={len(pieces): 0} if held else {},
+        mib=32,
+        nbytes=4 * length * width,
+    )[0]
+
+
+def panels(ref, value):
+    for c in range(value.shape[1] // 128):
+        ref[c] = value[:, c * 128 : (c + 1) * 128].astype(BF)
+
+
+def grad_rows_kernel(info_ref, left_a, left_b, right_a, right_b, send, keep, *, steps):
+    at = pl.program_id(0)
+    value = mm(left_a[...].T, right_a[...]) + mm(left_b[...].T, right_b[...])
+
+    @pl.when(at < steps)
+    def _():
+        panels(send, value)
+
+    @pl.when(at >= steps)
+    def _():
+        panels(keep, value)
+
+
+def lhs_spec(lhs, tile, index, row):
+    if lhs.ndim == 3:
+        return spec((None, lhs.shape[1], tile), lambda *a: (row, 0, index(*a)))
+    return spec((lhs.shape[0], tile), lambda *a: (0, index(*a)))
+
+
+def grad_rows(chain, info, lefts, rights, after=()):
+    rows = lefts[0].shape[-1]
+    tile = 256
+    steps = rows // tile // 2
+    length, columns = rights[0].shape
+
+    def at(i, info):
+        other = (1 - info[3]) * steps + i
+        own = info[3] * steps + i - steps
+        return jnp.where(i < steps, other, own)
+
+    shape = (columns // 128, rows // 2, 128)
+    out = chain(
+        functools.partial(grad_rows_kernel, steps=steps),
+        "grad_rows",
+        (2 * steps,),
+        (*lefts, *rights),
+        [lhs_spec(lefts[r], tile, at, r) for r in range(2)] + [const_spec(r.shape) for r in rights],
+        [(shape, BF)] * 2,
+        [
+            spec((shape[0], tile, 128), lambda i, *_: (0, jnp.minimum(i, steps - 1), 0)),
+            spec((shape[0], tile, 128), lambda i, *_: (0, jnp.maximum(i - steps, 0), 0)),
+        ],
+        scalars=(info,),
+        after=after,
+        flops=4 * rows * length * columns,
+        nbytes=2 * rows * columns + 4 * rows * length,
+    )
+    return out[0].reshape(-1, 128), out[1].reshape(-1, 128)
+
+
+def grad_columns_kernel(info_ref, left_a, left_b, right_a, right_b, send, keep, turned_a, turned_b, held):
+    @pl.when(pl.program_id(0) == 0)
+    def _():
+        turned_a[...] = left_a[...].T
+        turned_b[...] = left_b[...].T
+
+    held[...] = mm(turned_a[...], right_a[...]) + mm(turned_b[...], right_b[...])
+    half = held.shape[0] // 2
+    core = info_ref[3]
+    panels(send, held[pl.ds(pl.multiple_of((1 - core) * half, 8), half), :])
+    panels(keep, held[pl.ds(pl.multiple_of(core * half, 8), half), :])
+
+
+def grad_columns(chain, info, lefts, rights, after=()):
+    length, rows = lefts[0].shape
+    columns = rights[0].shape[1]
+    tile = 256
+    shape = (columns // 128, rows // 2, 128)
+    out = chain(
+        grad_columns_kernel,
+        "grad_columns",
+        (columns // tile,),
+        (*lefts, *rights),
+        [const_spec(left.shape) for left in lefts] + [spec((length, tile), lambda i, *_: (0, i))] * 2,
+        [(shape, BF)] * 2,
+        [spec((tile // 128, rows // 2, 128), lambda i, *_: (i, 0, 0))] * 2,
+        scalars=(info,),
+        after=after,
+        scratch=[pltpu.VMEM((rows, length), BF)] * 2 + [pltpu.VMEM((rows, tile), F32)],
+        flops=4 * rows * length * columns,
+        nbytes=2 * rows * columns + 4 * length * (rows + columns),
+    )
+    return out[0].reshape(-1, 128), out[1].reshape(-1, 128)
+
+
+def grad_plain_kernel(left_a, left_b, right_a, right_b, out_ref):
+    out_ref[...] = (mm(left_a[...].T, right_a[...]) + mm(left_b[...].T, right_b[...])).astype(BF)
+
+
+def grad_plain(chain, lefts, rights, after=()):
+    rows = lefts[0].shape[-1]
+    tile = 256
+    length, columns = rights[0].shape
+    return chain(
+        grad_plain_kernel,
+        "grad_plain",
+        (rows // tile,),
+        (*lefts, *rights),
+        [lhs_spec(lefts[r], tile, lambda i, *_: i, r) for r in range(2)] + [const_spec(r.shape) for r in rights],
+        [((rows, columns), BF)],
+        [spec((tile, columns), lambda i, *_: (i, 0))],
+        after=after,
+        flops=4 * rows * length * columns,
+        nbytes=2 * rows * columns + 4 * rows * length,
+    )[0]
+
+
+def grad_plain_columns_kernel(left_a, left_b, right_a, right_b, out_ref, turned_a, turned_b):
+    @pl.when(pl.program_id(0) == 0)
+    def _():
+        turned_a[...] = left_a[...].T
+        turned_b[...] = left_b[...].T
+
+    out_ref[...] = (mm(turned_a[...], right_a[...]) + mm(turned_b[...], right_b[...])).astype(BF)
+
+
+def grad_plain_columns(chain, lefts, rights, after=()):
+    length, rows = lefts[0].shape
+    columns = rights[0].shape[1]
+    tile = 256
+    return chain(
+        grad_plain_columns_kernel,
+        "grad_plain_columns",
+        (columns // tile,),
+        (*lefts, *rights),
+        [const_spec(left.shape) for left in lefts] + [spec((length, tile), lambda i, *_: (0, i))] * 2,
+        [((rows, columns), BF)],
+        [spec((rows, tile), lambda i, *_: (0, i))],
+        after=after,
+        scratch=[pltpu.VMEM((rows, length), BF)] * 2,
+        flops=4 * rows * length * columns,
+        nbytes=2 * rows * columns + 4 * length * (rows + columns),
+    )[0]
+
+
+def grad_out(lhs, pieces, me):
+    block = pieces[0].shape[0]
+    half = block // 2
+    total = 0.0
+    for r, piece in enumerate(pieces[:3]):
+        part = lhs[pl.ds(pl.multiple_of((me ^ r) * block, half), block), :]
+        total = total + mm(part.T, piece[...])
+    for lower, piece in ((0, pieces[3]), (half, pieces[4])):
+        part = lhs[pl.ds(pl.multiple_of((me ^ 3) * block + lower, half), half), :]
+        total = total + mm(part.T, piece[...])
+    return total
+
+
+def grad_out_kernel(info_ref, left_a, left_b, *refs):
+    pieces_a, pieces_b, (send, keep, held) = refs[:5], refs[5:10], refs[10:]
+    held[...] = grad_out(left_a, pieces_a, info_ref[0]) + grad_out(left_b, pieces_b, info_ref[0])
+    half = held.shape[0] // 2
+    core = info_ref[3]
+    panels(send, held[pl.ds(pl.multiple_of((1 - core) * half, 8), half), :])
+    panels(keep, held[pl.ds(pl.multiple_of(core * half, 8), half), :])
+
+
+def plane_grad_out(chain, info, lefts, pieces, after=()):
+    length, rows = lefts[0].shape
+    columns = pieces[0][0].shape[1]
+    tile = 512
+    shape = (columns // 128, rows // 2, 128)
+    every = (*pieces[0], *pieces[1])
+    out = chain(
+        grad_out_kernel,
+        "grad_out",
+        (columns // tile,),
+        (*lefts, *every),
+        [const_spec(left.shape) for left in lefts]
+        + [spec((p.shape[0], tile), lambda i, *_: (0, i)) for p in every],
+        [(shape, BF)] * 2,
+        [spec((tile // 128, rows // 2, 128), lambda i, *_: (i, 0, 0))] * 2,
+        scalars=(info,),
+        after=after,
+        scratch=[pltpu.VMEM((rows, tile), F32)],
+        flops=4 * rows * length * columns,
+        nbytes=2 * rows * columns + 4 * length * (rows + columns),
+    )
+    return out[0].reshape(-1, 128), out[1].reshape(-1, 128)
+
+
+class Line:
+    GRID = 4
+
+    def __init__(self, chain, edge):
+        self.chain, self.edge = chain, edge
+        self.pending = []
+        self.slots = []
+        self.step = 0
+        self.done = {}
+        self.first = self.second = None
+        self.sent = self.mid = None
+
+    def add(self, name, keep, got, chunks):
+        for k in range(chunks):
+            self.pending.append((name, keep, got, k, keep.shape[0] // chunks, keep.shape[0]))
+
+    def get(self, j):
+        return self.slots[j] if j >= 0 else None
+
+    def busy(self):
+        return bool(self.pending) or any(self.slots[-3:])
+
+    def complete(self, name):
+        return not any(slot and slot[0] == name for slot in self.pending + self.slots[-3:])
+
+    def advance(self, after=()):
+        j = self.step
+        self.slots.append(self.pending.pop(0) if self.pending else None)
+        new, cur, prev, last = self.get(j), self.get(j - 1), self.get(j - 2), self.get(j - 3)
+        ins, in_specs, outs, out_specs, aliases, roles = [], [], [], [], {}, []
+        grid = self.GRID
+
+        def give(array, rows, base, role, when):
+            block = rows // grid
+            if when is None:
+                index = lambda i, edge: (base + i, 0)
+            elif when:
+                index = lambda i, edge: (base + i * edge[0], 0)
+            else:
+                index = lambda i, edge: (base + i * (1 - edge[0]), 0)
+            ins.append(array)
+            in_specs.append(spec((block, 128), index))
+            roles.append(role)
+
+        if new:
+            name, keep, got, k, rows, _ = new
+            give(keep, rows, k * grid, "new_keep", True)
+            give(got, rows, k * grid, "new_got", True)
+        if cur:
+            name, keep, got, k, rows, _ = cur
+            give(keep, rows, k * grid, "cur_keep", False)
+            give(got, rows, k * grid, "cur_got", False)
+            give(self.first, rows, 0, "cur_in", False)
+        if prev:
+            rows = prev[4]
+            give(self.mid, rows, 0, "prev_mid", False)
+            give(self.second, rows, 0, "prev_in", False)
+        if last:
+            rows = last[4]
+            give(self.first, rows, 0, "last_in", True)
+            give(self.sent, rows, 0, "last_sent", False)
+            if last[3] > 0:
+                ins.append(self.done[last[0]])
+                in_specs.append(pl.BlockSpec(memory_space=ANY))
+                roles.append("held")
+        names = []
+        if new or prev:
+            rows = max(c[4] for c in (new, prev) if c)
+            outs.append(((rows, 128), BF))
+            out_specs.append(pl.BlockSpec((rows, 128), lambda i, *_: (0, 0)))
+            names.append("sent")
+        if cur:
+            outs.append(((cur[4], 128), BF))
+            out_specs.append(spec((cur[4] // grid, 128), lambda i, *_: (i, 0)))
+            names.append("mid")
+        if last:
+            base = last[3] * grid
+            outs.append(((last[5], 128), BF))
+            out_specs.append(spec((last[4] // grid, 128), lambda i, *_, base=base: (base + i, 0)))
+            names.append("done")
+            if last[3] > 0:
+                aliases = {len(ins) - 1: len(outs) - 1}
+
+        def kernel(edge_ref, *refs):
+            src = dict(zip(roles, refs[: len(roles)]))
+            dst = dict(zip(names, refs[len(roles) :]))
+            at = pl.program_id(0)
+            is_edge = edge_ref[0] == 1
+            f32 = lambda r: src[r][...].astype(F32)
+
+            if new:
+                @pl.when(is_edge)
+                def _():
+                    block = new[4] // grid
+                    rows = pl.ds(pl.multiple_of(at * block, block), block)
+                    dst["sent"][rows, :] = (f32("new_keep") + f32("new_got")).astype(BF)
+
+            @pl.when(jnp.logical_not(is_edge))
+            def _():
+                if cur:
+                    dst["mid"][...] = (f32("cur_keep") + f32("cur_got") + f32("cur_in")).astype(BF)
+                if prev:
+                    block = prev[4] // grid
+                    rows = pl.ds(pl.multiple_of(at * block, block), block)
+                    dst["sent"][rows, :] = (f32("prev_mid") + f32("prev_in")).astype(BF)
+
+            if last:
+                @pl.when(is_edge)
+                def _():
+                    dst["done"][...] = src["last_in"][...]
+
+                @pl.when(jnp.logical_not(is_edge))
+                def _():
+                    dst["done"][...] = src["last_sent"][...]
+
+        out = self.chain(
+            kernel,
+            "line_step",
+            (grid,),
+            tuple(ins),
+            in_specs,
+            outs,
+            out_specs,
+            scalars=(self.edge,),
+            after=after,
+            aliases=aliases,
+            mib=32,
+            nbytes=6 * 5632 * 256,
+        )
+        got = dict(zip(names, out))
+        if "done" in got:
+            self.done[last[0]] = got["done"]
+        self.sent = got.get("sent")
+        self.mid = got.get("mid")
+        if self.sent is not None:
+            self.first = lax.ppermute(self.sent, "obj", [(0, 1), (3, 2), (1, 0), (2, 3)])
+        if self.mid is not None:
+            self.second = lax.ppermute(self.mid, "obj", [(1, 2), (2, 1)])
+        self.step += 1
+
+
+def widen_kernel(info_ref, mine_ref, theirs_ref, out_ref, *, steps):
+    at = pl.program_id(0)
+
+    @pl.when(at < steps)
+    def _():
+        for c in range(mine_ref.shape[0]):
+            out_ref[:, c * 128 : (c + 1) * 128] = mine_ref[c].astype(F32)
+
+    @pl.when(at >= steps)
+    def _():
+        for c in range(theirs_ref.shape[0]):
+            out_ref[:, c * 128 : (c + 1) * 128] = theirs_ref[c].astype(F32)
+
+
+def widen(chain, info, mine, theirs, rows, columns, after=()):
+    count = columns // 128
+    half = rows // 2
+    tile = 176 if half % 176 == 0 else min(256, half)
+    steps = half // tile
+    mine, theirs = (a.reshape(count, half, 128) for a in (mine, theirs))
+
+    def at(i, info):
+        return jnp.where(i < steps, info[3] * steps + i, (1 - info[3]) * steps + i - steps)
+
+    return chain(
+        functools.partial(widen_kernel, steps=steps),
+        "widen",
+        (2 * steps,),
+        (mine, theirs),
+        [
+            spec((count, tile, 128), lambda i, *_: (0, jnp.minimum(i, steps - 1), 0)),
+            spec((count, tile, 128), lambda i, *_: (0, jnp.maximum(i - steps, 0), 0)),
+        ],
+        [((rows, columns), F32)],
+        [spec((tile, columns), lambda i, info: (at(i, info), 0))],
+        scalars=(info,),
+        after=after,
+        mib=32,
+        nbytes=6 * rows * columns,
+    )[0]
+
+
+def add_small_kernel(a_ref, b_ref, out_ref):
+    out_ref[...] = a_ref[...] + b_ref[...]
+
+
+def add_small(chain, a, b):
+    return chain(
+        add_small_kernel, "add_small", (1,), (a, b), [const_spec(a.shape)] * 2, [(a.shape, F32)],
+        [spec(a.shape, lambda i, *_: (0, 0))],
+    )[0]
+
+
+def plane_body(
+    tokens,
+    cotangent,
+    segment_ids,
+    mlm_mask,
+    glm_prefix,
+    glm_span,
+    qkv_weight,
+    out_weight,
+    gate_weight,
+    up_weight,
+    down_weight,
+    norm1_gain,
+    norm1_bias,
+    norm2_gain,
+    norm2_bias,
+):
+    seq_here, length, width = tokens.shape
+    data_ways = lax.axis_size("dp")
+    objective_ways = lax.axis_size("obj")
+    me = lax.axis_index("tensor").astype(jnp.int32)
+    core = lax.axis_index("dp").astype(jnp.int32)
+    at_obj = lax.axis_index("obj")
+    edge = ((at_obj == 0) | (at_obj == objective_ways - 1)).astype(jnp.int32).reshape(1)
+    block = length // 4
+    units = gate_weight.shape[1]
+    rows_all = mlm_mask.shape[0]
+    masked_limit = seq_here * data_ways * (objective_ways // 2)
+    row_ids = jnp.arange(rows_all, dtype=jnp.int32)
+    counts = jnp.where(row_ids < masked_limit, jnp.sum(mlm_mask, axis=1), glm_span).astype(F32)
+    weight_all = counts * rows_all / jnp.sum(counts)
+    first_row = (at_obj * data_ways + core) * seq_here
+    share_here = lax.dynamic_slice_in_dim(weight_all, first_row, seq_here)
+    prefix_here = lax.dynamic_slice_in_dim(glm_prefix, first_row, seq_here)
+    span_here = lax.dynamic_slice_in_dim(glm_span, first_row, seq_here)
+    open_here = jnp.where(first_row < masked_limit, length, prefix_here)
+    info = [jnp.stack([me, open_here[r], prefix_here[r] + span_here[r], core]) for r in range(2)]
+    order = jnp.stack([2 * (me ^ r) + h for r, h in ORDER])
+    share = [share_here[r : r + 1] for r in range(2)]
+    cosine, sine = constant_tables(length)
+    segc = [segment_ids[r].reshape(length, 1) for r in range(2)]
+    segr = [segment_ids[r].reshape(1, length) for r in range(2)]
+    gain1, bias1 = norm1_gain.reshape(1, width), norm1_bias.reshape(1, width)
+    gain2, bias2 = norm2_gain.reshape(1, width), norm2_bias.reshape(1, width)
+    weights = (gate_weight, up_weight, down_weight)
+    chain = Chain()
+    A, B = 0, 1
+
+    ow_half = out_weight.shape[0] // 2
+    ow_own = lax.dynamic_slice_in_dim(out_weight, core * ow_half, ow_half)
+    owx, owy = pair_swap(ow_own, ow_own)
+
+    def attention(r, after=()):
+        return plane_attn_fwd(chain, info[r], r, tokens, qkv_weight, cosine, sine, segc[r], segr[r], after)
+
+    def out_and_norm(r, ol_pieces, after=()):
+        return plane_out_norm(
+            chain, info[r], order, r, ol_pieces, out_weight, ow_mine, ow_other, tokens, gain1, bias1, after
+        )
+
+    qkv, ol, lse, hl, n1, rstd = {}, {}, {}, {}, {}, {}
+    qkv[A], ol[A], lse[A] = attention(A)
+    owra, owrb = forward(chain, owx, owy)
+    olx, oly, olr = {}, {}, {}
+    olx[A], oly[A] = pair_swap(ol[A], ol[A])
+    qkv[B], ol[B], lse[B] = attention(B)
+    ow_mine = ow_join(chain, (owx, owy, owra, owrb), after=(olx[A], oly[A]))
+    ow_other = lax.ppermute(ow_mine, "dp", CORES)
+    halves, ol[B] = forward(chain, olx[A], oly[A], (ol[B],))
+    olr[A], ol[B] = join_halves(chain, halves, ol[B])
+    olx[B], oly[B] = pair_swap(ol[B], ol[B])
+    hl[A], n1[A], rstd[A] = out_and_norm(A, (ol[A], olx[A], oly[A], olr[A]))
+    vec = const_spec((1, width))
+    tile = block // OWN_STEPS
+    full = rows_spec((block, width), tile)
+    ff, fb, ib, rs1, rs2 = {}, {}, {}, {}, {}
+    resid, rx, ry, rr = {}, {}, {}, {}
+
+    def sums_of(own, first, second):
+        return (own, first[0], first[1], second[0], second[1])
+
+    def second_resid(r, after=()):
+        return own_step(
+            chain, resid_two_kernel, "resid_two", sums_of(ff[r][2], rs1[r], rs2[r]), (n1[r], gain1, bias1),
+            [full, vec, vec], [((block, width), BF)], after,
+        )[0]
+
+    def second_norm(r, before, after=()):
+        pieces = (resid[r], rx[r], ry[r], *rr[r])
+        return plane_norm_two(
+            chain, info[r], order, share[r], r, pieces, cotangent, gain2, bias2, before, after
+        )
+
+    def first_norm_back(r, after=()):
+        return own_step(
+            chain, norm_one_back_kernel, "norm_one_back", sums_of(fb[r][2], rs1[r], rs2[r]),
+            (dffn[r], n1[r], rstd[r], gain1),
+            [rows_spec((block, width), tile, 3 * OWN_STEPS), full, rows_spec((block, HEAD_DIM), tile), vec],
+            [((block, width), BF), ((block, width), F32), ((2, width), F32)], after,
+        )
+
+    olrb = forward(chain, olx[B], oly[B])
+    sent, kept = plane_ffn_fwd(chain, True, hl[A], weights, ())
+    rs1[A] = pair_swap(*sent)
+    ff[A], kept_a = plane_ffn_fwd(chain, False, hl[A], weights, kept)
+    olr[B], rstd[A] = join_halves(chain, olrb, rstd[A])
+    hl[B], n1[B], rstd[B] = out_and_norm(B, (ol[B], olx[B], oly[B], olr[B]))
+    rs2[A] = pair_swap(*middle(chain, rs1[A], ff[A][0], ff[A][1]))
+    sent, kept = plane_ffn_fwd(chain, True, hl[B], weights, (), after=(*rs1[A],))
+    resid[A] = second_resid(A)
+    rx[A], ry[A] = pair_swap(resid[A], resid[A])
+    ff[B], kept_b = plane_ffn_fwd(chain, False, hl[B], weights, (*kept, *sent))
+    al, slopes = {A: kept_a[0], B: kept_b[0]}, {A: kept_a[1:], B: kept_b[1:]}
+    rr[A], *sent = forward(chain, rx[A], ry[A], ff[B][3:])
+    rs1[B] = pair_swap(*sent)
+
+    sums2, dffn, dgu, sums1, dr1, dattn, dax, day, dar = {}, {}, {}, {}, {}, {}, {}, {}, {}
+    activations, sums2[A], dffn[A] = second_norm(A, None)
+    rs2[B] = pair_swap(*middle(chain, rs1[B], ff[B][0], ff[B][1]))
+    sent, kept = plane_ffn_bwd(chain, True, dffn[A], slopes[A], weights, ())
+    resid[B] = second_resid(B)
+    rx[B], ry[B] = pair_swap(resid[B], resid[B])
+    fb[A], dgu[A] = plane_ffn_bwd(chain, False, dffn[A], slopes[A], weights, (*kept, *sent))
+    rr[B], *sent = forward(chain, rx[B], ry[B], fb[A][3:])
+    rs1[A] = pair_swap(*sent)
+    activations, sums2[B], dffn[B] = second_norm(B, activations)
+    down_update = grad_plain_columns(chain, (al[A], al[B]), (dffn[A], dffn[B]))
+    down_sum = lax.psum(down_update, ("obj", "dp"))
+    rs2[A] = pair_swap(*middle(chain, rs1[A], fb[A][0], fb[A][1]))
+    sent, dgu[B] = plane_ffn_bwd(chain, None, dffn[B], slopes[B], weights, ())
+    fb[B] = sent[2:]
+    dattn[A], dr1[A], sums1[A] = first_norm_back(A)
+    dax[A], day[A] = pair_swap(dattn[A], dattn[A])
+    rs1[B] = pair_swap(*sent[:2])
+    gate_send, gate_keep = grad_rows(chain, info[B], (hl[A], hl[B]), (dgu[A][0], dgu[B][0]))
+    line = Line(chain, edge)
+    line.add("gate", gate_keep, lax.ppermute(gate_send, "dp", CORES), 2)
+    rs2[B] = pair_swap(*middle(chain, rs1[B], fb[B][0], fb[B][1], after=(dax[A], day[A])))
+    dar[A] = forward(chain, dax[A], day[A])
+    up_send, up_keep = grad_rows(chain, info[B], (hl[A], hl[B]), (dgu[A][1], dgu[B][1]))
+    line.add("up", up_keep, lax.ppermute(up_send, "dp", CORES), 2)
+    line.advance()
+    dattn[B], dr1[B], sums1[B] = first_norm_back(B)
+    dax[B], day[B] = pair_swap(dattn[B], dattn[B])
+
+    pieces, dqkv, dx, dxx, dxy, dxr = {}, {}, {}, {}, {}, {}
+
+    def attention_back(r, after=()):
+        pieces[r] = (dattn[r], dax[r], day[r], *dar[r])
+        return plane_attn_bwd(
+            chain, info[r], qkv[r], pieces[r], out_weight, lse[r], cosine, sine, segc[r], segr[r], after
+        )
+
+    def input_back_sums(r, after=()):
+        x1, y1, r1b, r2a, own = plane_input_back(chain, order, dqkv[r], qkv_weight, after)
+        ib[r] = (r1b, r2a, own)
+        rs1[r] = pair_swap(x1, y1)
+
+    def input_grad_own(r, after=()):
+        return own_step(
+            chain, input_grad_kernel, "input_grad", sums_of(ib[r][2], rs1[r], rs2[r]), (dr1[r],), [full],
+            [((block, width), BF)], after,
+        )[0]
+
+    outs = {}
+
+    def finish_matrix(name, rows, columns, after=()):
+        mine = line.done[name]
+        theirs = lax.ppermute(mine, "dp", CORES)
+        outs[name] = widen(chain, info[B], mine, theirs, rows, columns, after)
+
+    mine = (me == 0).astype(F32)
+    sums = jnp.concatenate([sums1[A] + sums1[B], (sums2[A] + sums2[B]) * mine])
+    exchanges = [("dp", 1), ("tensor", 1), ("tensor", 2), ("obj", 1), ("obj", 2)]
+
+    def exchange(array):
+        axis, bit = exchanges.pop(0)
+        other = lax.ppermute(array, axis, [(i, i ^ bit) for i in range(lax.axis_size(axis))])
+        return array, other
+
+    dqkv[A] = attention_back(A)
+    pair = exchange(sums)
+    line.advance()
+    dar[B] = forward(chain, dax[B], day[B])
+    input_back_sums(A)
+    line.advance()
+    pair = exchange(add_small(chain, *pair))
+    dqkv[B] = attention_back(B)
+    rs2[A] = pair_swap(*middle(chain, rs1[A], ib[A][0], ib[A][1]))
+    line.advance()
+    pair = exchange(add_small(chain, *pair))
+    qkv_send, qkv_keep = grad_rows(chain, info[B], (tokens, tokens), (dqkv[A], dqkv[B]), after=(down_sum,))
+    line.add("qkv", qkv_keep, lax.ppermute(qkv_send, "dp", CORES), 3)
+    dx[A] = input_grad_own(A)
+    dxx[A], dxy[A] = pair_swap(dx[A], dx[A])
+    input_back_sums(B)
+    line.advance()
+    pair = exchange(add_small(chain, *pair))
+    out_send, out_keep = plane_grad_out(chain, info[B], (ol[A], ol[B]), (pieces[A], pieces[B]))
+    line.add("out", out_keep, lax.ppermute(out_send, "dp", CORES), 1)
+    dxr[A] = forward(chain, dxx[A], dxy[A])
+    rs2[B] = pair_swap(*middle(chain, rs1[B], ib[B][0], ib[B][1]))
+    line.advance()
+    pair = exchange(add_small(chain, *pair))
+    input_grad = plane_place(chain, info[A], A, (dx[A], dxx[A], dxy[A], *dxr[A]), tokens.shape, None)
+    dx[B] = input_grad_own(B)
+    dxx[B], dxy[B] = pair_swap(dx[B], dx[B])
+    finish_matrix("gate", width, units)
+    line.advance()
+    sums = add_small(chain, *pair)
+    dxr[B] = forward(chain, dxx[B], dxy[B])
+    finish_matrix("up", width, units)
+    line.advance()
+    input_grad = plane_place(chain, info[B], B, (dx[B], dxx[B], dxy[B], *dxr[B]), tokens.shape, input_grad)
+    while line.busy():
+        line.advance()
+        if "qkv" not in outs and line.complete("qkv"):
+            finish_matrix("qkv", width, qkv_weight.shape[1])
+    finish_matrix("out", out_weight.shape[0], width)
+    outs["down"] = down_sum.astype(F32)
+
+    return (
+        activations,
+        input_grad,
+        outs["qkv"],
+        outs["out"],
+        outs["gate"],
+        outs["up"],
+        outs["down"],
+        sums[0],
+        sums[1],
+        sums[2],
+        sums[3],
+    )
+
+
+def body(*args):
+    if plane_case(args[0].shape, args[10].shape):
+        return plane_body(*args)
+    return general_body(*args)
+
+
 def solution(mesh):
     rows3 = P(("obj", "dp"), None, None)
     in_specs = (

time: 1430 us -> 1030 us (0.72)
  waiting for transfers between devices: 653 us -> 221 us
  Pallas kernels: 305 us -> 620 us
  other arithmetic: 122 us -> 15.4 us
  matrix products: 104 us -> 0 us
  blocking collectives: 51.1 us -> 0 us
  local copies, waits for them, and re-layouts: 57.9 us -> 28.2 us
    pallas_call x16 -> x68, Pallas kernels: 305 us -> 620 us  [call(): pl.pallas_call(wrapped, grid_spec=grid_spec, out_shape=[jax.ShapeDtypeStr...]
    ppermute x28 -> x32, waiting for transfers between devices: 350 us -> 124 us  [the longest x10 89.6 us: advance(): lax.ppermute(self.sent, 'obj', [(0, 1), (3, 2), (1, 0), (2, 3)])]
    ppermute x90 -> x60, waiting for transfers between devices: 303 us -> 96 us  [swap(): return lax.ppermute(array, 'tensor', [(i, i ^ bit) for i in range(ways)])]
    dot_general x12 -> x0, matrix products: 104 us -> none  [the longest x10 98.9 us: mm_tn(): lax.dot_general(a, b, (((0,), (0,)), ((), ())), preferred_element_type=F32)]
    convert_element_type x34 -> x1, other arithmetic: 70 us -> 8.68 us  [plane_body(): outs['down'] = down_sum.astype(F32)]
    psum x1 -> x0, blocking collectives: 51.1 us -> none  [body(): sums = lax.psum(sums, ('obj', 'dp', 'tensor'))]
    ppermute x90 -> x60, starting transfers between devices: 93 us -> 63.7 us  [swap(): return lax.ppermute(array, 'tensor', [(i, i ^ bit) for i in range(ways)])]
    ppermute x28 -> x32, starting transfers between devices: 32.3 us -> 52.6 us  [the longest x10 34.1 us: advance(): lax.ppermute(self.sent, 'obj', [(0, 1), (3, 2), (1, 0), (2, 3)])]
  transfers between devices with their start and end apart: 118 -> 93, of which waited for: 55 -> 28; matrix products, arithmetic and copies ran while one was open for 17% -> 2% of each run, Pallas kernels for 15% -> 56%
where the time goes in v2:
time: 1030 us; the launch traced here: 1020 us
  Pallas kernels  620 us (60%)
  waiting for transfers between devices  221 us (21%)
  starting transfers between devices  116 us (11%)
  local copies, waits for them, and re-layouts  28.2 us (3%)
  between operations  17.5 us (2%)
  other arithmetic  15.4 us (1%)
    pallas_call x68, Pallas kernels, call(): pl.pallas_call(wrapped, grid_spec=grid_spec, out_shape=[jax.ShapeDtypeStr...  620 us
    ppermute x60, waiting for transfers between devices, swap(): return lax.ppermute(array, 'tensor', [(i, i ^ bit) for i in range(ways)])  96 us
    ppermute x10, waiting for transfers between devices, advance(): lax.ppermute(self.sent, 'obj', [(0, 1), (3, 2), (1, 0), (2, 3)])  89.6 us
    ppermute x60, starting transfers between devices, swap(): return lax.ppermute(array, 'tensor', [(i, i ^ bit) for i in range(ways)])  63.7 us
    ppermute x10, starting transfers between devices, advance(): lax.ppermute(self.sent, 'obj', [(0, 1), (3, 2), (1, 0), (2, 3)])  34.1 us
    ppermute x5, waiting for transfers between devices, exchange(): lax.ppermute(array, axis, [(i, i ^ bit) for i in range(lax.axis_size(axis...  31 us
  transfers between devices with their start and end apart: 93, of which 28 were waited for; matrix products, arithmetic and copies ran while one was open for 2% of the time, Pallas kernels for 56%

profile of v2, /device:TPU:0, one launch (start us, length us, event | category | flops | bytes accessed | tf_op | source)
XLA Modules:
  0.0 1018.4 jit_solution(17841873517240872509)
XLA Ops:
  21.6 27.5 %attn_fwd.2 = (bf16[1024,1536]{1,0:T(8,128)(2,1)}, bf16[1024,512]{1,0:T(8,128)(2,1)}, f32[4,1,1024]{2,1,0:T(1,128)}) custom-call(s32[4]{0:T(128)} %add_add_fusion.1.refs_0_, bf16[2,1024,2048]{2,1,0:T(8,128)(2,1)} %refs_2_.13, bf16[2048,1536]{1,0:T(8,128)(2,1)} %refs_3_.19, f32[1024,128]{1,0:T(8,128)} %constant.39.clone.refs_3_.refs_9_, ...), custom_call_target="tpu_custom_call" | custom-call | flops 107374182400 | bytes 146800640 | tf_op jit(solution)/shard_map/attn_fwd/pallas_call | solution.py:831
  60.0 27.7 %attn_fwd.3 = (bf16[1024,1536]{1,0:T(8,128)(2,1)}, bf16[1024,512]{1,0:T(8,128)(2,1)}, f32[4,1,1024]{2,1,0:T(1,128)}) custom-call(s32[4]{0:T(128)} %add_add_fusion.refs_0_, bf16[2,1024,2048]{2,1,0:T(8,128)(2,1)} %refs_2_.13, bf16[2048,1536]{1,0:T(8,128)(2,1)} %refs_3_.19, f32[1024,128]{1,0:T(8,128)} %constant.39.clone.refs_3_.refs_9_, ...), custom_call_target="tpu_custom_call" | custom-call | flops 107374182400 | bytes 146800640 | tf_op jit(solution)/shard_map/attn_fwd/pallas_call | solution.py:831
  114.5 20.4 %out_norm.2 = (bf16[1024,2048]{1,0:T(8,128)(2,1)}, f32[256,2048]{1,0:T(8,128)}, f32[256,128]{1,0:T(8,128)}) custom-call(s32[4]{0:T(128)} %add_add_fusion.1.refs_0_, s32[8]{0:T(128)} %stack.54.refs_1_.refs_0_, bf16[1024,512]{1,0:T(8,128)(2,1)} %get-tuple-element.158.refs_2_.refs_6_.refs_1_, ...), custom_call_target="tpu_custom_call" | custom-call | flops 85899345920 | bytes 209715200 | tf_op jit(solution)/shard_map/out_norm/pallas_call | solution.py:831
  142.7 17.7 %ffn_fwd.4 = (bf16[256,2048]{1,0:T(8,128)(2,1)}, bf16[256,2048]{1,0:T(8,128)(2,1)}, bf16[1024,1408]{1,0:T(8,128)(2,1)}, bf16[1024,1408]{1,0:T(8,128)(2,1)}, bf16[1024,1408]{1,0:T(8,128)(2,1)}) custom-call(bf16[1024,2048]{1,0:T(8,128)(2,1)} %get-tuple-element.169.refs_2_.refs_0_.refs_1_, bf16[2048,1408]{1,0:T(8,128)(2,1)} %refs_4_.7, ...), custom_call_target="tpu_custom_call" | custom-call | flops 88583700480 | bytes 216268800 | tf_op jit(solution)/shard_map/ffn_fwd/pallas_call | solution.py:831
  162.4 17.8 %ffn_fwd.5 = (bf16[128,2048]{1,0:T(8,128)(2,1)}, bf16[128,2048]{1,0:T(8,128)(2,1)}, bf16[256,2048]{1,0:T(8,128)(2,1)}, bf16[1024,1408]{1,0:T(8,128)(2,1)}, bf16[...) custom-call(bf16[1024,2048]{1,0:T(8,128)(2,1)} %get-tuple-element.16, ...), custom_call_target="tpu_custom_call", output_to_operand_aliasing={{3}: (4, {}), {4}: (5, {}), {5}: (6, {})} | custom-call | flops 88583700480 | bytes 216268800 | tf_op jit(solution)/shard_map/ffn_fwd/pallas_call | solution.py:831
  182.6 20.4 %out_norm.3 = (bf16[1024,2048]{1,0:T(8,128)(2,1)}, f32[256,2048]{1,0:T(8,128)}, f32[256,128]{1,0:T(8,128)}) custom-call(s32[4]{0:T(128)} %add_add_fusion.refs_0_, s32[8]{0:T(128)} %stack.54.refs_1_.refs_0_, bf16[1024,512]{1,0:T(8,128)(2,1)} %get-tuple-element.167.refs_2_.refs_6_, bf16[1024,512]{1,0:T(8,128)(2,1)} %collective-permute-done.8.refs_0_.refs_3_.refs_7_, ...), custom_call_target="tpu_custom_call" | custom-call | flops 85899345920 | bytes 209715200 | tf_op jit(solution)/shard_map/out_norm/pallas_call | solution.py:831
  208.1 18.1 %ffn_fwd.6 = (bf16[256,2048]{1,0:T(8,128)(2,1)}, bf16[256,2048]{1,0:T(8,128)(2,1)}, bf16[1024,1408]{1,0:T(8,128)(2,1)}, bf16[1024,1408]{1,0:T(8,128)(2,1)}, bf16[1024,1408]{1,0:T(8,128)(2,1)}) custom-call(bf16[1024,2048]{1,0:T(8,128)(2,1)} %get-tuple-element.179.refs_4_.refs_0_.refs_2_, bf16[2048,1408]{1,0:T(8,128)(2,1)} %refs_4_.7, ...), custom_call_target="tpu_custom_call" | custom-call | flops 88583700480 | bytes 216268800 | tf_op jit(solution)/shard_map/ffn_fwd/pallas_call | solution.py:831
  233.7 17.7 %ffn_fwd.7 = (bf16[128,2048]{1,0:T(8,128)(2,1)}, bf16[128,2048]{1,0:T(8,128)(2,1)}, bf16[256,2048]{1,0:T(8,128)(2,1)}, bf16[256,2048]{1,0:T(8,128)(2,1)}, bf16[2...) custom-call(bf16[1024,2048]{1,0:T(8,128)(2,1)} %get-tuple-element.17, ...), custom_call_target="tpu_custom_call", output_to_operand_aliasing={{5}: (4, {}), {6}: (5, {}), {7}: (6, {}), {3}: (7, {}), {4}... | custom-call | flops 88583700480 | bytes 216268800 | tf_op jit(solution)/shard_map/ffn_fwd/pallas_call | solution.py:831
  263.3 26.1 %collective-permute-done.22.refs_7_ = bf16[128,2048]{1,0:T(8,128)(2,1)S(1)} collective-permute-done((bf16[128,2048]{1,0:T(8,128)(2,1)}, bf16[128,2048]{1,0:T(8,128)(2,1)S(1)}, u32[]{:S(2)}, u32[]{:S(2)}) %collective-permute-start.22) | collective-permute-done | bytes 524320 | tf_op jit(solution)/shard_map/ppermute | solution.py:551
  290.5 14.6 %norm_two.2 = (bf16[2,1024,2048]{2,1,0:T(8,128)(2,1)}, f32[2,2048]{1,0:T(2,128)}, bf16[1024,2048]{1,0:T(8,128)(2,1)}) custom-call(s32[4]{0:T(128)} %add_add_fusion.1.refs_0_, s32[8]{0:T(128)} %stack.54.refs_1_.refs_0_, f32[1]{0:T(128)} %get-tuple-element.315.refs_2_, bf16[256,2048]{1,0:T(8,128)(2,1)} %resid_two.2.refs_9_.refs_3_, ...), custom_call_target="tpu_custom_call" | custom-call | flops 419430400 | bytes 167772160 | tf_op jit(solution)/shard_map/norm_two/pallas_call | solution.py:831
  311.6 19.2 %ffn_bwd.3 = (bf16[256,2048]{1,0:T(8,128)(2,1)}, bf16[256,2048]{1,0:T(8,128)(2,1)}, bf16[1024,1408]{1,0:T(8,128)(2,1)}, bf16[1024,1408]{1,0:T(8,128)(2,1)}) custom-call(bf16[1024,2048]{1,0:T(8,128)(2,1)} %get-tuple-element.204.refs_0_.refs_2_.refs_5_, bf16[1024,1408]{1,0:T(8,128)(2,1)} %get-tuple-element.205.refs_1_, ...), custom_call_target="tpu_custom_call" | custom-call | flops 88583700480 | bytes 230686720 | tf_op jit(solution)/shard_map/ffn_bwd/pallas_call | solution.py:831
  338.1 19.1 %ffn_bwd.4 = (bf16[128,2048]{1,0:T(8,128)(2,1)}, bf16[128,2048]{1,0:T(8,128)(2,1)}, bf16[256,2048]{1,0:T(8,128)(2,1)}, bf16[256,2048]{1,0:T(8,128)(2,1)}, bf16[2...) custom-call(bf16[1024,2048]{1,0:T(8,128)(2,1)} %get-tuple-element.20, ...), custom_call_target="tpu_custom_call", output_to_operand_aliasing={{5}: (6, {}), {6}: (7, {}), {3}: (8, {}), {4}: (9, {})} | custom-call | flops 88583700480 | bytes 230686720 | tf_op jit(solution)/shard_map/ffn_bwd/pallas_call | solution.py:831
  376.5 14.5 %norm_two.3 = (bf16[2,1024,2048]{2,1,0:T(8,128)(2,1)}, f32[2,2048]{1,0:T(2,128)}, bf16[1024,2048]{1,0:T(8,128)(2,1)}) custom-call(s32[4]{0:T(128)} %add_add_fusion.refs_0_, s32[8]{0:T(128)} %stack.54.refs_1_.refs_0_, f32[1]{0:T(128)} %get-tuple-element.316.refs_2_, bf16[256,2048]{1,0:T(8,128)(2,1)} %resid_two.3.refs_10_.refs_3_, ...), custom_call_target="tpu_custom_call", output_to_operand_aliasing={{0}: (11, {})} | custom-call | flops 419430400 | bytes 167772160 | tf_op jit(solution)/shard_map/norm_two/pallas_call | solution.py:831
  391.0 19.1 %grad_plain_columns.1.refs_4_ = bf16[1408,2048]{1,0:T(8,128)(2,1)} custom-call(bf16[1024,1408]{1,0:T(8,128)(2,1)} %get-tuple-element.223.refs_0_, bf16[1024,1408]{1,0:T(8,128)(2,1)} %get-tuple-element.224.refs_1_, bf16[1024,2048]{1,0:T(8,128)(2,1)} %get-tuple-element.204.refs_0_.refs_2_.refs_5_, ...), custom_call_target="tpu_custom_call" | custom-call | flops 118111600640 | bytes 199229440 | tf_op jit(solution)/shard_map/grad_plain_columns/pallas_call | solution.py:831
  418.0 32.6 %ffn_bwd.5 = (bf16[256,2048]{1,0:T(8,128)(2,1)}, bf16[256,2048]{1,0:T(8,128)(2,1)}, bf16[128,2048]{1,0:T(8,128)(2,1)}, bf16[128,2048]{1,0:T(8,128)(2,1)}, bf16[2...) custom-call(bf16[1024,2048]{1,0:T(8,128)(2,1)} %get-tuple-element.217.refs_3_.refs_0_.refs_5_, ...), custom_call_target="tpu_custom_call" | custom-call | flops 177167400960 | bytes 230686720 | tf_op jit(solution)/shard_map/ffn_bwd/pallas_call | solution.py:831
  461.0 20.6 %grad_rows.3 = (bf16[11,1024,128]{2,1,0:T(8,128)(2,1)}, bf16[11,1024,128]{2,1,0:T(8,128)(2,1)}) custom-call(s32[4]{0:T(128)} %add_add_fusion.refs_0_, bf16[1024,2048]{1,0:T(8,128)(2,1)} %get-tuple-element.169.refs_2_.refs_0_.refs_1_, bf16[1024,2048]{1,0:T(8,128)(2,1)} %get-tuple-element.179.refs_4_.refs_0_.refs_2_, ...), custom_call_target="tpu_custom_call" | custom-call | flops 118111600640 | bytes 141557760 | tf_op jit(solution)/shard_map/grad_rows/pallas_call | solution.py:831
  494.0 20.5 %grad_rows.4 = (bf16[11,1024,128]{2,1,0:T(8,128)(2,1)}, bf16[11,1024,128]{2,1,0:T(8,128)(2,1)}) custom-call(s32[4]{0:T(128)} %add_add_fusion.refs_0_, bf16[1024,2048]{1,0:T(8,128)(2,1)} %get-tuple-element.169.refs_2_.refs_0_.refs_1_, bf16[1024,2048]{1,0:T(8,128)(2,1)} %get-tuple-element.179.refs_4_.refs_0_.refs_2_, ...), custom_call_target="tpu_custom_call" | custom-call | flops 118111600640 | bytes 141557760 | tf_op jit(solution)/shard_map/grad_rows/pallas_call | solution.py:831
  529.9 26.7 %attn_bwd.2.refs_6_.refs_1_.refs_2_.refs_3_ = bf16[1024,1536]{1,0:T(8,128)(2,1)} custom-call(s32[4]{0:T(128)} %add_add_fusion.1.refs_0_, bf16[1024,1536]{1,0:T(8,128)(2,1)} %get-tuple-element.159.refs_2_.refs_1_, bf16[256,2048]{1,0:T(8,128)(2,1)} %get-tuple-element.236.refs_5_.refs_2_.refs_3_, ...), custom_call_target="tpu_custom_call" | custom-call | flops 128849018880 | bytes 83886080 | tf_op jit(solution)/shard_map/attn_bwd/pallas_call | solution.py:831
  556.6 19.3 %collective-permute-done.42.refs_5_ = bf16[5632,128]{1,0:T(8,128)(2,1)} collective-permute-done((bf16[5632,128]{1,0:T(8,128)(2,1)S(1)}, bf16[5632,128]{1,0:T(8,128)(2,1)}, u32[]{:S(2)}, u32[]{:S(2)}) %collective-permute-start.42) | collective-permute-done | bytes 1441824 | tf_op jit(solution)/shard_map/ppermute | solution.py:1880
  633.1 26.4 %attn_bwd.3.refs_4_.refs_1_.refs_2_ = bf16[1024,1536]{1,0:T(8,128)(2,1)} custom-call(s32[4]{0:T(128)} %add_add_fusion.refs_0_, bf16[1024,1536]{1,0:T(8,128)(2,1)} %get-tuple-element.163.refs_4_.refs_1_, bf16[256,2048]{1,0:T(8,128)(2,1)} %get-tuple-element.246.refs_13_.refs_2_.refs_8_, bf16[256,2048]{1,0:T(8,128)(2,1)} %collective-permute-done.40.refs_0_.refs_3_.refs_9_, ...), custom_call_target="tpu_custom_call" | custom-call | flops 128849018880 | bytes 83886080 | tf_op jit(solution)/shard_map/attn_bwd/pallas_call | solution.py:831
  677.6 20.7 %grad_rows.5 = (bf16[12,1024,128]{2,1,0:T(8,128)(2,1)}, bf16[12,1024,128]{2,1,0:T(8,128)(2,1)}) custom-call(s32[4]{0:T(128)} %add_add_fusion.refs_0_, bf16[2,1024,2048]{2,1,0:T(8,128)(2,1)} %refs_2_.13, bf16[2,1024,2048]{2,1,0:T(8,128)(2,1)} %refs_2_.13, bf16[1024,1536]{1,0:T(8,128)(2,1)} %attn_bwd.2.refs_6_.refs_1_.refs_2_.refs_3_, ...), custom_call_target="tpu_custom_call" | custom-call | flops 128849018880 | bytes 146800640 | tf_op jit(solution)/shard_map/grad_rows/pallas_call | solution.py:831
  777.8 29.6 %collective-permute-done.70.refs_1_ = f32[4,2048]{1,0:T(4,128)S(1)} collective-permute-done((f32[4,2048]{1,0:T(4,128)S(1)}, f32[4,2048]{1,0:T(4,128)S(1)}, u32[]{:S(2)}, u32[]{:S(2)}) %collective-permute-start.70) | collective-permute-done | bytes 32800 | tf_op jit(solution)/shard_map/ppermute | solution.py:2116
  852.5 17.3 %collective-permute-done.74.refs_1_.refs_3_ = bf16[256,2048]{1,0:T(8,128)(2,1)S(1)} collective-permute-done((bf16[256,2048]{1,0:T(8,128)(2,1)S(1)}, bf16[256,2048]{1,0:T(8,128)(2,1)S(1)}, u32[]{:S(2)}, u32[]{:S(2)}) %collective-permute-start.74) | collective-permute-done | bytes 1048608 | tf_op jit(solution)/shard_map/ppermute | solution.py:551
  940.4 21.1 %collective-permute-done.88.refs_3_ = bf16[4096,128]{1,0:T(8,128)(2,1)} collective-permute-done((bf16[4096,128]{1,0:T(8,128)(2,1)}, bf16[4096,128]{1,0:T(8,128)(2,1)}, u32[]{:S(2)}, u32[]{:S(2)}) %collective-permute-start.88) | collective-permute-done | bytes 1048608 | tf_op jit(solution)/shard_map/ppermute | solution.py:1880
  (350 shorter events, 486.0 us)
Async XLA Ops:
  9.5 43.9 %collective-permute-start.3 = (bf16[256,2048]{1,0:T(8,128)(2,1)}, bf16[256,2048]{1,0:T(8,128)(2,1)S(1)}, u32[]{:S(2)}, u32[]{:S(2)}) collective-permute-start(bf16[256,2048]{1,0:T(8,128)(2,1)} %constant_dynamic-slice_fusion), channel_id=1, source_target_pairs={{0,2},{1,3},{2,0},{3,1},{4,6},{5,7},{6,4},{7,5},{8,10},{9,11},{10,... | collective-permute-start | bytes 3145736 | tf_op jit(solution)/shard_map/ppermute | solution.py:551
  12.5 40.9 %collective-permute-start.2 = (bf16[256,2048]{1,0:T(8,128)(2,1)}, bf16[256,2048]{1,0:T(8,128)(2,1)}, u32[]{:S(2)}, u32[]{:S(2)}) collective-permute-start(bf16[256,2048]{1,0:T(8,128)(2,1)} %constant_dynamic-slice_fusion), channel_id=1, source_target_pairs={{0,1},{1,0},{2,3},{3,2},{4,5},{5,4},{6,7},{7,6},{8,9},{9,8},{10,11... | collective-permute-start | bytes 3145736 | tf_op jit(solution)/shard_map/ppermute | solution.py:551
  160.5 42.5 %collective-permute-start.14 = (bf16[256,2048]{1,0:T(8,128)(2,1)}, bf16[256,2048]{1,0:T(8,128)(2,1)}, u32[]{:S(2)}, u32[]{:S(2)}) collective-permute-start(bf16[256,2048]{1,0:T(8,128)(2,1)} %get-tuple-element.180), channel_id=1, source_target_pairs={{0,2},{1,3},{2,0},{3,1},{4,6},{5,7},{6,4},{7,5},{8,10},{9,11},{10,... | collective-permute-start | bytes 3145736 | tf_op jit(solution)/shard_map/ppermute | solution.py:551
  161.7 41.3 %collective-permute-start.13 = (bf16[256,2048]{1,0:T(8,128)(2,1)}, bf16[256,2048]{1,0:T(8,128)(2,1)}, u32[]{:S(2)}, u32[]{:S(2)}) collective-permute-start(bf16[256,2048]{1,0:T(8,128)(2,1)} %get-tuple-element.176.refs_7_), channel_id=1, source_target_pairs={{0,1},{1,0},{2,3},{3,2},{4,5},{5,4},{6,7},{7,6},{8,9},{9,8},{10,11... | collective-permute-start | bytes 3145736 | tf_op jit(solution)/shard_map/ppermute | solution.py:551
  257.2 48.0 %collective-permute-start.19 = (bf16[256,2048]{1,0:T(8,128)(2,1)}, bf16[256,2048]{1,0:T(8,128)(2,1)S(1)}, u32[]{:S(2)}, u32[]{:S(2)}) collective-permute-start(bf16[256,2048]{1,0:T(8,128)(2,1)} %get-tuple-element.195), channel_id=1, source_target_pairs={{0,1},{1,0},{2,3},{3,2},{4,5},{5,4},{6,7},{7,6},{8,9},{9,8},{10,11... | collective-permute-start | bytes 3145736 | tf_op jit(solution)/shard_map/ppermute | solution.py:551
  258.2 47.0 %collective-permute-start.20 = (bf16[256,2048]{1,0:T(8,128)(2,1)}, bf16[256,2048]{1,0:T(8,128)(2,1)}, u32[]{:S(2)}, u32[]{:S(2)}) collective-permute-start(bf16[256,2048]{1,0:T(8,128)(2,1)} %get-tuple-element.196), channel_id=1, source_target_pairs={{0,2},{1,3},{2,0},{3,1},{4,6},{5,7},{6,4},{7,5},{8,10},{9,11},{10,... | collective-permute-start | bytes 3145736 | tf_op jit(solution)/shard_map/ppermute | solution.py:551
  362.9 47.9 %collective-permute-start.29 = (bf16[256,2048]{1,0:T(8,128)(2,1)}, bf16[256,2048]{1,0:T(8,128)(2,1)S(1)}, u32[]{:S(2)}, u32[]{:S(2)}) collective-permute-start(bf16[256,2048]{1,0:T(8,128)(2,1)} %get-tuple-element.220), channel_id=1, source_target_pairs={{0,1},{1,0},{2,3},{3,2},{4,5},{5,4},{6,7},{7,6},{8,9},{9,8},{10,11... | collective-permute-start | bytes 3145736 | tf_op jit(solution)/shard_map/ppermute | solution.py:551
  363.9 46.8 %collective-permute-start.30 = (bf16[256,2048]{1,0:T(8,128)(2,1)}, bf16[256,2048]{1,0:T(8,128)(2,1)}, u32[]{:S(2)}, u32[]{:S(2)}) collective-permute-start(bf16[256,2048]{1,0:T(8,128)(2,1)} %get-tuple-element.221), channel_id=1, source_target_pairs={{0,2},{1,3},{2,0},{3,1},{4,6},{5,7},{6,4},{7,5},{8,10},{9,11},{10,... | collective-permute-start | bytes 3145736 | tf_op jit(solution)/shard_map/ppermute | solution.py:551
  414.7 262.9 %all-reduce.2.cloned.1.call-start = ((), (), s32[]{:S(2)}) async-start(), calls=%async_computation | async-start | bytes 11534336 | tf_op jit(solution)/shard_map/psum | solution.py:2066
  514.6 72.0 %collective-permute-start.48 = (bf16[11264,128]{1,0:T(8,128)(2,1)}, bf16[11264,128]{1,0:T(8,128)(2,1)}, u32[]{:S(2)}, u32[]{:S(2)}) collective-permute-start(bf16[11264,128]{1,0:T(8,128)(2,1)} %bitcast.60), channel_id=1, source_target_pairs={{0,4},{4,0},{1,5},{5,1},{2,6},{6,2},{3,7},{7,3},{8,12},{12,8},{9,1... | collective-permute-start | bytes 8650760 | tf_op jit(solution)/shard_map/ppermute | solution.py:2079
  525.7 55.5 %collective-permute-start.41 = (bf16[256,2048]{1,0:T(8,128)(2,1)}, bf16[256,2048]{1,0:T(8,128)(2,1)}, u32[]{:S(2)}, u32[]{:S(2)}) collective-permute-start(bf16[256,2048]{1,0:T(8,128)(2,1)} %get-tuple-element.246.refs_13_.refs_2_.refs_8_), channel_id=1, source_target_pairs={{0,2},{1,3},{2,0},{3,1},{4,6},{5,7},{6,4},{7,5},{8,10},{9,11},{10,... | collective-permute-start | bytes 3145736 | tf_op jit(solution)/shard_map/ppermute | solution.py:551
  527.4 53.8 %collective-permute-start.40 = (bf16[256,2048]{1,0:T(8,128)(2,1)}, bf16[256,2048]{1,0:T(8,128)(2,1)}, u32[]{:S(2)}, u32[]{:S(2)}) collective-permute-start(bf16[256,2048]{1,0:T(8,128)(2,1)} %get-tuple-element.246.refs_13_.refs_2_.refs_8_), channel_id=1, source_target_pairs={{0,1},{1,0},{2,3},{3,2},{4,5},{5,4},{6,7},{7,6},{8,9},{9,8},{10,11... | collective-permute-start | bytes 3145736 | tf_op jit(solution)/shard_map/ppermute | solution.py:551
  529.8 46.1 %collective-permute-start.42 = (bf16[5632,128]{1,0:T(8,128)(2,1)S(1)}, bf16[5632,128]{1,0:T(8,128)(2,1)}, u32[]{:S(2)}, u32[]{:S(2)}) collective-permute-start(bf16[5632,128]{1,0:T(8,128)(2,1)S(1)} %copy-done.2), channel_id=1, source_target_pairs={{0,8},{24,16},{8,0},{16,24},{1,9},{25,17},{9,1},{17,25},{2,10},{26... | collective-permute-start | bytes 4325384 | tf_op jit(solution)/shard_map/ppermute | solution.py:1880
  529.9 92.2 %collective-permute-start.47 = (f32[4,2048]{1,0:T(4,128)}, f32[4,2048]{1,0:T(4,128)}, u32[]{:S(2)}, u32[]{:S(2)}) collective-permute-start(f32[4,2048]{1,0:T(4,128)} %pad_maximum_fusion.refs_0_), channel_id=1, source_target_pairs={{0,4},{4,0},{1,5},{5,1},{2,6},{6,2},{3,7},{7,3},{8,12},{12,8},{9,1... | collective-permute-start | bytes 98312 | tf_op jit(solution)/shard_map/ppermute | solution.py:2116
  583.4 46.4 %collective-permute-start.46 = (bf16[128,2048]{1,0:T(8,128)(2,1)}, bf16[128,2048]{1,0:T(8,128)(2,1)S(1)}, u32[]{:S(2)}, u32[]{:S(2)}) collective-permute-start(bf16[128,2048]{1,0:T(8,128)(2,1)} %get-tuple-element.251), channel_id=1, source_target_pairs={{0,1},{1,0},{2,3},{3,2},{4,5},{5,4},{6,7},{7,6},{8,9},{9,8},{10,11... | collective-permute-start | bytes 1572872 | tf_op jit(solution)/shard_map/ppermute | solution.py:551
  585.1 46.2 %collective-permute-start.45 = (bf16[128,2048]{1,0:T(8,128)(2,1)}, bf16[128,2048]{1,0:T(8,128)(2,1)}, u32[]{:S(2)}, u32[]{:S(2)}) collective-permute-start(bf16[128,2048]{1,0:T(8,128)(2,1)} %get-tuple-element.250.refs_4_), channel_id=1, source_target_pairs={{0,2},{1,3},{2,0},{3,1},{4,6},{5,7},{6,4},{7,5},{8,10},{9,11},{10,... | collective-permute-start | bytes 1572872 | tf_op jit(solution)/shard_map/ppermute | solution.py:551
  614.2 45.3 %collective-permute-start.52 = (bf16[256,2048]{1,0:T(8,128)(2,1)}, bf16[256,2048]{1,0:T(8,128)(2,1)}, u32[]{:S(2)}, u32[]{:S(2)}) collective-permute-start(bf16[256,2048]{1,0:T(8,128)(2,1)} %get-tuple-element.262), channel_id=1, source_target_pairs={{0,2},{1,3},{2,0},{3,1},{4,6},{5,7},{6,4},{7,5},{8,10},{9,11},{10,... | collective-permute-start | bytes 3145736 | tf_op jit(solution)/shard_map/ppermute | solution.py:551
  615.6 43.8 %collective-permute-start.51 = (bf16[256,2048]{1,0:T(8,128)(2,1)}, bf16[256,2048]{1,0:T(8,128)(2,1)}, u32[]{:S(2)}, u32[]{:S(2)}) collective-permute-start(bf16[256,2048]{1,0:T(8,128)(2,1)} %get-tuple-element.259.refs_8_), channel_id=1, source_target_pairs={{0,1},{1,0},{2,3},{3,2},{4,5},{5,4},{6,7},{7,6},{8,9},{9,8},{10,11... | collective-permute-start | bytes 3145736 | tf_op jit(solution)/shard_map/ppermute | solution.py:551
  622.0 41.5 %collective-permute-start.56 = (bf16[5632,128]{1,0:T(8,128)(2,1)}, bf16[5632,128]{1,0:T(8,128)(2,1)S(1)}, u32[]{:S(2)}, u32[]{:S(2)}) collective-permute-start(bf16[5632,128]{1,0:T(8,128)(2,1)} %get-tuple-element.260.refs_2_.refs_9_), channel_id=1, source_target_pairs={{0,8},{24,16},{8,0},{16,24},{1,9},{25,17},{9,1},{17,25},{2,10},{26... | collective-permute-start | bytes 4325384 | tf_op jit(solution)/shard_map/ppermute | solution.py:1880
  629.8 43.5 %collective-permute-start.55 = (f32[4,2048]{1,0:T(4,128)}, f32[4,2048]{1,0:T(4,128)S(1)}, u32[]{:S(2)}, u32[]{:S(2)}) collective-permute-start(f32[4,2048]{1,0:T(4,128)} %add_small.5.refs_13_.refs_0_), channel_id=1, source_target_pairs={{0,1},{1,0},{2,3},{3,2},{4,5},{5,4},{6,7},{7,6},{8,9},{9,8},{10,11... | collective-permute-start | bytes 98312 | tf_op jit(solution)/shard_map/ppermute | solution.py:2116
  670.4 48.9 %collective-permute-start.64 = (bf16[5632,128]{1,0:T(8,128)(2,1)}, bf16[5632,128]{1,0:T(8,128)(2,1)}, u32[]{:S(2)}, u32[]{:S(2)}) collective-permute-start(bf16[5632,128]{1,0:T(8,128)(2,1)} %get-tuple-element.269.refs_2_.refs_9_), channel_id=1, source_target_pairs={{0,8},{24,16},{8,0},{16,24},{1,9},{25,17},{9,1},{17,25},{2,10},{26... | collective-permute-start | bytes 4325384 | tf_op jit(solution)/shard_map/ppermute | solution.py:1880
  675.3 51.7 %collective-permute-start.62 = (f32[4,2048]{1,0:T(4,128)}, f32[4,2048]{1,0:T(4,128)}, u32[]{:S(2)}, u32[]{:S(2)}) collective-permute-start(f32[4,2048]{1,0:T(4,128)} %add_small.6.refs_5_.refs_0_), channel_id=1, source_target_pairs={{0,2},{1,3},{2,0},{3,1},{4,6},{5,7},{6,4},{7,5},{8,10},{9,11},{10,... | collective-permute-start | bytes 98312 | tf_op jit(solution)/shard_map/ppermute | solution.py:2116
  734.6 93.6 %collective-permute-start.78 = (bf16[11264,128]{1,0:T(8,128)(2,1)}, bf16[11264,128]{1,0:T(8,128)(2,1)}, u32[]{:S(2)}, u32[]{:S(2)}) collective-permute-start(bf16[11264,128]{1,0:T(8,128)(2,1)} %get-tuple-element.290), channel_id=1, source_target_pairs={{0,4},{4,0},{1,5},{5,1},{2,6},{6,2},{3,7},{7,3},{8,12},{12,8},{9,1... | collective-permute-start | bytes 8650760 | tf_op jit(solution)/shard_map/ppermute | solution.py:2107
  769.8 68.1 %collective-permute-start.76 = (bf16[5632,128]{1,0:T(8,128)(2,1)}, bf16[5632,128]{1,0:T(8,128)(2,1)S(1)}, u32[]{:S(2)}, u32[]{:S(2)}) collective-permute-start(bf16[5632,128]{1,0:T(8,128)(2,1)} %get-tuple-element.287.refs_2_.refs_9_), channel_id=1, source_target_pairs={{0,8},{24,16},{8,0},{16,24},{1,9},{25,17},{9,1},{17,25},{2,10},{26... | collective-permute-start | bytes 4325384 | tf_op jit(solution)/shard_map/ppermute | solution.py:1880
  (118 other events, 2073.2 us)
Sparse Core Ops, SparseCore 0:
  418.4 139.5 all-reduce.1

commit v3 on v2

--- a/solution.py
+++ b/solution.py
@@ -793,10 +793,16 @@
 
 ORDER = ((1, 0), (3, 0), (2, 1), (3, 1), (1, 1), (2, 0), (0, 0), (0, 1))
 CORES = ((0, 1), (1, 0))
-COST_SHARE = 0.1
-
-
-def plane_case(token_shape, down_shape):
+DECLARED_FLOPS = 1e10
+MICROS = {
+    "attn_fwd": 21, "split": 2, "ow_join": 4, "relay": 1, "out_norm": 21, "middle_sum": 3, "resid_two": 5,
+    "norm_two": 15, "grad_columns": 20, "grad_plain_columns": 19, "grad_plain": 19, "line_step": 5, "grad_rows": 21,
+    "attn_bwd": 24, "norm_one_back": 6, "input_back": 14, "input_grad": 5, "grad_out": 11, "place": 5, "widen": 10,
+    "cast": 9, "total_sum": 2,
+}
+
+
+def plane_case(token_shape, out_shape, down_shape):
     return (
         lax.axis_size("tensor") == 4
         and lax.axis_size("dp") == 2
@@ -805,6 +811,7 @@
         and token_shape[1] % 1024 == 0
         and token_shape[2] % 1024 == 0
         and down_shape[0] % 128 == 0
+        and out_shape[0] % 256 == 0
     )
 
 
@@ -834,7 +841,7 @@
         out_shape=[jax.ShapeDtypeStruct(s, d) for s, d in outs],
         input_output_aliases={ns + k: v for k, v in (aliases or {}).items()},
         compiler_params=params(62, len(grid)),
-        cost_estimate=cost(flops / COST_SHARE, nbytes / COST_SHARE),
+        cost_estimate=cost(DECLARED_FLOPS * MICROS.get(name, 9 * grid[0]), 1e6),
         name=name,
     )(*scalars, *ins, *after)
 
@@ -851,28 +858,79 @@
 class Chain:
     def __init__(self):
         self.last = ()
+        self.ended = ()
+
+    def close(self, *arrays):
+        self.ended += arrays
 
     def __call__(self, *args, after=(), **kwargs):
-        out = call(*args, after=tuple(self.last) + tuple(after), **kwargs)
-        self.last = (out[0],)
+        out = call(*args, after=(*self.last, *self.ended, *after), **kwargs)
+        self.last, self.ended = (out[0],), ()
         return out
 
 
 def pair_swap(to_x, to_y):
     return swap(to_x, 1, 4), swap(to_y, 2, 4)
+
+
+def plane_attn_fwd_kernel(
+    info_ref, x_ref, w_ref, cos_ref, sin_ref, segc_ref, segr_ref, qkv_ref, ol_ref, lse_ref, bias_ref, *, tile
+):
+    length = x_ref.shape[0]
+
+    @pl.when(pl.program_id(0) == 0)
+    def _():
+        fill_bias(info_ref, segc_ref, segr_ref, bias_ref, tile)
+
+    for step in range(length // (2 * tile)):
+        rows = pl.ds(step * 2 * tile, 2 * tile)
+        proj = mm(x_ref[rows, :], w_ref[...])
+        cosine, sine = cos_ref[rows, :], sin_ref[rows, :]
+        for part in range(proj.shape[1] // HEAD_DIM):
+            low = part * HEAD_DIM
+            piece = proj[:, low : low + HEAD_DIM]
+            if part % 3 < 2:
+                piece = piece * cosine + pltpu.roll(piece, HEAD_DIM // 2, 1) * sine
+            qkv_ref[rows, low : low + HEAD_DIM] = piece.astype(BF)
+
+    heads = qkv_ref.shape[1] // (3 * HEAD_DIM)
+    units = [(h, t) for h in range(heads) for t in range(length // tile)]
+    keys, values_t = {}, {}
+
+    def scores_of(unit):
+        h, t = unit
+        base = 3 * HEAD_DIM * h
+        if h not in keys:
+            keys[h] = qkv_ref[:, base + HEAD_DIM : base + 2 * HEAD_DIM]
+            values_t[h] = qkv_ref[:, base + 2 * HEAD_DIM : base + 3 * HEAD_DIM].astype(F32).T.astype(BF)
+        return mm_nt(keys[h], qkv_ref[t * tile : (t + 1) * tile, base : base + HEAD_DIM])
+
+    later = scores_of(units[0])
+    for k, (h, t) in enumerate(units):
+        raw = later
+        if k + 1 < len(units):
+            later = scores_of(units[k + 1])
+        rows = pl.ds(t * tile, tile)
+        scores = raw * score_scale + bias_ref[:, rows]
+        top = jnp.max(scores, axis=0, keepdims=True)
+        exponent = jnp.exp(scores - top)
+        total = jnp.sum(exponent, axis=0, keepdims=True)
+        attended = mm(values_t[h], exponent.astype(BF)) * (1.0 / total)
+        ol_ref[rows, h * HEAD_DIM : (h + 1) * HEAD_DIM] = attended.T.astype(BF)
+        lse_ref[h, :, rows] = top + jnp.log(total)
 
 
 def plane_attn_fwd(chain, info, row, tokens, qkv_weight, cosine, sine, segc, segr, after=()):
     _, length, width = tokens.shape
     heads = qkv_weight.shape[1] // (3 * HEAD_DIM)
     return chain(
-        functools.partial(attn_fwd_kernel, tile=256),
+        functools.partial(plane_attn_fwd_kernel, tile=256),
         "attn_fwd",
-        (heads,),
+        (heads // 2,),
         (tokens, qkv_weight, cosine, sine, segc, segr),
         [
             pl.BlockSpec((None, length, width), lambda h, *_: (row, 0, 0), pipeline_mode=pl.Buffered(1)),
-            spec((width, 3 * HEAD_DIM), lambda h, *_: (0, h)),
+            spec((width, 768), lambda h, *_: (0, h)),
             const_spec((length, HEAD_DIM)),
             const_spec((length, HEAD_DIM)),
             const_spec((length, 1)),
@@ -880,9 +938,9 @@
         ],
         [((length, heads * 384), BF), ((length, heads * 128), BF), ((heads, 1, length), F32)],
         [
-            spec((length, 384), lambda h, *_: (0, h)),
-            spec((length, 128), lambda h, *_: (0, h)),
-            spec((None, 1, length), lambda h, *_: (h, 0, 0)),
+            spec((length, 768), lambda h, *_: (0, h)),
+            spec((length, 256), lambda h, *_: (0, h)),
+            spec((2, 1, length), lambda h, *_: (h, 0, 0)),
         ],
         scalars=(info,),
         after=after,
@@ -894,7 +952,7 @@
 
 def plane_attn_bwd_kernel(
     info_ref, qkv_ref, own, r1, r2, r3a, r3b, ow_ref, lse_ref, cos_ref, sin_ref, segc_ref, segr_ref, dqkv_ref,
-    bias_ref, dol_nat, dk_ref, dv_ref,
+    bias_ref, dol_nat, *, tile
 ):
     length = qkv_ref.shape[0]
     block = own.shape[0]
@@ -903,7 +961,7 @@
 
     @pl.when(pl.program_id(0) == 0)
     def _():
-        fill_bias(info_ref, segc_ref, segr_ref, bias_ref, block)
+        fill_bias(info_ref, segc_ref, segr_ref, bias_ref, tile)
 
     def natural(r, lower):
         return pl.multiple_of((me ^ r) * block + lower, half)
@@ -912,38 +970,46 @@
         dol_nat[pl.ds(natural(r, 0), block), :] = mm_nt(piece[...], ow_ref[...]).astype(BF)
     for lower, piece in ((0, r3a), (half, r3b)):
         dol_nat[pl.ds(natural(3, lower), half), :] = mm_nt(piece[...], ow_ref[...]).astype(BF)
-    attn_bwd_head(qkv_ref, dol_nat, lse_ref, cos_ref, sin_ref, dqkv_ref, bias_ref, dk_ref, dv_ref, block)
-
-
-def attn_bwd_head(qkv_ref, dol_nat, lse_ref, cos_ref, sin_ref, dqkv_ref, bias_ref, dk_ref, dv_ref, tile):
-    length = qkv_ref.shape[0]
-    keys = qkv_ref[:, HEAD_DIM : 2 * HEAD_DIM]
-    values = qkv_ref[:, 2 * HEAD_DIM :]
-    keys_t = keys.astype(F32).T.astype(BF)
-    for step in range(length // tile):
-        rows = pl.ds(step * tile, tile)
-        queries = qkv_ref[rows, :HEAD_DIM]
-        dol = dol_nat[rows, :]
-        scores = mm_nt(keys, queries) * score_scale + bias_ref[:, rows]
-        probs = jnp.exp(scores - lse_ref[:, rows])
-        dp = mm_nt(values, dol)
-        inner = jnp.sum(probs * dp, axis=0, keepdims=True)
-        draw = (probs * (dp - inner) * score_scale).astype(BF)
-        dv = mm(probs.astype(BF), dol)
-        dk = mm(draw, queries)
-        if step == 0:
-            dv_ref[...] = dv
-            dk_ref[...] = dk
-        else:
-            dv_ref[...] += dv
-            dk_ref[...] += dk
-        dq = mm(keys_t, draw).T
+
+    heads = qkv_ref.shape[1] // (3 * HEAD_DIM)
+    count = length // tile
+    units = [(h, t) for h in range(heads) for t in range(count)]
+    keys, values, keys_t = {}, {}, {}
+
+    def products_of(unit):
+        h, t = unit
+        base = 3 * HEAD_DIM * h
+        if h not in keys:
+            keys[h] = qkv_ref[:, base + HEAD_DIM : base + 2 * HEAD_DIM]
+            values[h] = qkv_ref[:, base + 2 * HEAD_DIM : base + 3 * HEAD_DIM]
+            keys_t[h] = keys[h].astype(F32).T.astype(BF)
+        rows = pl.ds(t * tile, tile)
+        queries = qkv_ref[rows, base : base + HEAD_DIM]
+        dol = dol_nat[rows, h * HEAD_DIM : (h + 1) * HEAD_DIM]
+        return queries, dol, mm_nt(keys[h], queries), mm_nt(values[h], dol)
+
+    dk = dv = None
+    later = products_of(units[0])
+    for k, (h, t) in enumerate(units):
+        queries, dol, raw, dp = later
+        if k + 1 < len(units):
+            later = products_of(units[k + 1])
+        base = 3 * HEAD_DIM * h
+        rows = pl.ds(t * tile, tile)
+        probs = jnp.exp(raw * score_scale + bias_ref[:, rows] - lse_ref[h, :, rows])
+        weighted = probs * dp
+        inner = jnp.sum(weighted, axis=0, keepdims=True)
+        draw = ((weighted - probs * inner) * score_scale).astype(BF)
+        dv_part, dk_part = mm(probs.astype(BF), dol), mm(draw, queries)
+        dv = dv_part if t == 0 else dv + dv_part
+        dk = dk_part if t == 0 else dk + dk_part
+        dq = mm(keys_t[h], draw).T
         turned = dq * cos_ref[rows, :] - pltpu.roll(dq, HEAD_DIM // 2, 1) * sin_ref[rows, :]
-        dqkv_ref[rows, :HEAD_DIM] = turned.astype(BF)
-    dk = dk_ref[...]
-    turned = dk * cos_ref[...] - pltpu.roll(dk, HEAD_DIM // 2, 1) * sin_ref[...]
-    dqkv_ref[:, HEAD_DIM : 2 * HEAD_DIM] = turned.astype(BF)
-    dqkv_ref[:, 2 * HEAD_DIM :] = dv_ref[...].astype(BF)
+        dqkv_ref[rows, base : base + HEAD_DIM] = turned.astype(BF)
+        if t == count - 1:
+            turned = dk * cos_ref[...] - pltpu.roll(dk, HEAD_DIM // 2, 1) * sin_ref[...]
+            dqkv_ref[:, base + HEAD_DIM : base + 2 * HEAD_DIM] = turned.astype(BF)
+            dqkv_ref[:, base + 2 * HEAD_DIM : base + 3 * HEAD_DIM] = dv.astype(BF)
 
 
 def plane_attn_bwd(chain, info, qkv, pieces, out_weight, lse, cosine, sine, segc, segr, after=()):
@@ -951,30 +1017,25 @@
     heads = qkv.shape[1] // 384
     width = out_weight.shape[1]
     return chain(
-        plane_attn_bwd_kernel,
+        functools.partial(plane_attn_bwd_kernel, tile=256),
         "attn_bwd",
-        (heads,),
+        (heads // 2,),
         (qkv, *pieces, out_weight, lse, cosine, sine, segc, segr),
-        [spec((length, 384), lambda h, *_: (0, h))]
+        [spec((length, 768), lambda h, *_: (0, h))]
         + [const_spec(p.shape) for p in pieces]
         + [
-            spec((128, width), lambda h, *_: (h, 0)),
-            spec((None, 1, length), lambda h, *_: (h, 0, 0)),
+            spec((256, width), lambda h, *_: (h, 0)),
+            spec((2, 1, length), lambda h, *_: (h, 0, 0)),
             const_spec((length, HEAD_DIM)),
             const_spec((length, HEAD_DIM)),
             const_spec((length, 1)),
             const_spec((1, length)),
         ],
         [(qkv.shape, BF)],
-        [spec((length, 384), lambda h, *_: (0, h))],
+        [spec((length, 768), lambda h, *_: (0, h))],
         scalars=(info,),
         after=after,
-        scratch=[
-            pltpu.VMEM((length, length), F32),
-            pltpu.VMEM((length, HEAD_DIM), BF),
-            pltpu.VMEM((length, HEAD_DIM), F32),
-            pltpu.VMEM((length, HEAD_DIM), F32),
-        ],
+        scratch=[pltpu.VMEM((length, length), F32), pltpu.VMEM((length, 256), BF)],
         flops=heads * 24 * length * length * 128,
         nbytes=16 * length * heads * 128,
     )[0]
@@ -983,14 +1044,21 @@
 def plane_out_norm_kernel(
     info_ref, order_ref, *refs
 ):
-    lows, highs = refs[:4], refs[4:8]
-    ow_ref, mine_ref, other_ref = refs[8:11]
-    xl_ref, xh_ref, gain_ref, bias_ref, hl_ref, n1_ref, rstd_ref, total_ref = refs[11:]
+    lows, highs = refs[:5], refs[5:10]
+    ow_ref, mine_ref, other_ref = refs[10:13]
+    xl_ref, xh_ref, gain_ref, bias_ref, hl_ref, n1_ref, rstd_ref, total_ref = refs[13:]
     half = xl_ref.shape[0]
+    at = pl.program_id(0)
+
+    def blocks(group, place):
+        diagonal = jnp.where(place < 4, group[3][...].astype(F32), group[4][...].astype(F32)).astype(BF)
+        return [ref[...] for ref in group[:3]] + [diagonal]
+
     feat = mine_ref.shape[0] // 3
     total_ref[:half] = xl_ref[...].astype(F32) * deep_alpha
     total_ref[half:] = xh_ref[...].astype(F32) * deep_alpha
-    ols = [jnp.concatenate([lo[...], hi[...]], axis=0) for lo, hi in zip(lows, highs)]
+    low, high = blocks(lows, order_ref[2 * at]), blocks(highs, order_ref[2 * at + 1])
+    ols = [jnp.concatenate([lo, hi], axis=0) for lo, hi in zip(low, high)]
 
     def add(first, second):
         total = mm(ols[0], ow_ref[...])
@@ -1028,6 +1096,12 @@
     head_width = out_weight.shape[0]
     low = lambda i, info, order: (order[2 * i], 0)
     high = lambda i, info, order: (order[2 * i + 1], 0)
+
+    def ol_specs(index):
+        upper = lambda i, info, order: (jnp.minimum(index(i, info, order)[0], 3), 0)
+        lower = lambda i, info, order: (jnp.maximum(index(i, info, order)[0] - 4, 0), 0)
+        return [spec((half, head_width), f) for f in (index, index, index, upper, lower)]
+
     low3 = lambda i, info, order: (row, order[2 * i], 0)
     high3 = lambda i, info, order: (row, order[2 * i + 1], 0)
     return chain(
@@ -1035,8 +1109,8 @@
         "out_norm",
         (4,),
         (*ol_pieces, *ol_pieces, out_weight, mine, other, tokens, tokens, gain, bias),
-        [spec((half, head_width), low)] * 4
-        + [spec((half, head_width), high)] * 4
+        ol_specs(low)
+        + ol_specs(high)
         + [const_spec(out_weight.shape), const_spec(mine.shape), const_spec(other.shape)]
         + [
             spec((None, half, width), low3),
@@ -1102,23 +1176,21 @@
     )[0]
 
 
-def join_kernel(a_ref, b_ref, carried, out_ref, carried_out):
-    half = a_ref.shape[0]
-    out_ref[:half] = a_ref[...]
-    out_ref[half:] = b_ref[...]
-
-
-def join_halves(chain, halves, carry, after=()):
-    rows, width = halves[0].shape
-    shape = (2 * rows, width)
+def relay_kernel(*refs):
+    refs[len(refs) // 2][...] = refs[0][...]
+
+
+def relay(chain, carry, after=()):
+    small = jnp.zeros((8, 128), F32)
+    any_spec = pl.BlockSpec(memory_space=ANY)
+    count = len(carry)
     out = chain(
-        join_kernel, "join_halves", (1,), (*halves, carry),
-        [const_spec(h.shape) for h in halves] + [pl.BlockSpec(memory_space=ANY)],
-        [(shape, BF), (carry.shape, carry.dtype)],
-        [spec(shape, lambda i, *_: (0, 0)), pl.BlockSpec(memory_space=ANY)],
-        after=after, aliases={2: 1}, nbytes=4 * rows * width,
-    )
-    return out
+        relay_kernel, "relay", (1,), (small, *carry), [const_spec(small.shape)] + [any_spec] * count,
+        [(small.shape, F32)] + [(c.shape, c.dtype) for c in carry],
+        [spec(small.shape, lambda i, *_: (0, 0))] + [any_spec] * count,
+        after=after, aliases={1 + k: 1 + k for k in range(count)},
+    )
+    return out[1:]
 
 
 def load_once(pairs, sem):
@@ -1206,15 +1278,16 @@
     length, width = hidden.shape
     units = weights[0].shape[1]
     block = length // 4
-    base = 0 if first else 2
+    base = 2 if first is False else 0
+    steps = 4 if first is None else 2
     tiled = lambda w: spec((block, w), lambda i, *_: (i + base, 0))
     outs, out_specs = half_outs(first, block, width)
     n = len(outs)
     any_spec = pl.BlockSpec(memory_space=ANY)
-    kept = () if first else tuple(kept)
-    held, carried = kept[:3], kept[3:]
+    kept = tuple(kept)
+    carried = kept[3:]
     kernel = functools.partial(plane_ffn_fwd_kernel, first=first)
-    if first:
+    if first is not False:
         body_kernel = kernel
     else:
         nk, nc = len(kept), len(carried)
@@ -1226,14 +1299,14 @@
     out = chain(
         body_kernel,
         "ffn_fwd",
-        (2,),
+        (steps,),
         (hidden, *weights, *kept),
         [tiled(width)] + [any_spec] * (3 + len(kept)),
         outs + [(c.shape, BF) for c in carried] + [((length, units), BF)] * 3,
         out_specs + [any_spec] * len(carried) + [tiled(units)] * 3,
         after=after,
         aliases={}
-        if first
+        if first is not False
         else {
             **{4 + k: n + len(carried) + k for k in range(3)},
             **{7 + k: n + k for k in range(len(carried))},
@@ -1245,7 +1318,7 @@
             pltpu.SemaphoreType.DMA((3,)),
         ],
         mib=60,
-        flops=3 * length * width * units,
+        flops=3 * length * width * units * steps // 2,
         nbytes=6 * units * width + 3 * length * units,
     )
     n += len(carried)
@@ -1925,14 +1998,28 @@
     )[0]
 
 
-def add_small_kernel(a_ref, b_ref, out_ref):
-    out_ref[...] = a_ref[...] + b_ref[...]
-
-
-def add_small(chain, a, b):
+def cast_kernel(in_ref, out_ref):
+    out_ref[...] = in_ref[...].astype(F32)
+
+
+def cast(chain, array, after=()):
+    rows, columns = array.shape
+    tile = 176 if rows % 256 else 256
     return chain(
-        add_small_kernel, "add_small", (1,), (a, b), [const_spec(a.shape)] * 2, [(a.shape, F32)],
-        [spec(a.shape, lambda i, *_: (0, 0))],
+        cast_kernel, "cast", (rows // tile,), (array,), [rows_spec(array.shape, tile)],
+        [(array.shape, F32)], [rows_spec(array.shape, tile)], after=after,
+    )[0]
+
+
+def total_sum_kernel(in_ref, out_ref):
+    out_ref[...] = jnp.sum(in_ref[...], axis=0)
+
+
+def total_sum(chain, array):
+    shape = array.shape[1:]
+    return chain(
+        total_sum_kernel, "total_sum", (1,), (array,), [const_spec(array.shape)], [(shape, F32)],
+        [spec(shape, lambda i, *_: (0, 0))],
     )[0]
 
 
@@ -2004,10 +2091,10 @@
     qkv[B], ol[B], lse[B] = attention(B)
     ow_mine = ow_join(chain, (owx, owy, owra, owrb), after=(olx[A], oly[A]))
     ow_other = lax.ppermute(ow_mine, "dp", CORES)
-    halves, ol[B] = forward(chain, olx[A], oly[A], (ol[B],))
-    olr[A], ol[B] = join_halves(chain, halves, ol[B])
+    olr[A], ol[B] = forward(chain, olx[A], oly[A], (ol[B],))
+    (ol[B],) = relay(chain, (ol[B],), after=olr[A])
     olx[B], oly[B] = pair_swap(ol[B], ol[B])
-    hl[A], n1[A], rstd[A] = out_and_norm(A, (ol[A], olx[A], oly[A], olr[A]))
+    hl[A], n1[A], rstd[A] = out_and_norm(A, (ol[A], olx[A], oly[A], *olr[A]))
     vec = const_spec((1, width))
     tile = block // OWN_STEPS
     full = rows_spec((block, width), tile)
@@ -2037,51 +2124,21 @@
             [((block, width), BF), ((block, width), F32), ((2, width), F32)], after,
         )
 
-    olrb = forward(chain, olx[B], oly[B])
-    sent, kept = plane_ffn_fwd(chain, True, hl[A], weights, ())
-    rs1[A] = pair_swap(*sent)
-    ff[A], kept_a = plane_ffn_fwd(chain, False, hl[A], weights, kept)
-    olr[B], rstd[A] = join_halves(chain, olrb, rstd[A])
-    hl[B], n1[B], rstd[B] = out_and_norm(B, (ol[B], olx[B], oly[B], olr[B]))
+    olr[B] = forward(chain, olx[B], oly[B])
+    sent, kept_a = plane_ffn_fwd(chain, None, hl[A], weights, ())
+    rs1[A], ff[A] = pair_swap(*sent[:2]), sent[2:]
+    hl[B], n1[B], rstd[B] = out_and_norm(B, (ol[B], olx[B], oly[B], *olr[B]))
     rs2[A] = pair_swap(*middle(chain, rs1[A], ff[A][0], ff[A][1]))
-    sent, kept = plane_ffn_fwd(chain, True, hl[B], weights, (), after=(*rs1[A],))
+    sent, kept = plane_ffn_fwd(chain, True, hl[B], weights, ())
     resid[A] = second_resid(A)
     rx[A], ry[A] = pair_swap(resid[A], resid[A])
     ff[B], kept_b = plane_ffn_fwd(chain, False, hl[B], weights, (*kept, *sent))
     al, slopes = {A: kept_a[0], B: kept_b[0]}, {A: kept_a[1:], B: kept_b[1:]}
-    rr[A], *sent = forward(chain, rx[A], ry[A], ff[B][3:])
-    rs1[B] = pair_swap(*sent)
+    rr[A] = forward(chain, rx[A], ry[A])
+    rs1[B] = pair_swap(*relay(chain, ff[B][3:], after=rr[A]))
 
     sums2, dffn, dgu, sums1, dr1, dattn, dax, day, dar = {}, {}, {}, {}, {}, {}, {}, {}, {}
-    activations, sums2[A], dffn[A] = second_norm(A, None)
-    rs2[B] = pair_swap(*middle(chain, rs1[B], ff[B][0], ff[B][1]))
-    sent, kept = plane_ffn_bwd(chain, True, dffn[A], slopes[A], weights, ())
-    resid[B] = second_resid(B)
-    rx[B], ry[B] = pair_swap(resid[B], resid[B])
-    fb[A], dgu[A] = plane_ffn_bwd(chain, False, dffn[A], slopes[A], weights, (*kept, *sent))
-    rr[B], *sent = forward(chain, rx[B], ry[B], fb[A][3:])
-    rs1[A] = pair_swap(*sent)
-    activations, sums2[B], dffn[B] = second_norm(B, activations)
-    down_update = grad_plain_columns(chain, (al[A], al[B]), (dffn[A], dffn[B]))
-    down_sum = lax.psum(down_update, ("obj", "dp"))
-    rs2[A] = pair_swap(*middle(chain, rs1[A], fb[A][0], fb[A][1]))
-    sent, dgu[B] = plane_ffn_bwd(chain, None, dffn[B], slopes[B], weights, ())
-    fb[B] = sent[2:]
-    dattn[A], dr1[A], sums1[A] = first_norm_back(A)
-    dax[A], day[A] = pair_swap(dattn[A], dattn[A])
-    rs1[B] = pair_swap(*sent[:2])
-    gate_send, gate_keep = grad_rows(chain, info[B], (hl[A], hl[B]), (dgu[A][0], dgu[B][0]))
-    line = Line(chain, edge)
-    line.add("gate", gate_keep, lax.ppermute(gate_send, "dp", CORES), 2)
-    rs2[B] = pair_swap(*middle(chain, rs1[B], fb[B][0], fb[B][1], after=(dax[A], day[A])))
-    dar[A] = forward(chain, dax[A], day[A])
-    up_send, up_keep = grad_rows(chain, info[B], (hl[A], hl[B]), (dgu[A][1], dgu[B][1]))
-    line.add("up", up_keep, lax.ppermute(up_send, "dp", CORES), 2)
-    line.advance()
-    dattn[B], dr1[B], sums1[B] = first_norm_back(B)
-    dax[B], day[B] = pair_swap(dattn[B], dattn[B])
-
-    pieces, dqkv, dx, dxx, dxy, dxr = {}, {}, {}, {}, {}, {}
+    pieces, dqkv, dx, dxx, dxy, dxr, outs = {}, {}, {}, {}, {}, {}, {}
 
     def attention_back(r, after=()):
         pieces[r] = (dattn[r], dax[r], day[r], *dar[r])
@@ -2100,62 +2157,96 @@
             [((block, width), BF)], after,
         )[0]
 
-    outs = {}
+    theirs = {}
+
+    def begin_finish(name):
+        theirs[name] = lax.ppermute(line.done[name], "dp", CORES)
 
     def finish_matrix(name, rows, columns, after=()):
-        mine = line.done[name]
-        theirs = lax.ppermute(mine, "dp", CORES)
-        outs[name] = widen(chain, info[B], mine, theirs, rows, columns, after)
-
-    mine = (me == 0).astype(F32)
-    sums = jnp.concatenate([sums1[A] + sums1[B], (sums2[A] + sums2[B]) * mine])
-    exchanges = [("dp", 1), ("tensor", 1), ("tensor", 2), ("obj", 1), ("obj", 2)]
-
-    def exchange(array):
-        axis, bit = exchanges.pop(0)
-        other = lax.ppermute(array, axis, [(i, i ^ bit) for i in range(lax.axis_size(axis))])
-        return array, other
-
+        outs[name] = widen(chain, info[B], line.done[name], theirs[name], rows, columns, after)
+
+    def middle_sums(r, after=()):
+        part = fb[r] if r not in ib else ib[r]
+        rs2[r] = pair_swap(*middle(chain, rs1[r], part[0], part[1], after))
+
+    line = Line(chain, edge)
+    activations, sums2[A], dffn[A] = second_norm(A, None)
+    sent, kept = plane_ffn_bwd(chain, True, dffn[A], slopes[A], weights, ())
+    rs1[A] = pair_swap(*sent)
+    rs2[B] = pair_swap(*middle(chain, rs1[B], ff[B][0], ff[B][1]))
+    fb[A], dgu[A] = plane_ffn_bwd(chain, False, dffn[A], slopes[A], weights, kept)
+    resid[B] = second_resid(B)
+    rx[B], ry[B] = pair_swap(resid[B], resid[B])
+    middle_sums(A)
+    rr[B] = forward(chain, rx[B], ry[B])
+    dattn[A], dr1[A], sums1[A] = first_norm_back(A)
+    dax[A], day[A] = pair_swap(dattn[A], dattn[A])
+    activations, sums2[B], dffn[B] = second_norm(B, activations)
+    down_update = grad_plain_columns(chain, (al[A], al[B]), (dffn[A], dffn[B]))
+    down_sum = lax.psum(down_update, ("obj", "dp"))
+    dar[A] = forward(chain, dax[A], day[A])
+    sent, dgu[B] = plane_ffn_bwd(chain, None, dffn[B], slopes[B], weights, ())
+    fb[B] = sent[2:]
+    rs1[B] = pair_swap(*sent[:2])
+    chain.close(*dar[A])
+    gate_send, gate_keep = grad_rows(chain, info[B], (hl[A], hl[B]), (dgu[A][0], dgu[B][0]))
+    gate_got = lax.ppermute(gate_send, "dp", CORES)
+    line.add("gate", gate_keep, gate_got, 2)
+    middle_sums(B)
+    up_send, up_keep = grad_rows(chain, info[B], (hl[A], hl[B]), (dgu[A][1], dgu[B][1]))
+    up_got = lax.ppermute(up_send, "dp", CORES)
+    line.add("up", up_keep, up_got, 2)
+    chain.close(gate_got)
+    dattn[B], dr1[B], sums1[B] = first_norm_back(B)
+    dax[B], day[B] = pair_swap(dattn[B], dattn[B])
+    chain.close(up_got)
+    line.advance()
     dqkv[A] = attention_back(A)
-    pair = exchange(sums)
-    line.advance()
     dar[B] = forward(chain, dax[B], day[B])
     input_back_sums(A)
     line.advance()
-    pair = exchange(add_small(chain, *pair))
     dqkv[B] = attention_back(B)
-    rs2[A] = pair_swap(*middle(chain, rs1[A], ib[A][0], ib[A][1]))
     line.advance()
-    pair = exchange(add_small(chain, *pair))
+    middle_sums(A)
     qkv_send, qkv_keep = grad_rows(chain, info[B], (tokens, tokens), (dqkv[A], dqkv[B]), after=(down_sum,))
-    line.add("qkv", qkv_keep, lax.ppermute(qkv_send, "dp", CORES), 3)
+    qkv_got = lax.ppermute(qkv_send, "dp", CORES)
+    line.add("qkv", qkv_keep, qkv_got, 3)
     dx[A] = input_grad_own(A)
     dxx[A], dxy[A] = pair_swap(dx[A], dx[A])
+    line.advance()
     input_back_sums(B)
+    chain.close(qkv_got, dxx[A], dxy[A])
+    out_send, out_keep = plane_grad_out(chain, info[B], (ol[A], ol[B]), (pieces[A], pieces[B]))
     line.advance()
-    pair = exchange(add_small(chain, *pair))
-    out_send, out_keep = plane_grad_out(chain, info[B], (ol[A], ol[B]), (pieces[A], pieces[B]))
-    line.add("out", out_keep, lax.ppermute(out_send, "dp", CORES), 1)
+    out_got = lax.ppermute(out_send, "dp", CORES)
+    line.add("out", out_keep, out_got, 1)
+    middle_sums(B)
+    line.advance()
+    chain.close(out_got)
     dxr[A] = forward(chain, dxx[A], dxy[A])
-    rs2[B] = pair_swap(*middle(chain, rs1[B], ib[B][0], ib[B][1]))
-    line.advance()
-    pair = exchange(add_small(chain, *pair))
-    input_grad = plane_place(chain, info[A], A, (dx[A], dxx[A], dxy[A], *dxr[A]), tokens.shape, None)
     dx[B] = input_grad_own(B)
     dxx[B], dxy[B] = pair_swap(dx[B], dx[B])
+    outs["down"] = cast(chain, down_sum)
+    line.advance()
+    begin_finish("gate")
+    input_grad = plane_place(chain, info[A], A, (dx[A], dxx[A], dxy[A], *dxr[A]), tokens.shape, None)
+    dxr[B] = forward(chain, dxx[B], dxy[B])
+    mine = (me == 0).astype(F32)
+    sums = jnp.concatenate([sums1[A] + sums1[B], (sums2[A] + sums2[B]) * mine])
+    every_sum = lax.all_gather(sums, ("obj", "dp", "tensor"))
+    line.advance()
     finish_matrix("gate", width, units)
     line.advance()
-    sums = add_small(chain, *pair)
-    dxr[B] = forward(chain, dxx[B], dxy[B])
+    begin_finish("up")
+    input_grad = plane_place(chain, info[B], B, (dx[B], dxx[B], dxy[B], *dxr[B]), tokens.shape, input_grad)
+    line.advance()
     finish_matrix("up", width, units)
+    begin_finish("qkv")
     line.advance()
-    input_grad = plane_place(chain, info[B], B, (dx[B], dxx[B], dxy[B], *dxr[B]), tokens.shape, input_grad)
-    while line.busy():
-        line.advance()
-        if "qkv" not in outs and line.complete("qkv"):
-            finish_matrix("qkv", width, qkv_weight.shape[1])
+    begin_finish("out")
+    finish_matrix("qkv", width, qkv_weight.shape[1])
+    sums = total_sum(chain, every_sum)
     finish_matrix("out", out_weight.shape[0], width)
-    outs["down"] = down_sum.astype(F32)
 
     return (
         activations,
@@ -2173,7 +2264,7 @@
 
 
 def body(*args):
-    if plane_case(args[0].shape, args[10].shape):
+    if plane_case(args[0].shape, args[7].shape, args[10].shape):
         return plane_body(*args)
     return general_body(*args)
 

time: 1030 us -> 956 us (0.928)
  waiting for transfers between devices: 221 us -> 183 us
  Pallas kernels: 620 us -> 600 us
    ppermute x13 -> x8, waiting for transfers between devices: 34.4 us -> 0.02 us  [the longest x4 0.01 us: begin_finish(): theirs[name] = lax.ppermute(line.done[name], 'dp', CORES)]
    ppermute x60, waiting for transfers between devices: 96 us -> 68.8 us  [swap(): return lax.ppermute(array, 'tensor', [(i, i ^ bit) for i in range(ways)])]
    ppermute x10, waiting for transfers between devices: 89.6 us -> 114 us  [advance(): lax.ppermute(self.sent, 'obj', [(0, 1), (3, 2), (1, 0), (2, 3)])]
    pallas_call x68 -> x64, Pallas kernels: 620 us -> 600 us  [call(): pl.pallas_call(wrapped, grid_spec=grid_spec, out_shape=[jax.ShapeDtypeStr...]
    unnamed x98 -> x54, local copies, waits for them, and re-layouts: 18.6 us -> 7.72 us
  transfers between devices with their start and end apart: 93 -> 89, of which waited for: 28 -> 27; matrix products, arithmetic and copies ran while one was open for 2% -> 2% of each run, Pallas kernels for 56% -> 61%
where the time goes in v3:
time: 956 us; the launch traced here: 946 us
  Pallas kernels  600 us (63%)
  waiting for transfers between devices  183 us (19%)
  starting transfers between devices  118 us (12%)
  local copies, waits for them, and re-layouts  19.1 us (2%)
  between operations  18.9 us (2%)
    pallas_call x64, Pallas kernels, call(): pl.pallas_call(wrapped, grid_spec=grid_spec, out_shape=[jax.ShapeDtypeStr...  600 us
    ppermute x10, waiting for transfers between devices, advance(): lax.ppermute(self.sent, 'obj', [(0, 1), (3, 2), (1, 0), (2, 3)])  114 us
    ppermute x60, waiting for transfers between devices, swap(): return lax.ppermute(array, 'tensor', [(i, i ^ bit) for i in range(ways)])  68.8 us
    ppermute x60, starting transfers between devices, swap(): return lax.ppermute(array, 'tensor', [(i, i ^ bit) for i in range(ways)])  63.7 us
    ppermute x10, starting transfers between devices, advance(): lax.ppermute(self.sent, 'obj', [(0, 1), (3, 2), (1, 0), (2, 3)])  41.7 us
  transfers between devices with their start and end apart: 89, of which 27 were waited for; matrix products, arithmetic and copies ran while one was open for 2% of the time, Pallas kernels for 61%

profile of v3, /device:TPU:0, one launch (start us, length us, event | category | flops | bytes accessed | tf_op | source)
XLA Modules:
  0.0 946.0 jit_solution(12638941609120562578)
XLA Ops:
  22.6 20.8 %attn_fwd.2 = (bf16[1024,1536]{1,0:T(8,128)(2,1)}, bf16[1024,512]{1,0:T(8,128)(2,1)}, f32[4,1,1024]{2,1,0:T(1,128)}) custom-call(s32[4]{0:T(128)} %add_add_fusion.1.refs_0_, bf16[2,1024,2048]{2,1,0:T(8,128)(2,1)} %refs_2_.11, bf16[2048,1536]{1,0:T(8,128)(2,1)} %refs_3_.17, f32[1024,128]{1,0:T(8,128)} %constant.40.clone.refs_3_.refs_9_, ...), custom_call_target="tpu_custom_call" | custom-call | flops 210000003072 | bytes 1000000 | tf_op jit(solution)/shard_map/attn_fwd/pallas_call | solution.py:838
  53.3 21.0 %attn_fwd.3 = (bf16[1024,1536]{1,0:T(8,128)(2,1)}, bf16[1024,512]{1,0:T(8,128)(2,1)}, f32[4,1,1024]{2,1,0:T(1,128)}) custom-call(s32[4]{0:T(128)} %add_add_fusion.refs_0_, bf16[2,1024,2048]{2,1,0:T(8,128)(2,1)} %refs_2_.11, bf16[2048,1536]{1,0:T(8,128)(2,1)} %refs_3_.17, f32[1024,128]{1,0:T(8,128)} %constant.40.clone.refs_3_.refs_9_, ...), custom_call_target="tpu_custom_call" | custom-call | flops 210000003072 | bytes 1000000 | tf_op jit(solution)/shard_map/attn_fwd/pallas_call | solution.py:838
  105.3 21.1 %out_norm.2 = (bf16[1024,2048]{1,0:T(8,128)(2,1)}, f32[256,2048]{1,0:T(8,128)}, f32[256,128]{1,0:T(8,128)}) custom-call(s32[4]{0:T(128)} %add_add_fusion.1.refs_0_, s32[8]{0:T(128)} %stack.54.refs_1_.refs_0_, bf16[1024,512]{1,0:T(8,128)(2,1)} %get-tuple-element.150.refs_2_.refs_7_.refs_1_, ...), custom_call_target="tpu_custom_call" | custom-call | flops 210000003072 | bytes 1000000 | tf_op jit(solution)/shard_map/out_norm/pallas_call | solution.py:838
  132.5 30.1 %ffn_fwd.3 = (bf16[256,2048]{1,0:T(8,128)(2,1)}, bf16[256,2048]{1,0:T(8,128)(2,1)}, bf16[128,2048]{1,0:T(8,128)(2,1)}, bf16[128,2048]{1,0:T(8,128)(2,1)}, bf16[2...) custom-call(bf16[1024,2048]{1,0:T(8,128)(2,1)} %get-tuple-element.161, ...), custom_call_target="tpu_custom_call" | custom-call | flops 359999995904 | bytes 1000000 | tf_op jit(solution)/shard_map/ffn_fwd/pallas_call | solution.py:838
  165.0 21.4 %out_norm.3 = (bf16[1024,2048]{1,0:T(8,128)(2,1)}, f32[256,2048]{1,0:T(8,128)}, f32[256,128]{1,0:T(8,128)}) custom-call(s32[4]{0:T(128)} %add_add_fusion.refs_0_, s32[8]{0:T(128)} %stack.54.refs_1_.refs_0_, bf16[1024,512]{1,0:T(8,128)(2,1)} %get-tuple-element.159.refs_2_.refs_7_, bf16[1024,512]{1,0:T(8,128)(2,1)} %collective-permute-done.8.refs_0_.refs_3_.refs_8_, ...), custom_call_target="tpu_custom_call" | custom-call | flops 210000003072 | bytes 1000000 | tf_op jit(solution)/shard_map/out_norm/pallas_call | solution.py:838
  191.5 17.7 %ffn_fwd.4 = (bf16[256,2048]{1,0:T(8,128)(2,1)}, bf16[256,2048]{1,0:T(8,128)(2,1)}, bf16[1024,1408]{1,0:T(8,128)(2,1)}, bf16[1024,1408]{1,0:T(8,128)(2,1)}, bf16[1024,1408]{1,0:T(8,128)(2,1)}) custom-call(bf16[1024,2048]{1,0:T(8,128)(2,1)} %get-tuple-element.165.refs_4_.refs_0_.refs_2_, bf16[2048,1408]{1,0:T(8,128)(2,1)} %refs_4_.7, ...), custom_call_target="tpu_custom_call" | custom-call | flops 179999997952 | bytes 1000000 | tf_op jit(solution)/shard_map/ffn_fwd/pallas_call | solution.py:838
  216.3 17.8 %ffn_fwd.5 = (bf16[128,2048]{1,0:T(8,128)(2,1)}, bf16[128,2048]{1,0:T(8,128)(2,1)}, bf16[256,2048]{1,0:T(8,128)(2,1)}, bf16[256,2048]{1,0:T(8,128)(2,1)}, bf16[2...) custom-call(bf16[1024,2048]{1,0:T(8,128)(2,1)} %get-tuple-element.16, ...), custom_call_target="tpu_custom_call", output_to_operand_aliasing={{5}: (4, {}), {6}: (5, {}), {7}: (6, {}), {3}: (7, {}), {4}... | custom-call | flops 179999997952 | bytes 1000000 | tf_op jit(solution)/shard_map/ffn_fwd/pallas_call | solution.py:838
  254.1 14.5 %norm_two.2 = (bf16[2,1024,2048]{2,1,0:T(8,128)(2,1)}, f32[2,2048]{1,0:T(2,128)}, bf16[1024,2048]{1,0:T(8,128)(2,1)}) custom-call(s32[4]{0:T(128)} %add_add_fusion.1.refs_0_, s32[8]{0:T(128)} %stack.54.refs_1_.refs_0_, f32[1]{0:T(128)} %get-tuple-element.299.refs_2_, bf16[256,2048]{1,0:T(8,128)(2,1)} %resid_two.2.refs_9_.refs_3_, ...), custom_call_target="tpu_custom_call" | custom-call | flops 149999992832 | bytes 1000000 | tf_op jit(solution)/shard_map/norm_two/pallas_call | solution.py:838
  268.6 19.1 %ffn_bwd.3 = (bf16[256,2048]{1,0:T(8,128)(2,1)}, bf16[256,2048]{1,0:T(8,128)(2,1)}, bf16[1024,1408]{1,0:T(8,128)(2,1)}, bf16[1024,1408]{1,0:T(8,128)(2,1)}) custom-call(bf16[1024,2048]{1,0:T(8,128)(2,1)} %get-tuple-element.188.refs_0_.refs_5_.refs_2_, bf16[1024,1408]{1,0:T(8,128)(2,1)} %get-tuple-element.189.refs_1_, ...), custom_call_target="tpu_custom_call" | custom-call | flops 179999997952 | bytes 1000000 | tf_op jit(solution)/shard_map/ffn_bwd/pallas_call | solution.py:838
  294.8 19.3 %ffn_bwd.4 = (bf16[128,2048]{1,0:T(8,128)(2,1)}, bf16[128,2048]{1,0:T(8,128)(2,1)}, bf16[256,2048]{1,0:T(8,128)(2,1)}, bf16[1024,1408]{1,0:T(8,128)(2,1)}, bf16[1024,1408]{1,0:T(8,128)(2,1)}) custom-call(bf16[1024,2048]{1,0:T(8,128)(2,1)} %get-tuple-element.188.refs_0_.refs_5_.refs_2_, ...), custom_call_target="tpu_custom_call", output_to_operand_aliasing={{3}: (6, {}), {4}: (7, {})} | custom-call | flops 179999997952 | bytes 1000000 | tf_op jit(solution)/shard_map/ffn_bwd/pallas_call | solution.py:838
  330.4 19.3 %collective-permute-done.25.refs_0_.refs_4_ = bf16[256,2048]{1,0:T(8,128)(2,1)S(1)} collective-permute-done((bf16[256,2048]{1,0:T(8,128)(2,1)}, bf16[256,2048]{1,0:T(8,128)(2,1)S(1)}, u32[]{:S(2)}, u32[]{:S(2)}) %collective-permute-start.25) | collective-permute-done | bytes 1048608 | tf_op jit(solution)/shard_map/ppermute | solution.py:551
  373.5 14.5 %norm_two.3 = (bf16[2,1024,2048]{2,1,0:T(8,128)(2,1)}, f32[2,2048]{1,0:T(2,128)}, bf16[1024,2048]{1,0:T(8,128)(2,1)}) custom-call(s32[4]{0:T(128)} %add_add_fusion.refs_0_, s32[8]{0:T(128)} %stack.54.refs_1_.refs_0_, f32[1]{0:T(128)} %get-tuple-element.300.refs_2_, bf16[256,2048]{1,0:T(8,128)(2,1)} %resid_two.3.refs_4_.refs_3_, ...), custom_call_target="tpu_custom_call", output_to_operand_aliasing={{0}: (11, {})} | custom-call | flops 149999992832 | bytes 1000000 | tf_op jit(solution)/shard_map/norm_two/pallas_call | solution.py:838
  388.0 19.1 %grad_plain_columns.1.refs_2_ = bf16[1408,2048]{1,0:T(8,128)(2,1)} custom-call(bf16[1024,1408]{1,0:T(8,128)(2,1)} %get-tuple-element.212.refs_0_, bf16[1024,1408]{1,0:T(8,128)(2,1)} %get-tuple-element.213.refs_1_, bf16[1024,2048]{1,0:T(8,128)(2,1)} %get-tuple-element.188.refs_0_.refs_5_.refs_2_, ...), custom_call_target="tpu_custom_call" | custom-call | flops 190000005120 | bytes 1000000 | tf_op jit(solution)/shard_map/grad_plain_columns/pallas_call | solution.py:838
  413.1 32.7 %ffn_bwd.5 = (bf16[256,2048]{1,0:T(8,128)(2,1)}, bf16[256,2048]{1,0:T(8,128)(2,1)}, bf16[128,2048]{1,0:T(8,128)(2,1)}, bf16[128,2048]{1,0:T(8,128)(2,1)}, bf16[2...) custom-call(bf16[1024,2048]{1,0:T(8,128)(2,1)} %get-tuple-element.209.refs_3_.refs_0_.refs_5_, ...), custom_call_target="tpu_custom_call" | custom-call | flops 359999995904 | bytes 1000000 | tf_op jit(solution)/shard_map/ffn_bwd/pallas_call | solution.py:838
  447.1 20.6 %grad_rows.3 = (bf16[11,1024,128]{2,1,0:T(8,128)(2,1)}, bf16[11,1024,128]{2,1,0:T(8,128)(2,1)}) custom-call(s32[4]{0:T(128)} %add_add_fusion.refs_0_, bf16[1024,2048]{1,0:T(8,128)(2,1)} %get-tuple-element.161.refs_2_.refs_0_.refs_1_, bf16[1024,2048]{1,0:T(8,128)(2,1)} %get-tuple-element.165.refs_4_.refs_0_.refs_2_, ...), custom_call_target="tpu_custom_call" | custom-call | flops 210000003072 | bytes 1000000 | tf_op jit(solution)/shard_map/grad_rows/pallas_call | solution.py:838
  473.5 20.6 %grad_rows.4 = (bf16[11,1024,128]{2,1,0:T(8,128)(2,1)}, bf16[11,1024,128]{2,1,0:T(8,128)(2,1)}) custom-call(s32[4]{0:T(128)} %add_add_fusion.refs_0_, bf16[1024,2048]{1,0:T(8,128)(2,1)} %get-tuple-element.161.refs_2_.refs_0_.refs_1_, bf16[1024,2048]{1,0:T(8,128)(2,1)} %get-tuple-element.165.refs_4_.refs_0_.refs_2_, ...), custom_call_target="tpu_custom_call" | custom-call | flops 210000003072 | bytes 1000000 | tf_op jit(solution)/shard_map/grad_rows/pallas_call | solution.py:838
  506.9 23.9 %attn_bwd.2.refs_2_.refs_1_.refs_3_ = bf16[1024,1536]{1,0:T(8,128)(2,1)} custom-call(s32[4]{0:T(128)} %add_add_fusion.1.refs_0_, bf16[1024,1536]{1,0:T(8,128)(2,1)} %get-tuple-element.151.refs_2_.refs_1_, bf16[256,2048]{1,0:T(8,128)(2,1)} %get-tuple-element.207.refs_12_.refs_2_.refs_3_, bf16[256,2048]{1,0:T(8,128)(2,1)} %collective-permute-done.33.refs_0_.refs_3_.refs_4_, ...), custom_call_target="tpu_custom_call" | custom-call | flops 240000008192 | bytes 1000000 | tf_op jit(solution)/shard_map/attn_bwd/pallas_call | solution.py:838
  550.8 20.8 %collective-permute-done.47.refs_5_ = bf16[5632,128]{1,0:T(8,128)(2,1)} collective-permute-done((bf16[5632,128]{1,0:T(8,128)(2,1)}, bf16[5632,128]{1,0:T(8,128)(2,1)}, u32[]{:S(2)}, u32[]{:S(2)}) %collective-permute-start.47) | collective-permute-done | bytes 1441824 | tf_op jit(solution)/shard_map/ppermute | solution.py:1953
  579.5 24.1 %attn_bwd.3.refs_8_.refs_4_.refs_1_.refs_2_ = bf16[1024,1536]{1,0:T(8,128)(2,1)} custom-call(s32[4]{0:T(128)} %add_add_fusion.refs_0_, bf16[1024,1536]{1,0:T(8,128)(2,1)} %get-tuple-element.155.refs_4_.refs_1_, bf16[256,2048]{1,0:T(8,128)(2,1)} %get-tuple-element.230.refs_3_.refs_2_.refs_8_, ...), custom_call_target="tpu_custom_call" | custom-call | flops 240000008192 | bytes 1000000 | tf_op jit(solution)/shard_map/attn_bwd/pallas_call | solution.py:838
  629.9 21.0 %grad_rows.5 = (bf16[12,1024,128]{2,1,0:T(8,128)(2,1)}, bf16[12,1024,128]{2,1,0:T(8,128)(2,1)}) custom-call(s32[4]{0:T(128)} %add_add_fusion.refs_0_, bf16[2,1024,2048]{2,1,0:T(8,128)(2,1)} %refs_2_.11, bf16[2,1024,2048]{2,1,0:T(8,128)(2,1)} %refs_2_.11, bf16[1024,1536]{1,0:T(8,128)(2,1)} %attn_bwd.2.refs_2_.refs_1_.refs_3_, ...), custom_call_target="tpu_custom_call" | custom-call | flops 210000003072 | bytes 1000000 | tf_op jit(solution)/shard_map/grad_rows/pallas_call | solution.py:838
  662.6 13.8 %input_back.3 = (bf16[256,2048]{1,0:T(8,128)(2,1)}, bf16[256,2048]{1,0:T(8,128)(2,1)}, bf16[128,2048]{1,0:T(8,128)(2,1)}, bf16[128,2048]{1,0:T(8,128)(2,1)}, bf16[256,2048]{1,0:T(8,128)(2,1)}) custom-call(s32[8]{0:T(128)} %stack.54.refs_1_.refs_0_, bf16[1024,1536]{1,0:T(8,128)(2,1)} %attn_bwd.3.refs_8_.refs_4_.refs_1_.refs_2_, ...), custom_call_target="tpu_custom_call" | custom-call | flops 140000002048 | bytes 1000000 | tf_op jit(solution)/shard_map/input_back/pallas_call | solution.py:838
  696.3 15.3 %collective-permute-done.59.refs_5_.refs_8_ = bf16[5632,128]{1,0:T(8,128)(2,1)} collective-permute-done((bf16[5632,128]{1,0:T(8,128)(2,1)S(1)}, bf16[5632,128]{1,0:T(8,128)(2,1)}, u32[]{:S(2)}, u32[]{:S(2)}) %collective-permute-start.59) | collective-permute-done | bytes 1441824 | tf_op jit(solution)/shard_map/ppermute | solution.py:1953
  729.1 21.5 %collective-permute-done.65.refs_5_.refs_8_ = bf16[5632,128]{1,0:T(8,128)(2,1)S(1)} collective-permute-done((bf16[5632,128]{1,0:T(8,128)(2,1)}, bf16[5632,128]{1,0:T(8,128)(2,1)S(1)}, u32[]{:S(2)}, u32[]{:S(2)}) %collective-permute-start.65) | collective-permute-done | bytes 1441824 | tf_op jit(solution)/shard_map/ppermute | solution.py:1953
  874.7 14.0 %collective-permute-done.82.refs_3_ = bf16[4096,128]{1,0:T(8,128)(2,1)} collective-permute-done((bf16[4096,128]{1,0:T(8,128)(2,1)}, bf16[4096,128]{1,0:T(8,128)(2,1)}, u32[]{:S(2)}, u32[]{:S(2)}) %collective-permute-start.82) | collective-permute-done | bytes 1048608 | tf_op jit(solution)/shard_map/ppermute | solution.py:1953
  (295 shorter events, 443.2 us)
Async XLA Ops:
  10.3 37.3 %collective-permute-start.2 = (bf16[256,2048]{1,0:T(8,128)(2,1)}, bf16[256,2048]{1,0:T(8,128)(2,1)}, u32[]{:S(2)}, u32[]{:S(2)}) collective-permute-start(bf16[256,2048]{1,0:T(8,128)(2,1)} %constant_dynamic-slice_fusion), channel_id=1, source_target_pairs={{0,1},{1,0},{2,3},{3,2},{4,5},{5,4},{6,7},{7,6},{8,9},{9,8},{10,11... | collective-permute-start | bytes 3145736 | tf_op jit(solution)/shard_map/ppermute | solution.py:551
  252.5 37.7 %collective-permute-start.21 = (bf16[256,2048]{1,0:T(8,128)(2,1)}, bf16[256,2048]{1,0:T(8,128)(2,1)}, u32[]{:S(2)}, u32[]{:S(2)}) collective-permute-start(bf16[256,2048]{1,0:T(8,128)(2,1)} %get-tuple-element.184), channel_id=1, source_target_pairs={{0,1},{1,0},{2,3},{3,2},{4,5},{5,4},{6,7},{7,6},{8,9},{9,8},{10,11... | collective-permute-start | bytes 3145736 | tf_op jit(solution)/shard_map/ppermute | solution.py:551
  253.1 37.1 %collective-permute-start.22 = (bf16[256,2048]{1,0:T(8,128)(2,1)}, bf16[256,2048]{1,0:T(8,128)(2,1)}, u32[]{:S(2)}, u32[]{:S(2)}) collective-permute-start(bf16[256,2048]{1,0:T(8,128)(2,1)} %get-tuple-element.185), channel_id=1, source_target_pairs={{0,2},{1,3},{2,0},{3,1},{4,6},{5,7},{6,4},{7,5},{8,10},{9,11},{10,... | collective-permute-start | bytes 3145736 | tf_op jit(solution)/shard_map/ppermute | solution.py:551
  287.7 36.9 %collective-permute-start.27 = (bf16[256,2048]{1,0:T(8,128)(2,1)}, bf16[256,2048]{1,0:T(8,128)(2,1)}, u32[]{:S(2)}, u32[]{:S(2)}) collective-permute-start(bf16[256,2048]{1,0:T(8,128)(2,1)} %get-tuple-element.192.refs_4_), channel_id=1, source_target_pairs={{0,1},{1,0},{2,3},{3,2},{4,5},{5,4},{6,7},{7,6},{8,9},{9,8},{10,11... | collective-permute-start | bytes 3145736 | tf_op jit(solution)/shard_map/ppermute | solution.py:551
  367.8 39.9 %collective-permute-start.33 = (bf16[256,2048]{1,0:T(8,128)(2,1)}, bf16[256,2048]{1,0:T(8,128)(2,1)}, u32[]{:S(2)}, u32[]{:S(2)}) collective-permute-start(bf16[256,2048]{1,0:T(8,128)(2,1)} %get-tuple-element.207.refs_12_.refs_2_.refs_3_), channel_id=1, source_target_pairs={{0,1},{1,0},{2,3},{3,2},{4,5},{5,4},{6,7},{7,6},{8,9},{9,8},{10,11... | collective-permute-start | bytes 3145736 | tf_op jit(solution)/shard_map/ppermute | solution.py:551
  368.9 38.8 %collective-permute-start.34 = (bf16[256,2048]{1,0:T(8,128)(2,1)}, bf16[256,2048]{1,0:T(8,128)(2,1)}, u32[]{:S(2)}, u32[]{:S(2)}) collective-permute-start(bf16[256,2048]{1,0:T(8,128)(2,1)} %get-tuple-element.207.refs_12_.refs_2_.refs_3_), channel_id=1, source_target_pairs={{0,2},{1,3},{2,0},{3,1},{4,6},{5,7},{6,4},{7,5},{8,10},{9,11},{10,... | collective-permute-start | bytes 3145736 | tf_op jit(solution)/shard_map/ppermute | solution.py:551
  409.9 219.9 %all-reduce.2.cloned.1.call-start = ((), (), s32[]{:S(2)}) async-start(), calls=%async_computation | async-start | bytes 11534336 | tf_op jit(solution)/shard_map/psum | solution.py:2186
  410.7 518.4 %all-gather.4.cloned.1.call-start = ((), (), s32[]{:S(2)}) async-start(), calls=%async_computation.1 | async-start | bytes 1081344 | tf_op jit(solution)/shard_map/all_gather | solution.py:2236
  506.7 64.9 %collective-permute-start.47 = (bf16[5632,128]{1,0:T(8,128)(2,1)}, bf16[5632,128]{1,0:T(8,128)(2,1)}, u32[]{:S(2)}, u32[]{:S(2)}) collective-permute-start(bf16[5632,128]{1,0:T(8,128)(2,1)} %line_step.11.refs_13_), channel_id=1, source_target_pairs={{0,8},{24,16},{8,0},{16,24},{1,9},{25,17},{9,1},{17,25},{2,10},{26... | collective-permute-start | bytes 4325384 | tf_op jit(solution)/shard_map/ppermute | solution.py:1953
  549.6 72.8 %collective-permute-start.52 = (bf16[256,2048]{1,0:T(8,128)(2,1)}, bf16[256,2048]{1,0:T(8,128)(2,1)}, u32[]{:S(2)}, u32[]{:S(2)}) collective-permute-start(bf16[256,2048]{1,0:T(8,128)(2,1)} %get-tuple-element.236.refs_6_), channel_id=1, source_target_pairs={{0,1},{1,0},{2,3},{3,2},{4,5},{5,4},{6,7},{7,6},{8,9},{9,8},{10,11... | collective-permute-start | bytes 3145736 | tf_op jit(solution)/shard_map/ppermute | solution.py:551
  549.9 72.5 %collective-permute-start.53 = (bf16[256,2048]{1,0:T(8,128)(2,1)}, bf16[256,2048]{1,0:T(8,128)(2,1)}, u32[]{:S(2)}, u32[]{:S(2)}) collective-permute-start(bf16[256,2048]{1,0:T(8,128)(2,1)} %get-tuple-element.243), channel_id=1, source_target_pairs={{0,2},{1,3},{2,0},{3,1},{4,6},{5,7},{6,4},{7,5},{8,10},{9,11},{10,... | collective-permute-start | bytes 3145736 | tf_op jit(solution)/shard_map/ppermute | solution.py:551
  576.3 37.2 %collective-permute-start.48 = (bf16[5632,128]{1,0:T(8,128)(2,1)}, bf16[5632,128]{1,0:T(8,128)(2,1)}, u32[]{:S(2)}, u32[]{:S(2)}) collective-permute-start(bf16[5632,128]{1,0:T(8,128)(2,1)} %get-tuple-element.237.refs_13_), channel_id=1, source_target_pairs={{0,8},{24,16},{8,0},{16,24},{1,9},{25,17},{9,1},{17,25},{2,10},{26... | collective-permute-start | bytes 4325384 | tf_op jit(solution)/shard_map/ppermute | solution.py:1953
  576.9 36.7 %collective-permute-start.49 = (bf16[5632,128]{1,0:T(8,128)(2,1)}, bf16[5632,128]{1,0:T(8,128)(2,1)}, u32[]{:S(2)}, u32[]{:S(2)}) collective-permute-start(bf16[5632,128]{1,0:T(8,128)(2,1)} %get-tuple-element.239.refs_6_), channel_id=1, source_target_pairs={{8,16},{16,8},{9,17},{17,9},{10,18},{18,10},{11,19},{19,11},{12,20... | collective-permute-start | bytes 4325384 | tf_op jit(solution)/shard_map/ppermute | solution.py:1955
  618.6 38.2 %collective-permute-start.50 = (bf16[5632,128]{1,0:T(8,128)(2,1)}, bf16[5632,128]{1,0:T(8,128)(2,1)}, u32[]{:S(2)}, u32[]{:S(2)}) collective-permute-start(bf16[5632,128]{1,0:T(8,128)(2,1)} %get-tuple-element.240.refs_4_.refs_9_), channel_id=1, source_target_pairs={{0,8},{24,16},{8,0},{16,24},{1,9},{25,17},{9,1},{17,25},{2,10},{26... | collective-permute-start | bytes 4325384 | tf_op jit(solution)/shard_map/ppermute | solution.py:1953
  684.3 39.8 %collective-permute-start.56 = (bf16[256,2048]{1,0:T(8,128)(2,1)}, bf16[256,2048]{1,0:T(8,128)(2,1)}, u32[]{:S(2)}, u32[]{:S(2)}) collective-permute-start(bf16[256,2048]{1,0:T(8,128)(2,1)} %get-tuple-element.252.refs_13_), channel_id=1, source_target_pairs={{0,1},{1,0},{2,3},{3,2},{4,5},{5,4},{6,7},{7,6},{8,9},{9,8},{10,11... | collective-permute-start | bytes 3145736 | tf_op jit(solution)/shard_map/ppermute | solution.py:551
  685.0 39.1 %collective-permute-start.57 = (bf16[256,2048]{1,0:T(8,128)(2,1)}, bf16[256,2048]{1,0:T(8,128)(2,1)}, u32[]{:S(2)}, u32[]{:S(2)}) collective-permute-start(bf16[256,2048]{1,0:T(8,128)(2,1)} %get-tuple-element.253), channel_id=1, source_target_pairs={{0,2},{1,3},{2,0},{3,1},{4,6},{5,7},{6,4},{7,5},{8,10},{9,11},{10,... | collective-permute-start | bytes 3145736 | tf_op jit(solution)/shard_map/ppermute | solution.py:551
  724.1 36.8 %collective-permute-start.67 = (bf16[4096,128]{1,0:T(8,128)(2,1)}, bf16[4096,128]{1,0:T(8,128)(2,1)}, u32[]{:S(2)}, u32[]{:S(2)}) collective-permute-start(bf16[4096,128]{1,0:T(8,128)(2,1)} %bitcast.51), channel_id=1, source_target_pairs={{0,4},{4,0},{1,5},{5,1},{2,6},{6,2},{3,7},{7,3},{8,12},{12,8},{9,1... | collective-permute-start | bytes 3145736 | tf_op jit(solution)/shard_map/ppermute | solution.py:2221
  727.0 37.7 %collective-permute-start.63 = (bf16[128,2048]{1,0:T(8,128)(2,1)}, bf16[128,2048]{1,0:T(8,128)(2,1)S(1)}, u32[]{:S(2)}, u32[]{:S(2)}) collective-permute-start(bf16[128,2048]{1,0:T(8,128)(2,1)} %get-tuple-element.261.refs_10_), channel_id=1, source_target_pairs={{0,1},{1,0},{2,3},{3,2},{4,5},{5,4},{6,7},{7,6},{8,9},{9,8},{10,11... | collective-permute-start | bytes 1572872 | tf_op jit(solution)/shard_map/ppermute | solution.py:551
  727.7 38.0 %collective-permute-start.64 = (bf16[128,2048]{1,0:T(8,128)(2,1)}, bf16[128,2048]{1,0:T(8,128)(2,1)}, u32[]{:S(2)}, u32[]{:S(2)}) collective-permute-start(bf16[128,2048]{1,0:T(8,128)(2,1)} %get-tuple-element.262), channel_id=1, source_target_pairs={{0,2},{1,3},{2,0},{3,1},{4,6},{5,7},{6,4},{7,5},{8,10},{9,11},{10,... | collective-permute-start | bytes 1572872 | tf_op jit(solution)/shard_map/ppermute | solution.py:551
  750.6 87.1 %collective-permute-start.80 = (bf16[11264,128]{1,0:T(8,128)(2,1)}, bf16[11264,128]{1,0:T(8,128)(2,1)}, u32[]{:S(2)}, u32[]{:S(2)}) collective-permute-start(bf16[11264,128]{1,0:T(8,128)(2,1)} %get-tuple-element.278), channel_id=1, source_target_pairs={{0,4},{4,0},{1,5},{5,1},{2,6},{6,2},{3,7},{7,3},{8,12},{12,8},{9,1... | collective-permute-start | bytes 8650760 | tf_op jit(solution)/shard_map/ppermute | solution.py:2163
  770.2 41.7 %collective-permute-start.68 = (bf16[256,2048]{1,0:T(8,128)(2,1)}, bf16[256,2048]{1,0:T(8,128)(2,1)}, u32[]{:S(2)}, u32[]{:S(2)}) collective-permute-start(bf16[256,2048]{1,0:T(8,128)(2,1)} %input_grad.3.refs_1_), channel_id=1, source_target_pairs={{0,1},{1,0},{2,3},{3,2},{4,5},{5,4},{6,7},{7,6},{8,9},{9,8},{10,11... | collective-permute-start | bytes 3145736 | tf_op jit(solution)/shard_map/ppermute | solution.py:551
  814.2 55.2 %collective-permute-start.74 = (bf16[128,2048]{1,0:T(8,128)(2,1)}, bf16[128,2048]{1,0:T(8,128)(2,1)}, u32[]{:S(2)}, u32[]{:S(2)}) collective-permute-start(bf16[128,2048]{1,0:T(8,128)(2,1)} %get-tuple-element.271.refs_10_), channel_id=1, source_target_pairs={{0,2},{1,3},{2,0},{3,1},{4,6},{5,7},{6,4},{7,5},{8,10},{9,11},{10,... | collective-permute-start | bytes 1572872 | tf_op jit(solution)/shard_map/ppermute | solution.py:551
  815.3 54.2 %collective-permute-start.75 = (bf16[128,2048]{1,0:T(8,128)(2,1)}, bf16[128,2048]{1,0:T(8,128)(2,1)}, u32[]{:S(2)}, u32[]{:S(2)}) collective-permute-start(bf16[128,2048]{1,0:T(8,128)(2,1)} %get-tuple-element.272), channel_id=1, source_target_pairs={{0,1},{1,0},{2,3},{3,2},{4,5},{5,4},{6,7},{7,6},{8,9},{9,8},{10,11... | collective-permute-start | bytes 1572872 | tf_op jit(solution)/shard_map/ppermute | solution.py:551
  820.9 74.7 %collective-permute-start.85 = (bf16[11264,128]{1,0:T(8,128)(2,1)}, bf16[11264,128]{1,0:T(8,128)(2,1)}, u32[]{:S(2)}, u32[]{:S(2)}) collective-permute-start(bf16[11264,128]{1,0:T(8,128)(2,1)} %get-tuple-element.284), channel_id=1, source_target_pairs={{0,4},{4,0},{1,5},{5,1},{2,6},{6,2},{3,7},{7,3},{8,12},{12,8},{9,1... | collective-permute-start | bytes 8650760 | tf_op jit(solution)/shard_map/ppermute | solution.py:2163
  (92 other events, 1813.9 us)
Sparse Core Ops, SparseCore 0:
  413.7 158.0 all-reduce.1
Sparse Core Ops, SparseCore 1:
  503.0 99.8 all-gather.3

commit v4 on v3

--- a/solution.py
+++ b/solution.py
@@ -793,12 +793,13 @@
 
 ORDER = ((1, 0), (3, 0), (2, 1), (3, 1), (1, 1), (2, 0), (0, 0), (0, 1))
 CORES = ((0, 1), (1, 0))
-DECLARED_FLOPS = 1e10
+DECLARED_FLOPS = 1e9
 MICROS = {
-    "attn_fwd": 21, "split": 2, "ow_join": 4, "relay": 1, "out_norm": 21, "middle_sum": 3, "resid_two": 5,
-    "norm_two": 15, "grad_columns": 20, "grad_plain_columns": 19, "grad_plain": 19, "line_step": 5, "grad_rows": 21,
-    "attn_bwd": 24, "norm_one_back": 6, "input_back": 14, "input_grad": 5, "grad_out": 11, "place": 5, "widen": 10,
-    "cast": 9, "total_sum": 2,
+    "attn_fwd": 1050, "split": 2, "ow_join": 4, "relay": 0.05, "out_norm": 21,
+    "middle_sum": 0.6, "resid_two": 25, "norm_two": 15, "grad_columns": 1000, "grad_plain_columns": 0.57,
+    "grad_plain": 3.8, "line_step": 5, "grad_rows": 1050, "attn_bwd": 1200, "norm_one_back": 30,
+    "input_back": 70, "input_grad": 5, "grad_out": 0.55, "place": 5, "widen": 50,
+    "cast": 9, "total_sum": 1,
 }
 
 
@@ -2221,31 +2222,32 @@
     out_got = lax.ppermute(out_send, "dp", CORES)
     line.add("out", out_keep, out_got, 1)
     middle_sums(B)
+    outs["down"] = cast(chain, down_sum)
     line.advance()
     chain.close(out_got)
+    begin_finish("gate")
     dxr[A] = forward(chain, dxx[A], dxy[A])
     dx[B] = input_grad_own(B)
     dxx[B], dxy[B] = pair_swap(dx[B], dx[B])
-    outs["down"] = cast(chain, down_sum)
+    chain.close(theirs["gate"])
     line.advance()
-    begin_finish("gate")
+    begin_finish("up")
+    finish_matrix("gate", width, units)
     input_grad = plane_place(chain, info[A], A, (dx[A], dxx[A], dxy[A], *dxr[A]), tokens.shape, None)
     dxr[B] = forward(chain, dxx[B], dxy[B])
     mine = (me == 0).astype(F32)
     sums = jnp.concatenate([sums1[A] + sums1[B], (sums2[A] + sums2[B]) * mine])
     every_sum = lax.all_gather(sums, ("obj", "dp", "tensor"))
     line.advance()
-    finish_matrix("gate", width, units)
-    line.advance()
-    begin_finish("up")
+    finish_matrix("up", width, units)
     input_grad = plane_place(chain, info[B], B, (dx[B], dxx[B], dxy[B], *dxr[B]), tokens.shape, input_grad)
     line.advance()
-    finish_matrix("up", width, units)
+    sums = total_sum(chain, every_sum)
+    line.advance()
     begin_finish("qkv")
+    finish_matrix("qkv", width, qkv_weight.shape[1])
     line.advance()
     begin_finish("out")
-    finish_matrix("qkv", width, qkv_weight.shape[1])
-    sums = total_sum(chain, every_sum)
     finish_matrix("out", out_weight.shape[0], width)
 
     return (

time: 956 us -> 1010 us (1.056)
  waiting for transfers between devices: 183 us -> 248 us
  starting transfers between devices: 118 us -> 103 us
    psum x1, waiting for transfers between devices: 0.01 us -> 59.2 us  [plane_body(): down_sum = lax.psum(down_update, ('obj', 'dp'))]
    ppermute x10, starting transfers between devices: 41.7 us -> 24.9 us  [advance(): lax.ppermute(self.sent, 'obj', [(0, 1), (3, 2), (1, 0), (2, 3)])]
  transfers between devices with their start and end apart: 89 -> 89, of which waited for: 27 -> 30; matrix products, arithmetic and copies ran while one was open for 2% -> 1% of each run, Pallas kernels for 61% -> 57%
where the time goes in v4:
time: 1010 us; the launch traced here: 1000 us
  Pallas kernels  599 us (59%)
  waiting for transfers between devices  248 us (25%)
  starting transfers between devices  103 us (10%)
  local copies, waits for them, and re-layouts  28 us (3%)
  between operations  18.9 us (2%)
    pallas_call x64, Pallas kernels, call(): pl.pallas_call(wrapped, grid_spec=grid_spec, out_shape=[jax.ShapeDtypeStr...  599 us
    ppermute x10, waiting for transfers between devices, advance(): lax.ppermute(self.sent, 'obj', [(0, 1), (3, 2), (1, 0), (2, 3)])  112 us
    ppermute x60, waiting for transfers between devices, swap(): return lax.ppermute(array, 'tensor', [(i, i ^ bit) for i in range(ways)])  70.8 us
    ppermute x60, starting transfers between devices, swap(): return lax.ppermute(array, 'tensor', [(i, i ^ bit) for i in range(ways)])  64.2 us
    psum x1, waiting for transfers between devices, plane_body(): down_sum = lax.psum(down_update, ('obj', 'dp'))  59.2 us
    ppermute x10, starting transfers between devices, advance(): lax.ppermute(self.sent, 'obj', [(0, 1), (3, 2), (1, 0), (2, 3)])  24.9 us
  transfers between devices with their start and end apart: 89, of which 30 were waited for; matrix products, arithmetic and copies ran while one was open for 1% of the time, Pallas kernels for 57%

profile of v4, /device:TPU:0, one launch (start us, length us, event | category | flops | bytes accessed | tf_op | source)
XLA Modules:
  0.0 1001.9 jit_solution(7242676250771284458)
XLA Ops:
  22.4 20.9 %attn_fwd.2 = (bf16[1024,1536]{1,0:T(8,128)(2,1)}, bf16[1024,512]{1,0:T(8,128)(2,1)}, f32[4,1,1024]{2,1,0:T(1,128)}) custom-call(s32[4]{0:T(128)} %add_add_fusion.1.refs_0_, bf16[2,1024,2048]{2,1,0:T(8,128)(2,1)} %refs_2_.11, bf16[2048,1536]{1,0:T(8,128)(2,1)} %refs_3_.17, f32[1024,128]{1,0:T(8,128)} %constant.40.clone.refs_3_.refs_9_, ...), custom_call_target="tpu_custom_call" | custom-call | flops 1050000031744 | bytes 1000000 | tf_op jit(solution)/shard_map/attn_fwd/pallas_call | solution.py:839
  53.1 20.9 %attn_fwd.3 = (bf16[1024,1536]{1,0:T(8,128)(2,1)}, bf16[1024,512]{1,0:T(8,128)(2,1)}, f32[4,1,1024]{2,1,0:T(1,128)}) custom-call(s32[4]{0:T(128)} %add_add_fusion.refs_0_, bf16[2,1024,2048]{2,1,0:T(8,128)(2,1)} %refs_2_.11, bf16[2048,1536]{1,0:T(8,128)(2,1)} %refs_3_.17, f32[1024,128]{1,0:T(8,128)} %constant.40.clone.refs_3_.refs_9_, ...), custom_call_target="tpu_custom_call" | custom-call | flops 1050000031744 | bytes 1000000 | tf_op jit(solution)/shard_map/attn_fwd/pallas_call | solution.py:839
  105.3 21.1 %out_norm.2 = (bf16[1024,2048]{1,0:T(8,128)(2,1)}, f32[256,2048]{1,0:T(8,128)}, f32[256,128]{1,0:T(8,128)}) custom-call(s32[4]{0:T(128)} %add_add_fusion.1.refs_0_, s32[8]{0:T(128)} %stack.54.refs_1_.refs_0_, bf16[1024,512]{1,0:T(8,128)(2,1)} %get-tuple-element.150.refs_2_.refs_7_.refs_1_, ...), custom_call_target="tpu_custom_call" | custom-call | flops 20999999488 | bytes 1000000 | tf_op jit(solution)/shard_map/out_norm/pallas_call | solution.py:839
  133.1 30.1 %ffn_fwd.3 = (bf16[256,2048]{1,0:T(8,128)(2,1)}, bf16[256,2048]{1,0:T(8,128)(2,1)}, bf16[128,2048]{1,0:T(8,128)(2,1)}, bf16[128,2048]{1,0:T(8,128)(2,1)}, bf16[2...) custom-call(bf16[1024,2048]{1,0:T(8,128)(2,1)} %get-tuple-element.161, ...), custom_call_target="tpu_custom_call" | custom-call | flops 35999997952 | bytes 1000000 | tf_op jit(solution)/shard_map/ffn_fwd/pallas_call | solution.py:839
  165.8 21.3 %out_norm.3 = (bf16[1024,2048]{1,0:T(8,128)(2,1)}, f32[256,2048]{1,0:T(8,128)}, f32[256,128]{1,0:T(8,128)}) custom-call(s32[4]{0:T(128)} %add_add_fusion.refs_0_, s32[8]{0:T(128)} %stack.54.refs_1_.refs_0_, bf16[1024,512]{1,0:T(8,128)(2,1)} %get-tuple-element.159.refs_2_.refs_7_, bf16[1024,512]{1,0:T(8,128)(2,1)} %copy-done.26, ...), custom_call_target="tpu_custom_call" | custom-call | flops 20999999488 | bytes 1000000 | tf_op jit(solution)/shard_map/out_norm/pallas_call | solution.py:839
  193.4 17.6 %ffn_fwd.4 = (bf16[256,2048]{1,0:T(8,128)(2,1)}, bf16[256,2048]{1,0:T(8,128)(2,1)}, bf16[1024,1408]{1,0:T(8,128)(2,1)}, bf16[1024,1408]{1,0:T(8,128)(2,1)}, bf16[1024,1408]{1,0:T(8,128)(2,1)}) custom-call(bf16[1024,2048]{1,0:T(8,128)(2,1)} %get-tuple-element.165.refs_4_.refs_0_.refs_2_, bf16[2048,1408]{1,0:T(8,128)(2,1)} %refs_4_.7, ...), custom_call_target="tpu_custom_call" | custom-call | flops 17999998976 | bytes 1000000 | tf_op jit(solution)/shard_map/ffn_fwd/pallas_call | solution.py:839
  218.3 17.9 %ffn_fwd.5 = (bf16[128,2048]{1,0:T(8,128)(2,1)}, bf16[128,2048]{1,0:T(8,128)(2,1)}, bf16[256,2048]{1,0:T(8,128)(2,1)}, bf16[256,2048]{1,0:T(8,128)(2,1)}, bf16[2...) custom-call(bf16[1024,2048]{1,0:T(8,128)(2,1)} %get-tuple-element.16, ...), custom_call_target="tpu_custom_call", output_to_operand_aliasing={{5}: (4, {}), {6}: (5, {}), {7}: (6, {}), {3}: (7, {}), {4}... | custom-call | flops 17999998976 | bytes 1000000 | tf_op jit(solution)/shard_map/ffn_fwd/pallas_call | solution.py:839
  256.6 14.4 %norm_two.2 = (bf16[2,1024,2048]{2,1,0:T(8,128)(2,1)}, f32[2,2048]{1,0:T(2,128)}, bf16[1024,2048]{1,0:T(8,128)(2,1)}) custom-call(s32[4]{0:T(128)} %add_add_fusion.1.refs_0_, s32[8]{0:T(128)} %stack.54.refs_1_.refs_0_, f32[1]{0:T(128)} %get-tuple-element.299.refs_2_, bf16[256,2048]{1,0:T(8,128)(2,1)} %resid_two.2.refs_9_.refs_3_, ...), custom_call_target="tpu_custom_call" | custom-call | flops 15000000512 | bytes 1000000 | tf_op jit(solution)/shard_map/norm_two/pallas_call | solution.py:839
  271.0 19.2 %ffn_bwd.3 = (bf16[256,2048]{1,0:T(8,128)(2,1)}, bf16[256,2048]{1,0:T(8,128)(2,1)}, bf16[1024,1408]{1,0:T(8,128)(2,1)}, bf16[1024,1408]{1,0:T(8,128)(2,1)}) custom-call(bf16[1024,2048]{1,0:T(8,128)(2,1)} %get-tuple-element.188.refs_0_.refs_5_.refs_2_, bf16[1024,1408]{1,0:T(8,128)(2,1)} %get-tuple-element.189.refs_1_, ...), custom_call_target="tpu_custom_call" | custom-call | flops 17999998976 | bytes 1000000 | tf_op jit(solution)/shard_map/ffn_bwd/pallas_call | solution.py:839
  297.3 19.3 %ffn_bwd.4 = (bf16[128,2048]{1,0:T(8,128)(2,1)}, bf16[128,2048]{1,0:T(8,128)(2,1)}, bf16[256,2048]{1,0:T(8,128)(2,1)}, bf16[1024,1408]{1,0:T(8,128)(2,1)}, bf16[1024,1408]{1,0:T(8,128)(2,1)}) custom-call(bf16[1024,2048]{1,0:T(8,128)(2,1)} %get-tuple-element.188.refs_0_.refs_5_.refs_2_, ...), custom_call_target="tpu_custom_call", output_to_operand_aliasing={{3}: (6, {}), {4}: (7, {})} | custom-call | flops 17999998976 | bytes 1000000 | tf_op jit(solution)/shard_map/ffn_bwd/pallas_call | solution.py:839
  335.5 18.5 %collective-permute-done.25.refs_0_.refs_4_ = bf16[256,2048]{1,0:T(8,128)(2,1)} collective-permute-done((bf16[256,2048]{1,0:T(8,128)(2,1)}, bf16[256,2048]{1,0:T(8,128)(2,1)}, u32[]{:S(2)}, u32[]{:S(2)}) %collective-permute-start.25) | collective-permute-done | bytes 1048608 | tf_op jit(solution)/shard_map/ppermute | solution.py:551
  378.0 14.5 %norm_two.3 = (bf16[2,1024,2048]{2,1,0:T(8,128)(2,1)}, f32[2,2048]{1,0:T(2,128)}, bf16[1024,2048]{1,0:T(8,128)(2,1)}) custom-call(s32[4]{0:T(128)} %add_add_fusion.refs_0_, s32[8]{0:T(128)} %stack.54.refs_1_.refs_0_, f32[1]{0:T(128)} %get-tuple-element.300.refs_2_, bf16[256,2048]{1,0:T(8,128)(2,1)} %resid_two.3.refs_4_.refs_3_, ...), custom_call_target="tpu_custom_call", output_to_operand_aliasing={{0}: (11, {})} | custom-call | flops 15000000512 | bytes 1000000 | tf_op jit(solution)/shard_map/norm_two/pallas_call | solution.py:839
  392.5 19.1 %grad_plain_columns.1.refs_2_ = bf16[1408,2048]{1,0:T(8,128)(2,1)} custom-call(bf16[1024,1408]{1,0:T(8,128)(2,1)} %get-tuple-element.212.refs_0_, bf16[1024,1408]{1,0:T(8,128)(2,1)} %get-tuple-element.213.refs_1_, bf16[1024,2048]{1,0:T(8,128)(2,1)} %get-tuple-element.188.refs_0_.refs_5_.refs_2_, ...), custom_call_target="tpu_custom_call" | custom-call | flops 570000000 | bytes 1000000 | tf_op jit(solution)/shard_map/grad_plain_columns/pallas_call | solution.py:839
  416.9 32.2 %ffn_bwd.5 = (bf16[256,2048]{1,0:T(8,128)(2,1)}, bf16[256,2048]{1,0:T(8,128)(2,1)}, bf16[128,2048]{1,0:T(8,128)(2,1)}, bf16[128,2048]{1,0:T(8,128)(2,1)}, bf16[2...) custom-call(bf16[1024,2048]{1,0:T(8,128)(2,1)} %get-tuple-element.209.refs_3_.refs_0_.refs_5_, ...), custom_call_target="tpu_custom_call" | custom-call | flops 35999997952 | bytes 1000000 | tf_op jit(solution)/shard_map/ffn_bwd/pallas_call | solution.py:839
  452.1 20.5 %grad_rows.3 = (bf16[11,1024,128]{2,1,0:T(8,128)(2,1)}, bf16[11,1024,128]{2,1,0:T(8,128)(2,1)}) custom-call(s32[4]{0:T(128)} %add_add_fusion.refs_0_, bf16[1024,2048]{1,0:T(8,128)(2,1)} %get-tuple-element.161.refs_2_.refs_0_.refs_1_, bf16[1024,2048]{1,0:T(8,128)(2,1)} %get-tuple-element.165.refs_4_.refs_0_.refs_2_, ...), custom_call_target="tpu_custom_call" | custom-call | flops 1050000031744 | bytes 1000000 | tf_op jit(solution)/shard_map/grad_rows/pallas_call | solution.py:839
  477.7 20.5 %grad_rows.4 = (bf16[11,1024,128]{2,1,0:T(8,128)(2,1)}, bf16[11,1024,128]{2,1,0:T(8,128)(2,1)}) custom-call(s32[4]{0:T(128)} %add_add_fusion.refs_0_, bf16[1024,2048]{1,0:T(8,128)(2,1)} %get-tuple-element.161.refs_2_.refs_0_.refs_1_, bf16[1024,2048]{1,0:T(8,128)(2,1)} %get-tuple-element.165.refs_4_.refs_0_.refs_2_, ...), custom_call_target="tpu_custom_call" | custom-call | flops 1050000031744 | bytes 1000000 | tf_op jit(solution)/shard_map/grad_rows/pallas_call | solution.py:839
  510.5 23.7 %attn_bwd.2.refs_2_.refs_1_.refs_3_ = bf16[1024,1536]{1,0:T(8,128)(2,1)} custom-call(s32[4]{0:T(128)} %add_add_fusion.1.refs_0_, bf16[1024,1536]{1,0:T(8,128)(2,1)} %get-tuple-element.151.refs_2_.refs_1_, bf16[256,2048]{1,0:T(8,128)(2,1)} %get-tuple-element.207.refs_12_.refs_2_.refs_3_, bf16[256,2048]{1,0:T(8,128)(2,1)} %copy-done.3, ...), custom_call_target="tpu_custom_call" | custom-call | flops 1199999942656 | bytes 1000000 | tf_op jit(solution)/shard_map/attn_bwd/pallas_call | solution.py:839
  554.2 21.6 %collective-permute-done.47.refs_5_ = bf16[5632,128]{1,0:T(8,128)(2,1)} collective-permute-done((bf16[5632,128]{1,0:T(8,128)(2,1)}, bf16[5632,128]{1,0:T(8,128)(2,1)}, u32[]{:S(2)}, u32[]{:S(2)}) %collective-permute-start.47) | collective-permute-done | bytes 1441824 | tf_op jit(solution)/shard_map/ppermute | solution.py:1954
  583.4 23.9 %attn_bwd.3.refs_8_.refs_4_.refs_1_.refs_2_ = bf16[1024,1536]{1,0:T(8,128)(2,1)} custom-call(s32[4]{0:T(128)} %add_add_fusion.refs_0_, bf16[1024,1536]{1,0:T(8,128)(2,1)} %get-tuple-element.155.refs_4_.refs_1_, bf16[256,2048]{1,0:T(8,128)(2,1)} %get-tuple-element.230.refs_3_.refs_2_.refs_8_, ...), custom_call_target="tpu_custom_call" | custom-call | flops 1199999942656 | bytes 1000000 | tf_op jit(solution)/shard_map/attn_bwd/pallas_call | solution.py:839
  607.3 27.4 %collective-permute-done.48.refs_5_ = bf16[5632,128]{1,0:T(8,128)(2,1)} collective-permute-done((bf16[5632,128]{1,0:T(8,128)(2,1)}, bf16[5632,128]{1,0:T(8,128)(2,1)}, u32[]{:S(2)}, u32[]{:S(2)}) %collective-permute-start.48) | collective-permute-done | bytes 1441824 | tf_op jit(solution)/shard_map/ppermute | solution.py:1954
  648.4 59.2 %all-reduce.2.cloned.1.call-done.refs_6_.refs_0_ = bf16[1408,2048]{1,0:T(8,128)(2,1)} async-done(((bf16[1408,2048]{1,0:T(8,128)(2,1)}), bf16[1408,2048]{1,0:T(8,128)(2,1)}) %all-reduce.2.cloned.1.call-update) | async-done | bytes 5767184 | tf_op jit(solution)/shard_map/psum | solution.py:2187
  707.6 20.7 %grad_rows.5 = (bf16[12,1024,128]{2,1,0:T(8,128)(2,1)}, bf16[12,1024,128]{2,1,0:T(8,128)(2,1)}) custom-call(s32[4]{0:T(128)} %add_add_fusion.refs_0_, bf16[2,1024,2048]{2,1,0:T(8,128)(2,1)} %refs_2_.11, bf16[2,1024,2048]{2,1,0:T(8,128)(2,1)} %refs_2_.11, bf16[1024,1536]{1,0:T(8,128)(2,1)} %attn_bwd.2.refs_2_.refs_1_.refs_3_, ...), custom_call_target="tpu_custom_call" | custom-call | flops 1050000031744 | bytes 1000000 | tf_op jit(solution)/shard_map/grad_rows/pallas_call | solution.py:839
  800.0 17.7 %collective-permute-done.65.refs_5_.refs_8_ = bf16[5632,128]{1,0:T(8,128)(2,1)S(1)} collective-permute-done((bf16[5632,128]{1,0:T(8,128)(2,1)}, bf16[5632,128]{1,0:T(8,128)(2,1)S(1)}, u32[]{:S(2)}, u32[]{:S(2)}) %collective-permute-start.65) | collective-permute-done | bytes 1441824 | tf_op jit(solution)/shard_map/ppermute | solution.py:1954
  934.7 16.5 %collective-permute-done.83.refs_3_ = bf16[4096,128]{1,0:T(8,128)(2,1)} collective-permute-done((bf16[4096,128]{1,0:T(8,128)(2,1)}, bf16[4096,128]{1,0:T(8,128)(2,1)}, u32[]{:S(2)}, u32[]{:S(2)}) %collective-permute-start.83) | collective-permute-done | bytes 1048608 | tf_op jit(solution)/shard_map/ppermute | solution.py:1954
  (319 shorter events, 444.2 us)
Async XLA Ops:
  10.3 37.1 %collective-permute-start.2 = (bf16[256,2048]{1,0:T(8,128)(2,1)}, bf16[256,2048]{1,0:T(8,128)(2,1)}, u32[]{:S(2)}, u32[]{:S(2)}) collective-permute-start(bf16[256,2048]{1,0:T(8,128)(2,1)} %constant_dynamic-slice_fusion), channel_id=1, source_target_pairs={{0,1},{1,0},{2,3},{3,2},{4,5},{5,4},{6,7},{7,6},{8,9},{9,8},{10,11... | collective-permute-start | bytes 3145736 | tf_op jit(solution)/shard_map/ppermute | solution.py:551
  255.4 37.8 %collective-permute-start.21 = (bf16[256,2048]{1,0:T(8,128)(2,1)}, bf16[256,2048]{1,0:T(8,128)(2,1)}, u32[]{:S(2)}, u32[]{:S(2)}) collective-permute-start(bf16[256,2048]{1,0:T(8,128)(2,1)} %get-tuple-element.184), channel_id=1, source_target_pairs={{0,1},{1,0},{2,3},{3,2},{4,5},{5,4},{6,7},{7,6},{8,9},{9,8},{10,11... | collective-permute-start | bytes 3145736 | tf_op jit(solution)/shard_map/ppermute | solution.py:551
  255.9 37.3 %collective-permute-start.22 = (bf16[256,2048]{1,0:T(8,128)(2,1)}, bf16[256,2048]{1,0:T(8,128)(2,1)}, u32[]{:S(2)}, u32[]{:S(2)}) collective-permute-start(bf16[256,2048]{1,0:T(8,128)(2,1)} %get-tuple-element.185), channel_id=1, source_target_pairs={{0,2},{1,3},{2,0},{3,1},{4,6},{5,7},{6,4},{7,5},{8,10},{9,11},{10,... | collective-permute-start | bytes 3145736 | tf_op jit(solution)/shard_map/ppermute | solution.py:551
  290.2 39.5 %collective-permute-start.27 = (bf16[256,2048]{1,0:T(8,128)(2,1)}, bf16[256,2048]{1,0:T(8,128)(2,1)S(1)}, u32[]{:S(2)}, u32[]{:S(2)}) collective-permute-start(bf16[256,2048]{1,0:T(8,128)(2,1)} %get-tuple-element.192.refs_4_), channel_id=1, source_target_pairs={{0,1},{1,0},{2,3},{3,2},{4,5},{5,4},{6,7},{7,6},{8,9},{9,8},{10,11... | collective-permute-start | bytes 3145736 | tf_op jit(solution)/shard_map/ppermute | solution.py:551
  291.8 37.9 %collective-permute-start.28 = (bf16[256,2048]{1,0:T(8,128)(2,1)}, bf16[256,2048]{1,0:T(8,128)(2,1)}, u32[]{:S(2)}, u32[]{:S(2)}) collective-permute-start(bf16[256,2048]{1,0:T(8,128)(2,1)} %get-tuple-element.199), channel_id=1, source_target_pairs={{0,2},{1,3},{2,0},{3,1},{4,6},{5,7},{6,4},{7,5},{8,10},{9,11},{10,... | collective-permute-start | bytes 3145736 | tf_op jit(solution)/shard_map/ppermute | solution.py:551
  373.0 38.7 %collective-permute-start.33 = (bf16[256,2048]{1,0:T(8,128)(2,1)}, bf16[256,2048]{1,0:T(8,128)(2,1)S(1)}, u32[]{:S(2)}, u32[]{:S(2)}) collective-permute-start(bf16[256,2048]{1,0:T(8,128)(2,1)} %get-tuple-element.207.refs_12_.refs_2_.refs_3_), channel_id=1, source_target_pairs={{0,1},{1,0},{2,3},{3,2},{4,5},{5,4},{6,7},{7,6},{8,9},{9,8},{10,11... | collective-permute-start | bytes 3145736 | tf_op jit(solution)/shard_map/ppermute | solution.py:551
  373.8 37.9 %collective-permute-start.34 = (bf16[256,2048]{1,0:T(8,128)(2,1)}, bf16[256,2048]{1,0:T(8,128)(2,1)}, u32[]{:S(2)}, u32[]{:S(2)}) collective-permute-start(bf16[256,2048]{1,0:T(8,128)(2,1)} %get-tuple-element.207.refs_12_.refs_2_.refs_3_), channel_id=1, source_target_pairs={{0,2},{1,3},{2,0},{3,1},{4,6},{5,7},{6,4},{7,5},{8,10},{9,11},{10,... | collective-permute-start | bytes 3145736 | tf_op jit(solution)/shard_map/ppermute | solution.py:551
  414.9 292.7 %all-reduce.2.cloned.1.call-start = ((), (), s32[]{:S(2)}) async-start(), calls=%async_computation | async-start | bytes 11534336 | tf_op jit(solution)/shard_map/psum | solution.py:2187
  498.2 434.5 %all-gather.4.cloned.1.call-start = ((), (), s32[]{:S(2)}) async-start(), calls=%async_computation.1 | async-start | bytes 1081344 | tf_op jit(solution)/shard_map/all_gather | solution.py:2240
  510.5 65.3 %collective-permute-start.47 = (bf16[5632,128]{1,0:T(8,128)(2,1)}, bf16[5632,128]{1,0:T(8,128)(2,1)}, u32[]{:S(2)}, u32[]{:S(2)}) collective-permute-start(bf16[5632,128]{1,0:T(8,128)(2,1)} %line_step.11.refs_13_), channel_id=1, source_target_pairs={{0,8},{24,16},{8,0},{16,24},{1,9},{25,17},{9,1},{17,25},{2,10},{26... | collective-permute-start | bytes 4325384 | tf_op jit(solution)/shard_map/ppermute | solution.py:1954
  536.5 44.3 %collective-permute-start.45 = (bf16[128,2048]{1,0:T(8,128)(2,1)}, bf16[128,2048]{1,0:T(8,128)(2,1)S(1)}, u32[]{:S(2)}, u32[]{:S(2)}) collective-permute-start(bf16[128,2048]{1,0:T(8,128)(2,1)} %get-tuple-element.233.refs_4_), channel_id=1, source_target_pairs={{0,2},{1,3},{2,0},{3,1},{4,6},{5,7},{6,4},{7,5},{8,10},{9,11},{10,... | collective-permute-start | bytes 1572872 | tf_op jit(solution)/shard_map/ppermute | solution.py:551
  537.8 44.8 %collective-permute-start.46 = (bf16[128,2048]{1,0:T(8,128)(2,1)}, bf16[128,2048]{1,0:T(8,128)(2,1)S(1)}, u32[]{:S(2)}, u32[]{:S(2)}) collective-permute-start(bf16[128,2048]{1,0:T(8,128)(2,1)} %get-tuple-element.234), channel_id=1, source_target_pairs={{0,1},{1,0},{2,3},{3,2},{4,5},{5,4},{6,7},{7,6},{8,9},{9,8},{10,11... | collective-permute-start | bytes 1572872 | tf_op jit(solution)/shard_map/ppermute | solution.py:551
  552.3 88.2 %collective-permute-start.52 = (bf16[256,2048]{1,0:T(8,128)(2,1)}, bf16[256,2048]{1,0:T(8,128)(2,1)}, u32[]{:S(2)}, u32[]{:S(2)}) collective-permute-start(bf16[256,2048]{1,0:T(8,128)(2,1)} %get-tuple-element.236.refs_6_), channel_id=1, source_target_pairs={{0,1},{1,0},{2,3},{3,2},{4,5},{5,4},{6,7},{7,6},{8,9},{9,8},{10,11... | collective-permute-start | bytes 3145736 | tf_op jit(solution)/shard_map/ppermute | solution.py:551
  553.4 87.0 %collective-permute-start.53 = (bf16[256,2048]{1,0:T(8,128)(2,1)}, bf16[256,2048]{1,0:T(8,128)(2,1)}, u32[]{:S(2)}, u32[]{:S(2)}) collective-permute-start(bf16[256,2048]{1,0:T(8,128)(2,1)} %get-tuple-element.243), channel_id=1, source_target_pairs={{0,2},{1,3},{2,0},{3,1},{4,6},{5,7},{6,4},{7,5},{8,10},{9,11},{10,... | collective-permute-start | bytes 3145736 | tf_op jit(solution)/shard_map/ppermute | solution.py:551
  580.5 54.2 %collective-permute-start.48 = (bf16[5632,128]{1,0:T(8,128)(2,1)}, bf16[5632,128]{1,0:T(8,128)(2,1)}, u32[]{:S(2)}, u32[]{:S(2)}) collective-permute-start(bf16[5632,128]{1,0:T(8,128)(2,1)} %get-tuple-element.237.refs_13_), channel_id=1, source_target_pairs={{0,8},{24,16},{8,0},{16,24},{1,9},{25,17},{9,1},{17,25},{2,10},{26... | collective-permute-start | bytes 4325384 | tf_op jit(solution)/shard_map/ppermute | solution.py:1954
  580.9 53.8 %collective-permute-start.49 = (bf16[5632,128]{1,0:T(8,128)(2,1)}, bf16[5632,128]{1,0:T(8,128)(2,1)}, u32[]{:S(2)}, u32[]{:S(2)}) collective-permute-start(bf16[5632,128]{1,0:T(8,128)(2,1)} %get-tuple-element.239.refs_6_), channel_id=1, source_target_pairs={{8,16},{16,8},{9,17},{17,9},{10,18},{18,10},{11,19},{19,11},{12,20... | collective-permute-start | bytes 4325384 | tf_op jit(solution)/shard_map/ppermute | solution.py:1956
  639.6 96.3 %collective-permute-start.50 = (bf16[5632,128]{1,0:T(8,128)(2,1)}, bf16[5632,128]{1,0:T(8,128)(2,1)}, u32[]{:S(2)}, u32[]{:S(2)}) collective-permute-start(bf16[5632,128]{1,0:T(8,128)(2,1)} %get-tuple-element.240.refs_4_.refs_9_), channel_id=1, source_target_pairs={{0,8},{24,16},{8,0},{16,24},{1,9},{25,17},{9,1},{17,25},{2,10},{26... | collective-permute-start | bytes 4325384 | tf_op jit(solution)/shard_map/ppermute | solution.py:1954
  643.4 84.9 %collective-permute-start.54 = (bf16[128,2048]{1,0:T(8,128)(2,1)}, bf16[128,2048]{1,0:T(8,128)(2,1)}, u32[]{:S(2)}, u32[]{:S(2)}) collective-permute-start(bf16[128,2048]{1,0:T(8,128)(2,1)} %get-tuple-element.246.refs_5_), channel_id=1, source_target_pairs={{0,1},{1,0},{2,3},{3,2},{4,5},{5,4},{6,7},{7,6},{8,9},{9,8},{10,11... | collective-permute-start | bytes 1572872 | tf_op jit(solution)/shard_map/ppermute | solution.py:551
  645.1 83.2 %collective-permute-start.55 = (bf16[128,2048]{1,0:T(8,128)(2,1)}, bf16[128,2048]{1,0:T(8,128)(2,1)}, u32[]{:S(2)}, u32[]{:S(2)}) collective-permute-start(bf16[128,2048]{1,0:T(8,128)(2,1)} %get-tuple-element.247), channel_id=1, source_target_pairs={{0,2},{1,3},{2,0},{3,1},{4,6},{5,7},{6,4},{7,5},{8,10},{9,11},{10,... | collective-permute-start | bytes 1572872 | tf_op jit(solution)/shard_map/ppermute | solution.py:551
  646.6 89.3 %collective-permute-start.51 = (bf16[5632,128]{1,0:T(8,128)(2,1)}, bf16[5632,128]{1,0:T(8,128)(2,1)}, u32[]{:S(2)}, u32[]{:S(2)}) collective-permute-start(bf16[5632,128]{1,0:T(8,128)(2,1)} %get-tuple-element.241.refs_6_), channel_id=1, source_target_pairs={{8,16},{16,8},{9,17},{17,9},{10,18},{18,10},{11,19},{19,11},{12,20... | collective-permute-start | bytes 4325384 | tf_op jit(solution)/shard_map/ppermute | solution.py:1956
  788.3 59.3 %collective-permute-start.72 = (bf16[11264,128]{1,0:T(8,128)(2,1)}, bf16[11264,128]{1,0:T(8,128)(2,1)}, u32[]{:S(2)}, u32[]{:S(2)}) collective-permute-start(bf16[11264,128]{1,0:T(8,128)(2,1)} %get-tuple-element.268), channel_id=1, source_target_pairs={{0,4},{4,0},{1,5},{5,1},{2,6},{6,2},{3,7},{7,3},{8,12},{12,8},{9,1... | collective-permute-start | bytes 8650760 | tf_op jit(solution)/shard_map/ppermute | solution.py:2164
  788.3 40.6 %collective-permute-start.67 = (bf16[4096,128]{1,0:T(8,128)(2,1)}, bf16[4096,128]{1,0:T(8,128)(2,1)}, u32[]{:S(2)}, u32[]{:S(2)}) collective-permute-start(bf16[4096,128]{1,0:T(8,128)(2,1)} %bitcast.59), channel_id=1, source_target_pairs={{0,4},{4,0},{1,5},{5,1},{2,6},{6,2},{3,7},{7,3},{8,12},{12,8},{9,1... | collective-permute-start | bytes 3145736 | tf_op jit(solution)/shard_map/ppermute | solution.py:2222
  847.5 37.3 %collective-permute-start.68 = (bf16[256,2048]{1,0:T(8,128)(2,1)}, bf16[256,2048]{1,0:T(8,128)(2,1)}, u32[]{:S(2)}, u32[]{:S(2)}) collective-permute-start(bf16[256,2048]{1,0:T(8,128)(2,1)} %input_grad.3.refs_11_.refs_1_), channel_id=1, source_target_pairs={{0,1},{1,0},{2,3},{3,2},{4,5},{5,4},{6,7},{7,6},{8,9},{9,8},{10,11... | collective-permute-start | bytes 3145736 | tf_op jit(solution)/shard_map/ppermute | solution.py:551
  847.6 37.3 %collective-permute-start.69 = (bf16[256,2048]{1,0:T(8,128)(2,1)}, bf16[256,2048]{1,0:T(8,128)(2,1)}, u32[]{:S(2)}, u32[]{:S(2)}) collective-permute-start(bf16[256,2048]{1,0:T(8,128)(2,1)} %input_grad.3.refs_11_.refs_1_), channel_id=1, source_target_pairs={{0,2},{1,3},{2,0},{3,1},{4,6},{5,7},{6,4},{7,5},{8,10},{9,11},{10,... | collective-permute-start | bytes 3145736 | tf_op jit(solution)/shard_map/ppermute | solution.py:551
  (104 other events, 1834.0 us)
Sparse Core Ops, SparseCore 0:
  498.3 209.1 all-reduce.1
Sparse Core Ops, SparseCore 1:
  831.3 55.3 all-gather.3

commit v5 on v4

--- a/solution.py
+++ b/solution.py
@@ -793,13 +793,12 @@
 
 ORDER = ((1, 0), (3, 0), (2, 1), (3, 1), (1, 1), (2, 0), (0, 0), (0, 1))
 CORES = ((0, 1), (1, 0))
-DECLARED_FLOPS = 1e9
+DECLARED_FLOPS = 1e10
 MICROS = {
-    "attn_fwd": 1050, "split": 2, "ow_join": 4, "relay": 0.05, "out_norm": 21,
-    "middle_sum": 0.6, "resid_two": 25, "norm_two": 15, "grad_columns": 1000, "grad_plain_columns": 0.57,
-    "grad_plain": 3.8, "line_step": 5, "grad_rows": 1050, "attn_bwd": 1200, "norm_one_back": 30,
-    "input_back": 70, "input_grad": 5, "grad_out": 0.55, "place": 5, "widen": 50,
-    "cast": 9, "total_sum": 1,
+    "attn_fwd": 21, "split": 2, "ow_join": 4, "relay": 1, "out_norm": 21, "middle_sum": 3, "resid_two": 5,
+    "norm_two": 15, "grad_columns": 20, "grad_plain_columns": 19, "grad_plain": 19, "line_step": 5, "grad_rows": 21,
+    "attn_bwd": 24, "norm_one_back": 6, "input_back": 14, "input_grad": 5, "grad_out": 11, "place": 5, "widen": 10,
+    "cast": 9, "total_sum": 2,
 }
 
 

time: 1010 us -> 952 us (0.943)
  waiting for transfers between devices: 248 us -> 178 us
  starting transfers between devices: 103 us -> 122 us
    psum x1, waiting for transfers between devices: 59.2 us -> 0.01 us  [plane_body(): down_sum = lax.psum(down_update, ('obj', 'dp'))]
    ppermute x10, starting transfers between devices: 24.9 us -> 44.5 us  [advance(): lax.ppermute(self.sent, 'obj', [(0, 1), (3, 2), (1, 0), (2, 3)])]
  transfers between devices with their start and end apart: 89 -> 89, of which waited for: 30 -> 27; matrix products, arithmetic and copies ran while one was open for 1% -> 2% of each run, Pallas kernels for 57% -> 60%
where the time goes in v5:
time: 952 us; the launch traced here: 943 us
  Pallas kernels  600 us (63%)
  waiting for transfers between devices  178 us (19%)
  starting transfers between devices  122 us (13%)
  between operations  18.9 us (2%)
  local copies, waits for them, and re-layouts  18.4 us (2%)
    pallas_call x64, Pallas kernels, call(): pl.pallas_call(wrapped, grid_spec=grid_spec, out_shape=[jax.ShapeDtypeStr...  600 us
    ppermute x10, waiting for transfers between devices, advance(): lax.ppermute(self.sent, 'obj', [(0, 1), (3, 2), (1, 0), (2, 3)])  108 us
    ppermute x60, starting transfers between devices, swap(): return lax.ppermute(array, 'tensor', [(i, i ^ bit) for i in range(ways)])  64.3 us
    ppermute x60, waiting for transfers between devices, swap(): return lax.ppermute(array, 'tensor', [(i, i ^ bit) for i in range(ways)])  63 us
    ppermute x10, starting transfers between devices, advance(): lax.ppermute(self.sent, 'obj', [(0, 1), (3, 2), (1, 0), (2, 3)])  44.5 us
  transfers between devices with their start and end apart: 89, of which 27 were waited for; matrix products, arithmetic and copies ran while one was open for 2% of the time, Pallas kernels for 60%

profile of v5, /device:TPU:0, one launch (start us, length us, event | category | flops | bytes accessed | tf_op | source)
XLA Modules:
  0.0 943.1 jit_solution(11942535043665267491)
XLA Ops:
  22.4 20.9 %attn_fwd.2 = (bf16[1024,1536]{1,0:T(8,128)(2,1)}, bf16[1024,512]{1,0:T(8,128)(2,1)}, f32[4,1,1024]{2,1,0:T(1,128)}) custom-call(s32[4]{0:T(128)} %add_add_fusion.1.refs_0_, bf16[2,1024,2048]{2,1,0:T(8,128)(2,1)} %refs_2_.11, bf16[2048,1536]{1,0:T(8,128)(2,1)} %refs_3_.17, f32[1024,128]{1,0:T(8,128)} %constant.40.clone.refs_3_.refs_9_, ...), custom_call_target="tpu_custom_call" | custom-call | flops 210000003072 | bytes 1000000 | tf_op jit(solution)/shard_map/attn_fwd/pallas_call | solution.py:838
  53.1 21.0 %attn_fwd.3 = (bf16[1024,1536]{1,0:T(8,128)(2,1)}, bf16[1024,512]{1,0:T(8,128)(2,1)}, f32[4,1,1024]{2,1,0:T(1,128)}) custom-call(s32[4]{0:T(128)} %add_add_fusion.refs_0_, bf16[2,1024,2048]{2,1,0:T(8,128)(2,1)} %refs_2_.11, bf16[2048,1536]{1,0:T(8,128)(2,1)} %refs_3_.17, f32[1024,128]{1,0:T(8,128)} %constant.40.clone.refs_3_.refs_9_, ...), custom_call_target="tpu_custom_call" | custom-call | flops 210000003072 | bytes 1000000 | tf_op jit(solution)/shard_map/attn_fwd/pallas_call | solution.py:838
  105.2 21.1 %out_norm.2 = (bf16[1024,2048]{1,0:T(8,128)(2,1)}, f32[256,2048]{1,0:T(8,128)}, f32[256,128]{1,0:T(8,128)}) custom-call(s32[4]{0:T(128)} %add_add_fusion.1.refs_0_, s32[8]{0:T(128)} %stack.54.refs_1_.refs_0_, bf16[1024,512]{1,0:T(8,128)(2,1)} %get-tuple-element.150.refs_2_.refs_7_.refs_1_, ...), custom_call_target="tpu_custom_call" | custom-call | flops 210000003072 | bytes 1000000 | tf_op jit(solution)/shard_map/out_norm/pallas_call | solution.py:838
  132.4 30.1 %ffn_fwd.3 = (bf16[256,2048]{1,0:T(8,128)(2,1)}, bf16[256,2048]{1,0:T(8,128)(2,1)}, bf16[128,2048]{1,0:T(8,128)(2,1)}, bf16[128,2048]{1,0:T(8,128)(2,1)}, bf16[2...) custom-call(bf16[1024,2048]{1,0:T(8,128)(2,1)} %get-tuple-element.161, ...), custom_call_target="tpu_custom_call" | custom-call | flops 359999995904 | bytes 1000000 | tf_op jit(solution)/shard_map/ffn_fwd/pallas_call | solution.py:838
  164.9 21.4 %out_norm.3 = (bf16[1024,2048]{1,0:T(8,128)(2,1)}, f32[256,2048]{1,0:T(8,128)}, f32[256,128]{1,0:T(8,128)}) custom-call(s32[4]{0:T(128)} %add_add_fusion.refs_0_, s32[8]{0:T(128)} %stack.54.refs_1_.refs_0_, bf16[1024,512]{1,0:T(8,128)(2,1)} %get-tuple-element.159.refs_2_.refs_7_, bf16[1024,512]{1,0:T(8,128)(2,1)} %collective-permute-done.8.refs_0_.refs_3_.refs_8_, ...), custom_call_target="tpu_custom_call" | custom-call | flops 210000003072 | bytes 1000000 | tf_op jit(solution)/shard_map/out_norm/pallas_call | solution.py:838
  191.4 17.6 %ffn_fwd.4 = (bf16[256,2048]{1,0:T(8,128)(2,1)}, bf16[256,2048]{1,0:T(8,128)(2,1)}, bf16[1024,1408]{1,0:T(8,128)(2,1)}, bf16[1024,1408]{1,0:T(8,128)(2,1)}, bf16[1024,1408]{1,0:T(8,128)(2,1)}) custom-call(bf16[1024,2048]{1,0:T(8,128)(2,1)} %get-tuple-element.165.refs_4_.refs_0_.refs_2_, bf16[2048,1408]{1,0:T(8,128)(2,1)} %refs_4_.7, ...), custom_call_target="tpu_custom_call" | custom-call | flops 179999997952 | bytes 1000000 | tf_op jit(solution)/shard_map/ffn_fwd/pallas_call | solution.py:838
  216.2 17.8 %ffn_fwd.5 = (bf16[128,2048]{1,0:T(8,128)(2,1)}, bf16[128,2048]{1,0:T(8,128)(2,1)}, bf16[256,2048]{1,0:T(8,128)(2,1)}, bf16[256,2048]{1,0:T(8,128)(2,1)}, bf16[2...) custom-call(bf16[1024,2048]{1,0:T(8,128)(2,1)} %get-tuple-element.16, ...), custom_call_target="tpu_custom_call", output_to_operand_aliasing={{5}: (4, {}), {6}: (5, {}), {7}: (6, {}), {3}: (7, {}), {4}... | custom-call | flops 179999997952 | bytes 1000000 | tf_op jit(solution)/shard_map/ffn_fwd/pallas_call | solution.py:838
  254.0 14.5 %norm_two.2 = (bf16[2,1024,2048]{2,1,0:T(8,128)(2,1)}, f32[2,2048]{1,0:T(2,128)}, bf16[1024,2048]{1,0:T(8,128)(2,1)}) custom-call(s32[4]{0:T(128)} %add_add_fusion.1.refs_0_, s32[8]{0:T(128)} %stack.54.refs_1_.refs_0_, f32[1]{0:T(128)} %get-tuple-element.299.refs_2_, bf16[256,2048]{1,0:T(8,128)(2,1)} %resid_two.2.refs_9_.refs_3_, ...), custom_call_target="tpu_custom_call" | custom-call | flops 149999992832 | bytes 1000000 | tf_op jit(solution)/shard_map/norm_two/pallas_call | solution.py:838
  268.5 19.1 %ffn_bwd.3 = (bf16[256,2048]{1,0:T(8,128)(2,1)}, bf16[256,2048]{1,0:T(8,128)(2,1)}, bf16[1024,1408]{1,0:T(8,128)(2,1)}, bf16[1024,1408]{1,0:T(8,128)(2,1)}) custom-call(bf16[1024,2048]{1,0:T(8,128)(2,1)} %get-tuple-element.188.refs_0_.refs_5_.refs_2_, bf16[1024,1408]{1,0:T(8,128)(2,1)} %get-tuple-element.189.refs_1_, ...), custom_call_target="tpu_custom_call" | custom-call | flops 179999997952 | bytes 1000000 | tf_op jit(solution)/shard_map/ffn_bwd/pallas_call | solution.py:838
  294.7 19.3 %ffn_bwd.4 = (bf16[128,2048]{1,0:T(8,128)(2,1)}, bf16[128,2048]{1,0:T(8,128)(2,1)}, bf16[256,2048]{1,0:T(8,128)(2,1)}, bf16[1024,1408]{1,0:T(8,128)(2,1)}, bf16[1024,1408]{1,0:T(8,128)(2,1)}) custom-call(bf16[1024,2048]{1,0:T(8,128)(2,1)} %get-tuple-element.188.refs_0_.refs_5_.refs_2_, ...), custom_call_target="tpu_custom_call", output_to_operand_aliasing={{3}: (6, {}), {4}: (7, {})} | custom-call | flops 179999997952 | bytes 1000000 | tf_op jit(solution)/shard_map/ffn_bwd/pallas_call | solution.py:838
  330.1 19.3 %collective-permute-done.25.refs_0_.refs_4_ = bf16[256,2048]{1,0:T(8,128)(2,1)S(1)} collective-permute-done((bf16[256,2048]{1,0:T(8,128)(2,1)}, bf16[256,2048]{1,0:T(8,128)(2,1)S(1)}, u32[]{:S(2)}, u32[]{:S(2)}) %collective-permute-start.25) | collective-permute-done | bytes 1048608 | tf_op jit(solution)/shard_map/ppermute | solution.py:551
  373.2 14.5 %norm_two.3 = (bf16[2,1024,2048]{2,1,0:T(8,128)(2,1)}, f32[2,2048]{1,0:T(2,128)}, bf16[1024,2048]{1,0:T(8,128)(2,1)}) custom-call(s32[4]{0:T(128)} %add_add_fusion.refs_0_, s32[8]{0:T(128)} %stack.54.refs_1_.refs_0_, f32[1]{0:T(128)} %get-tuple-element.300.refs_2_, bf16[256,2048]{1,0:T(8,128)(2,1)} %resid_two.3.refs_4_.refs_3_, ...), custom_call_target="tpu_custom_call", output_to_operand_aliasing={{0}: (11, {})} | custom-call | flops 149999992832 | bytes 1000000 | tf_op jit(solution)/shard_map/norm_two/pallas_call | solution.py:838
  387.7 19.1 %grad_plain_columns.1.refs_2_ = bf16[1408,2048]{1,0:T(8,128)(2,1)} custom-call(bf16[1024,1408]{1,0:T(8,128)(2,1)} %get-tuple-element.212.refs_0_, bf16[1024,1408]{1,0:T(8,128)(2,1)} %get-tuple-element.213.refs_1_, bf16[1024,2048]{1,0:T(8,128)(2,1)} %get-tuple-element.188.refs_0_.refs_5_.refs_2_, ...), custom_call_target="tpu_custom_call" | custom-call | flops 190000005120 | bytes 1000000 | tf_op jit(solution)/shard_map/grad_plain_columns/pallas_call | solution.py:838
  413.1 32.7 %ffn_bwd.5 = (bf16[256,2048]{1,0:T(8,128)(2,1)}, bf16[256,2048]{1,0:T(8,128)(2,1)}, bf16[128,2048]{1,0:T(8,128)(2,1)}, bf16[128,2048]{1,0:T(8,128)(2,1)}, bf16[2...) custom-call(bf16[1024,2048]{1,0:T(8,128)(2,1)} %get-tuple-element.209.refs_3_.refs_0_.refs_5_, ...), custom_call_target="tpu_custom_call" | custom-call | flops 359999995904 | bytes 1000000 | tf_op jit(solution)/shard_map/ffn_bwd/pallas_call | solution.py:838
  447.0 20.6 %grad_rows.3 = (bf16[11,1024,128]{2,1,0:T(8,128)(2,1)}, bf16[11,1024,128]{2,1,0:T(8,128)(2,1)}) custom-call(s32[4]{0:T(128)} %add_add_fusion.refs_0_, bf16[1024,2048]{1,0:T(8,128)(2,1)} %get-tuple-element.161.refs_2_.refs_0_.refs_1_, bf16[1024,2048]{1,0:T(8,128)(2,1)} %get-tuple-element.165.refs_4_.refs_0_.refs_2_, ...), custom_call_target="tpu_custom_call" | custom-call | flops 210000003072 | bytes 1000000 | tf_op jit(solution)/shard_map/grad_rows/pallas_call | solution.py:838
  473.6 20.7 %grad_rows.4 = (bf16[11,1024,128]{2,1,0:T(8,128)(2,1)}, bf16[11,1024,128]{2,1,0:T(8,128)(2,1)}) custom-call(s32[4]{0:T(128)} %add_add_fusion.refs_0_, bf16[1024,2048]{1,0:T(8,128)(2,1)} %get-tuple-element.161.refs_2_.refs_0_.refs_1_, bf16[1024,2048]{1,0:T(8,128)(2,1)} %get-tuple-element.165.refs_4_.refs_0_.refs_2_, ...), custom_call_target="tpu_custom_call" | custom-call | flops 210000003072 | bytes 1000000 | tf_op jit(solution)/shard_map/grad_rows/pallas_call | solution.py:838
  506.9 23.9 %attn_bwd.2.refs_2_.refs_1_.refs_3_ = bf16[1024,1536]{1,0:T(8,128)(2,1)} custom-call(s32[4]{0:T(128)} %add_add_fusion.1.refs_0_, bf16[1024,1536]{1,0:T(8,128)(2,1)} %get-tuple-element.151.refs_2_.refs_1_, bf16[256,2048]{1,0:T(8,128)(2,1)} %get-tuple-element.207.refs_12_.refs_2_.refs_3_, bf16[256,2048]{1,0:T(8,128)(2,1)} %collective-permute-done.33.refs_0_.refs_3_.refs_4_, ...), custom_call_target="tpu_custom_call" | custom-call | flops 240000008192 | bytes 1000000 | tf_op jit(solution)/shard_map/attn_bwd/pallas_call | solution.py:838
  550.9 20.7 %collective-permute-done.47.refs_5_ = bf16[5632,128]{1,0:T(8,128)(2,1)} collective-permute-done((bf16[5632,128]{1,0:T(8,128)(2,1)}, bf16[5632,128]{1,0:T(8,128)(2,1)}, u32[]{:S(2)}, u32[]{:S(2)}) %collective-permute-start.47) | collective-permute-done | bytes 1441824 | tf_op jit(solution)/shard_map/ppermute | solution.py:1953
  579.5 23.9 %attn_bwd.3.refs_8_.refs_4_.refs_1_.refs_2_ = bf16[1024,1536]{1,0:T(8,128)(2,1)} custom-call(s32[4]{0:T(128)} %add_add_fusion.refs_0_, bf16[1024,1536]{1,0:T(8,128)(2,1)} %get-tuple-element.155.refs_4_.refs_1_, bf16[256,2048]{1,0:T(8,128)(2,1)} %get-tuple-element.230.refs_3_.refs_2_.refs_8_, ...), custom_call_target="tpu_custom_call" | custom-call | flops 240000008192 | bytes 1000000 | tf_op jit(solution)/shard_map/attn_bwd/pallas_call | solution.py:838
  629.8 21.0 %grad_rows.5 = (bf16[12,1024,128]{2,1,0:T(8,128)(2,1)}, bf16[12,1024,128]{2,1,0:T(8,128)(2,1)}) custom-call(s32[4]{0:T(128)} %add_add_fusion.refs_0_, bf16[2,1024,2048]{2,1,0:T(8,128)(2,1)} %refs_2_.11, bf16[2,1024,2048]{2,1,0:T(8,128)(2,1)} %refs_2_.11, bf16[1024,1536]{1,0:T(8,128)(2,1)} %attn_bwd.2.refs_2_.refs_1_.refs_3_, ...), custom_call_target="tpu_custom_call" | custom-call | flops 210000003072 | bytes 1000000 | tf_op jit(solution)/shard_map/grad_rows/pallas_call | solution.py:838
  662.6 13.8 %input_back.3 = (bf16[256,2048]{1,0:T(8,128)(2,1)}, bf16[256,2048]{1,0:T(8,128)(2,1)}, bf16[128,2048]{1,0:T(8,128)(2,1)}, bf16[128,2048]{1,0:T(8,128)(2,1)}, bf16[256,2048]{1,0:T(8,128)(2,1)}) custom-call(s32[8]{0:T(128)} %stack.54.refs_1_.refs_0_, bf16[1024,1536]{1,0:T(8,128)(2,1)} %attn_bwd.3.refs_8_.refs_4_.refs_1_.refs_2_, ...), custom_call_target="tpu_custom_call" | custom-call | flops 140000002048 | bytes 1000000 | tf_op jit(solution)/shard_map/input_back/pallas_call | solution.py:838
  696.5 15.1 %collective-permute-done.59.refs_5_.refs_8_ = bf16[5632,128]{1,0:T(8,128)(2,1)} collective-permute-done((bf16[5632,128]{1,0:T(8,128)(2,1)S(1)}, bf16[5632,128]{1,0:T(8,128)(2,1)}, u32[]{:S(2)}, u32[]{:S(2)}) %collective-permute-start.59) | collective-permute-done | bytes 1441824 | tf_op jit(solution)/shard_map/ppermute | solution.py:1953
  773.1 17.9 %collective-permute-done.73.refs_5_.refs_8_ = bf16[5632,128]{1,0:T(8,128)(2,1)S(1)} collective-permute-done((bf16[5632,128]{1,0:T(8,128)(2,1)}, bf16[5632,128]{1,0:T(8,128)(2,1)S(1)}, u32[]{:S(2)}, u32[]{:S(2)}) %collective-permute-start.73) | collective-permute-done | bytes 1441824 | tf_op jit(solution)/shard_map/ppermute | solution.py:1953
  875.2 17.2 %collective-permute-done.83.refs_3_ = bf16[4096,128]{1,0:T(8,128)(2,1)} collective-permute-done((bf16[4096,128]{1,0:T(8,128)(2,1)}, bf16[4096,128]{1,0:T(8,128)(2,1)}, u32[]{:S(2)}, u32[]{:S(2)}) %collective-permute-start.83) | collective-permute-done | bytes 1048608 | tf_op jit(solution)/shard_map/ppermute | solution.py:1953
  (293 shorter events, 441.0 us)
Async XLA Ops:
  10.3 37.1 %collective-permute-start.2 = (bf16[256,2048]{1,0:T(8,128)(2,1)}, bf16[256,2048]{1,0:T(8,128)(2,1)}, u32[]{:S(2)}, u32[]{:S(2)}) collective-permute-start(bf16[256,2048]{1,0:T(8,128)(2,1)} %constant_dynamic-slice_fusion), channel_id=1, source_target_pairs={{0,1},{1,0},{2,3},{3,2},{4,5},{5,4},{6,7},{7,6},{8,9},{9,8},{10,11... | collective-permute-start | bytes 3145736 | tf_op jit(solution)/shard_map/ppermute | solution.py:551
  252.4 37.8 %collective-permute-start.21 = (bf16[256,2048]{1,0:T(8,128)(2,1)}, bf16[256,2048]{1,0:T(8,128)(2,1)}, u32[]{:S(2)}, u32[]{:S(2)}) collective-permute-start(bf16[256,2048]{1,0:T(8,128)(2,1)} %get-tuple-element.184), channel_id=1, source_target_pairs={{0,1},{1,0},{2,3},{3,2},{4,5},{5,4},{6,7},{7,6},{8,9},{9,8},{10,11... | collective-permute-start | bytes 3145736 | tf_op jit(solution)/shard_map/ppermute | solution.py:551
  253.0 37.2 %collective-permute-start.22 = (bf16[256,2048]{1,0:T(8,128)(2,1)}, bf16[256,2048]{1,0:T(8,128)(2,1)}, u32[]{:S(2)}, u32[]{:S(2)}) collective-permute-start(bf16[256,2048]{1,0:T(8,128)(2,1)} %get-tuple-element.185), channel_id=1, source_target_pairs={{0,2},{1,3},{2,0},{3,1},{4,6},{5,7},{6,4},{7,5},{8,10},{9,11},{10,... | collective-permute-start | bytes 3145736 | tf_op jit(solution)/shard_map/ppermute | solution.py:551
  287.6 37.0 %collective-permute-start.27 = (bf16[256,2048]{1,0:T(8,128)(2,1)}, bf16[256,2048]{1,0:T(8,128)(2,1)}, u32[]{:S(2)}, u32[]{:S(2)}) collective-permute-start(bf16[256,2048]{1,0:T(8,128)(2,1)} %get-tuple-element.192.refs_4_), channel_id=1, source_target_pairs={{0,1},{1,0},{2,3},{3,2},{4,5},{5,4},{6,7},{7,6},{8,9},{9,8},{10,11... | collective-permute-start | bytes 3145736 | tf_op jit(solution)/shard_map/ppermute | solution.py:551
  367.6 39.8 %collective-permute-start.33 = (bf16[256,2048]{1,0:T(8,128)(2,1)}, bf16[256,2048]{1,0:T(8,128)(2,1)}, u32[]{:S(2)}, u32[]{:S(2)}) collective-permute-start(bf16[256,2048]{1,0:T(8,128)(2,1)} %get-tuple-element.207.refs_12_.refs_2_.refs_3_), channel_id=1, source_target_pairs={{0,1},{1,0},{2,3},{3,2},{4,5},{5,4},{6,7},{7,6},{8,9},{9,8},{10,11... | collective-permute-start | bytes 3145736 | tf_op jit(solution)/shard_map/ppermute | solution.py:551
  368.9 38.5 %collective-permute-start.34 = (bf16[256,2048]{1,0:T(8,128)(2,1)}, bf16[256,2048]{1,0:T(8,128)(2,1)}, u32[]{:S(2)}, u32[]{:S(2)}) collective-permute-start(bf16[256,2048]{1,0:T(8,128)(2,1)} %get-tuple-element.207.refs_12_.refs_2_.refs_3_), channel_id=1, source_target_pairs={{0,2},{1,3},{2,0},{3,1},{4,6},{5,7},{6,4},{7,5},{8,10},{9,11},{10,... | collective-permute-start | bytes 3145736 | tf_op jit(solution)/shard_map/ppermute | solution.py:551
  409.7 220.1 %all-reduce.2.cloned.1.call-start = ((), (), s32[]{:S(2)}) async-start(), calls=%async_computation | async-start | bytes 11534336 | tf_op jit(solution)/shard_map/psum | solution.py:2186
  410.4 462.7 %all-gather.4.cloned.1.call-start = ((), (), s32[]{:S(2)}) async-start(), calls=%async_computation.1 | async-start | bytes 1081344 | tf_op jit(solution)/shard_map/all_gather | solution.py:2239
  410.4 36.5 %collective-permute-start.37 = (bf16[128,2048]{1,0:T(8,128)(2,1)}, bf16[128,2048]{1,0:T(8,128)(2,1)}, u32[]{:S(2)}, u32[]{:S(2)}) collective-permute-start(bf16[128,2048]{1,0:T(8,128)(2,1)} %get-tuple-element.214.refs_6_), channel_id=1, source_target_pairs={{0,2},{1,3},{2,0},{3,1},{4,6},{5,7},{6,4},{7,5},{8,10},{9,11},{10,... | collective-permute-start | bytes 1572872 | tf_op jit(solution)/shard_map/ppermute | solution.py:551
  506.9 64.7 %collective-permute-start.47 = (bf16[5632,128]{1,0:T(8,128)(2,1)}, bf16[5632,128]{1,0:T(8,128)(2,1)}, u32[]{:S(2)}, u32[]{:S(2)}) collective-permute-start(bf16[5632,128]{1,0:T(8,128)(2,1)} %line_step.11.refs_13_), channel_id=1, source_target_pairs={{0,8},{24,16},{8,0},{16,24},{1,9},{25,17},{9,1},{17,25},{2,10},{26... | collective-permute-start | bytes 4325384 | tf_op jit(solution)/shard_map/ppermute | solution.py:1953
  549.6 72.8 %collective-permute-start.52 = (bf16[256,2048]{1,0:T(8,128)(2,1)}, bf16[256,2048]{1,0:T(8,128)(2,1)}, u32[]{:S(2)}, u32[]{:S(2)}) collective-permute-start(bf16[256,2048]{1,0:T(8,128)(2,1)} %get-tuple-element.236.refs_6_), channel_id=1, source_target_pairs={{0,1},{1,0},{2,3},{3,2},{4,5},{5,4},{6,7},{7,6},{8,9},{9,8},{10,11... | collective-permute-start | bytes 3145736 | tf_op jit(solution)/shard_map/ppermute | solution.py:551
  549.9 72.6 %collective-permute-start.53 = (bf16[256,2048]{1,0:T(8,128)(2,1)}, bf16[256,2048]{1,0:T(8,128)(2,1)}, u32[]{:S(2)}, u32[]{:S(2)}) collective-permute-start(bf16[256,2048]{1,0:T(8,128)(2,1)} %get-tuple-element.243), channel_id=1, source_target_pairs={{0,2},{1,3},{2,0},{3,1},{4,6},{5,7},{6,4},{7,5},{8,10},{9,11},{10,... | collective-permute-start | bytes 3145736 | tf_op jit(solution)/shard_map/ppermute | solution.py:551
  576.3 37.3 %collective-permute-start.48 = (bf16[5632,128]{1,0:T(8,128)(2,1)}, bf16[5632,128]{1,0:T(8,128)(2,1)}, u32[]{:S(2)}, u32[]{:S(2)}) collective-permute-start(bf16[5632,128]{1,0:T(8,128)(2,1)} %get-tuple-element.237.refs_13_), channel_id=1, source_target_pairs={{0,8},{24,16},{8,0},{16,24},{1,9},{25,17},{9,1},{17,25},{2,10},{26... | collective-permute-start | bytes 4325384 | tf_op jit(solution)/shard_map/ppermute | solution.py:1953
  576.9 36.7 %collective-permute-start.49 = (bf16[5632,128]{1,0:T(8,128)(2,1)}, bf16[5632,128]{1,0:T(8,128)(2,1)}, u32[]{:S(2)}, u32[]{:S(2)}) collective-permute-start(bf16[5632,128]{1,0:T(8,128)(2,1)} %get-tuple-element.239.refs_6_), channel_id=1, source_target_pairs={{8,16},{16,8},{9,17},{17,9},{10,18},{18,10},{11,19},{19,11},{12,20... | collective-permute-start | bytes 4325384 | tf_op jit(solution)/shard_map/ppermute | solution.py:1955
  618.6 38.2 %collective-permute-start.50 = (bf16[5632,128]{1,0:T(8,128)(2,1)}, bf16[5632,128]{1,0:T(8,128)(2,1)}, u32[]{:S(2)}, u32[]{:S(2)}) collective-permute-start(bf16[5632,128]{1,0:T(8,128)(2,1)} %get-tuple-element.240.refs_4_.refs_9_), channel_id=1, source_target_pairs={{0,8},{24,16},{8,0},{16,24},{1,9},{25,17},{9,1},{17,25},{2,10},{26... | collective-permute-start | bytes 4325384 | tf_op jit(solution)/shard_map/ppermute | solution.py:1953
  684.2 39.8 %collective-permute-start.56 = (bf16[256,2048]{1,0:T(8,128)(2,1)}, bf16[256,2048]{1,0:T(8,128)(2,1)}, u32[]{:S(2)}, u32[]{:S(2)}) collective-permute-start(bf16[256,2048]{1,0:T(8,128)(2,1)} %get-tuple-element.252.refs_13_), channel_id=1, source_target_pairs={{0,1},{1,0},{2,3},{3,2},{4,5},{5,4},{6,7},{7,6},{8,9},{9,8},{10,11... | collective-permute-start | bytes 3145736 | tf_op jit(solution)/shard_map/ppermute | solution.py:551
  684.9 39.1 %collective-permute-start.57 = (bf16[256,2048]{1,0:T(8,128)(2,1)}, bf16[256,2048]{1,0:T(8,128)(2,1)}, u32[]{:S(2)}, u32[]{:S(2)}) collective-permute-start(bf16[256,2048]{1,0:T(8,128)(2,1)} %get-tuple-element.253), channel_id=1, source_target_pairs={{0,2},{1,3},{2,0},{3,1},{4,6},{5,7},{6,4},{7,5},{8,10},{9,11},{10,... | collective-permute-start | bytes 3145736 | tf_op jit(solution)/shard_map/ppermute | solution.py:551
  724.0 36.5 %collective-permute-start.67 = (bf16[4096,128]{1,0:T(8,128)(2,1)}, bf16[4096,128]{1,0:T(8,128)(2,1)}, u32[]{:S(2)}, u32[]{:S(2)}) collective-permute-start(bf16[4096,128]{1,0:T(8,128)(2,1)} %bitcast.51), channel_id=1, source_target_pairs={{0,4},{4,0},{1,5},{5,1},{2,6},{6,2},{3,7},{7,3},{8,12},{12,8},{9,1... | collective-permute-start | bytes 3145736 | tf_op jit(solution)/shard_map/ppermute | solution.py:2221
  727.0 37.5 %collective-permute-start.63 = (bf16[128,2048]{1,0:T(8,128)(2,1)}, bf16[128,2048]{1,0:T(8,128)(2,1)}, u32[]{:S(2)}, u32[]{:S(2)}) collective-permute-start(bf16[128,2048]{1,0:T(8,128)(2,1)} %get-tuple-element.261.refs_1_), channel_id=1, source_target_pairs={{0,1},{1,0},{2,3},{3,2},{4,5},{5,4},{6,7},{7,6},{8,9},{9,8},{10,11... | collective-permute-start | bytes 1572872 | tf_op jit(solution)/shard_map/ppermute | solution.py:551
  727.7 37.5 %collective-permute-start.64 = (bf16[128,2048]{1,0:T(8,128)(2,1)}, bf16[128,2048]{1,0:T(8,128)(2,1)}, u32[]{:S(2)}, u32[]{:S(2)}) collective-permute-start(bf16[128,2048]{1,0:T(8,128)(2,1)} %get-tuple-element.262), channel_id=1, source_target_pairs={{0,2},{1,3},{2,0},{3,1},{4,6},{5,7},{6,4},{7,5},{8,10},{9,11},{10,... | collective-permute-start | bytes 1572872 | tf_op jit(solution)/shard_map/ppermute | solution.py:551
  764.4 45.3 %collective-permute-start.70 = (bf16[128,2048]{1,0:T(8,128)(2,1)}, bf16[128,2048]{1,0:T(8,128)(2,1)}, u32[]{:S(2)}, u32[]{:S(2)}) collective-permute-start(bf16[128,2048]{1,0:T(8,128)(2,1)} %get-tuple-element.266.refs_6_), channel_id=1, source_target_pairs={{0,2},{1,3},{2,0},{3,1},{4,6},{5,7},{6,4},{7,5},{8,10},{9,11},{10,... | collective-permute-start | bytes 1572872 | tf_op jit(solution)/shard_map/ppermute | solution.py:551
  769.9 46.8 %collective-permute-start.68 = (bf16[256,2048]{1,0:T(8,128)(2,1)}, bf16[256,2048]{1,0:T(8,128)(2,1)}, u32[]{:S(2)}, u32[]{:S(2)}) collective-permute-start(bf16[256,2048]{1,0:T(8,128)(2,1)} %input_grad.3.refs_11_.refs_1_), channel_id=1, source_target_pairs={{0,1},{1,0},{2,3},{3,2},{4,5},{5,4},{6,7},{7,6},{8,9},{9,8},{10,11... | collective-permute-start | bytes 3145736 | tf_op jit(solution)/shard_map/ppermute | solution.py:551
  771.7 44.9 %collective-permute-start.69 = (bf16[256,2048]{1,0:T(8,128)(2,1)}, bf16[256,2048]{1,0:T(8,128)(2,1)}, u32[]{:S(2)}, u32[]{:S(2)}) collective-permute-start(bf16[256,2048]{1,0:T(8,128)(2,1)} %input_grad.3.refs_11_.refs_1_), channel_id=1, source_target_pairs={{0,2},{1,3},{2,0},{3,1},{4,6},{5,7},{6,4},{7,5},{8,10},{9,11},{10,... | collective-permute-start | bytes 3145736 | tf_op jit(solution)/shard_map/ppermute | solution.py:551
  771.9 39.5 %collective-permute-start.71 = (bf16[128,2048]{1,0:T(8,128)(2,1)}, bf16[128,2048]{1,0:T(8,128)(2,1)}, u32[]{:S(2)}, u32[]{:S(2)}) collective-permute-start(bf16[128,2048]{1,0:T(8,128)(2,1)} %get-tuple-element.267), channel_id=1, source_target_pairs={{0,1},{1,0},{2,3},{3,2},{4,5},{5,4},{6,7},{7,6},{8,9},{9,8},{10,11... | collective-permute-start | bytes 1572872 | tf_op jit(solution)/shard_map/ppermute | solution.py:551
  (91 other events, 1777.3 us)
Sparse Core Ops, SparseCore 0:
  413.4 158.2 all-reduce.1
Sparse Core Ops, SparseCore 1:
  503.2 99.5 all-gather.3

commit v6 on v5

--- a/solution.py
+++ b/solution.py
@@ -2210,7 +2210,7 @@
     middle_sums(A)
     qkv_send, qkv_keep = grad_rows(chain, info[B], (tokens, tokens), (dqkv[A], dqkv[B]), after=(down_sum,))
     qkv_got = lax.ppermute(qkv_send, "dp", CORES)
-    line.add("qkv", qkv_keep, qkv_got, 3)
+    line.add("qkv", qkv_keep, qkv_got, 2)
     dx[A] = input_grad_own(A)
     dxx[A], dxy[A] = pair_swap(dx[A], dx[A])
     line.advance()
@@ -2241,9 +2241,8 @@
     finish_matrix("up", width, units)
     input_grad = plane_place(chain, info[B], B, (dx[B], dxx[B], dxy[B], *dxr[B]), tokens.shape, input_grad)
     line.advance()
+    begin_finish("qkv")
     sums = total_sum(chain, every_sum)
-    line.advance()
-    begin_finish("qkv")
     finish_matrix("qkv", width, qkv_weight.shape[1])
     line.advance()
     begin_finish("out")

time: 952 us -> 955 us (level)
  waiting for transfers between devices: 178 us -> 191 us
    ppermute x10 -> x9, waiting for transfers between devices: 108 us -> 123 us  [advance(): lax.ppermute(self.sent, 'obj', [(0, 1), (3, 2), (1, 0), (2, 3)])]
    ppermute x10 -> x9, starting transfers between devices: 44.5 us -> 39.3 us  [advance(): lax.ppermute(self.sent, 'obj', [(0, 1), (3, 2), (1, 0), (2, 3)])]
    pallas_call x64 -> x63, Pallas kernels: 600 us -> 597 us  [call(): pl.pallas_call(wrapped, grid_spec=grid_spec, out_shape=[jax.ShapeDtypeStr...]
  transfers between devices with their start and end apart: 89 -> 87, of which waited for: 27 -> 27; matrix products, arithmetic and copies ran while one was open for 2% -> 2% of each run, Pallas kernels for 60% -> 60%
where the time goes in v6:
time: 955 us; the launch traced here: 946 us
  Pallas kernels  597 us (63%)
  waiting for transfers between devices  191 us (20%)
  starting transfers between devices  115 us (12%)
  between operations  18.8 us (2%)
  local copies, waits for them, and re-layouts  17.8 us (2%)
    pallas_call x63, Pallas kernels, call(): pl.pallas_call(wrapped, grid_spec=grid_spec, out_shape=[jax.ShapeDtypeStr...  597 us
    ppermute x9, waiting for transfers between devices, advance(): lax.ppermute(self.sent, 'obj', [(0, 1), (3, 2), (1, 0), (2, 3)])  123 us
    ppermute x60, waiting for transfers between devices, swap(): return lax.ppermute(array, 'tensor', [(i, i ^ bit) for i in range(ways)])  63.3 us
    ppermute x60, starting transfers between devices, swap(): return lax.ppermute(array, 'tensor', [(i, i ^ bit) for i in range(ways)])  62.7 us
    ppermute x9, starting transfers between devices, advance(): lax.ppermute(self.sent, 'obj', [(0, 1), (3, 2), (1, 0), (2, 3)])  39.3 us
  transfers between devices with their start and end apart: 87, of which 27 were waited for; matrix products, arithmetic and copies ran while one was open for 2% of the time, Pallas kernels for 60%

profile of v6, /device:TPU:0, one launch (start us, length us, event | category | flops | bytes accessed | tf_op | source)
XLA Modules:
  0.0 946.1 jit_solution(15199768529457222396)
XLA Ops:
  22.5 20.9 %attn_fwd.2 = (bf16[1024,1536]{1,0:T(8,128)(2,1)}, bf16[1024,512]{1,0:T(8,128)(2,1)}, f32[4,1,1024]{2,1,0:T(1,128)}) custom-call(s32[4]{0:T(128)} %add_add_fusion.1.refs_0_, bf16[2,1024,2048]{2,1,0:T(8,128)(2,1)} %refs_2_.11, bf16[2048,1536]{1,0:T(8,128)(2,1)} %refs_3_.17, f32[1024,128]{1,0:T(8,128)} %constant.40.clone.refs_3_.refs_9_, ...), custom_call_target="tpu_custom_call" | custom-call | flops 210000003072 | bytes 1000000 | tf_op jit(solution)/shard_map/attn_fwd/pallas_call | solution.py:838
  53.2 21.0 %attn_fwd.3 = (bf16[1024,1536]{1,0:T(8,128)(2,1)}, bf16[1024,512]{1,0:T(8,128)(2,1)}, f32[4,1,1024]{2,1,0:T(1,128)}) custom-call(s32[4]{0:T(128)} %add_add_fusion.refs_0_, bf16[2,1024,2048]{2,1,0:T(8,128)(2,1)} %refs_2_.11, bf16[2048,1536]{1,0:T(8,128)(2,1)} %refs_3_.17, f32[1024,128]{1,0:T(8,128)} %constant.40.clone.refs_3_.refs_9_, ...), custom_call_target="tpu_custom_call" | custom-call | flops 210000003072 | bytes 1000000 | tf_op jit(solution)/shard_map/attn_fwd/pallas_call | solution.py:838
  105.3 21.1 %out_norm.2 = (bf16[1024,2048]{1,0:T(8,128)(2,1)}, f32[256,2048]{1,0:T(8,128)}, f32[256,128]{1,0:T(8,128)}) custom-call(s32[4]{0:T(128)} %add_add_fusion.1.refs_0_, s32[8]{0:T(128)} %stack.54.refs_1_.refs_0_, bf16[1024,512]{1,0:T(8,128)(2,1)} %get-tuple-element.147.refs_2_.refs_7_.refs_1_, ...), custom_call_target="tpu_custom_call" | custom-call | flops 210000003072 | bytes 1000000 | tf_op jit(solution)/shard_map/out_norm/pallas_call | solution.py:838
  132.6 30.1 %ffn_fwd.3 = (bf16[256,2048]{1,0:T(8,128)(2,1)}, bf16[256,2048]{1,0:T(8,128)(2,1)}, bf16[128,2048]{1,0:T(8,128)(2,1)}, bf16[128,2048]{1,0:T(8,128)(2,1)}, bf16[2...) custom-call(bf16[1024,2048]{1,0:T(8,128)(2,1)} %get-tuple-element.158, ...), custom_call_target="tpu_custom_call" | custom-call | flops 359999995904 | bytes 1000000 | tf_op jit(solution)/shard_map/ffn_fwd/pallas_call | solution.py:838
  165.1 21.4 %out_norm.3 = (bf16[1024,2048]{1,0:T(8,128)(2,1)}, f32[256,2048]{1,0:T(8,128)}, f32[256,128]{1,0:T(8,128)}) custom-call(s32[4]{0:T(128)} %add_add_fusion.refs_0_, s32[8]{0:T(128)} %stack.54.refs_1_.refs_0_, bf16[1024,512]{1,0:T(8,128)(2,1)} %get-tuple-element.156.refs_2_.refs_7_, bf16[1024,512]{1,0:T(8,128)(2,1)} %collective-permute-done.8.refs_0_.refs_3_.refs_8_, ...), custom_call_target="tpu_custom_call" | custom-call | flops 210000003072 | bytes 1000000 | tf_op jit(solution)/shard_map/out_norm/pallas_call | solution.py:838
  191.6 17.6 %ffn_fwd.4 = (bf16[256,2048]{1,0:T(8,128)(2,1)}, bf16[256,2048]{1,0:T(8,128)(2,1)}, bf16[1024,1408]{1,0:T(8,128)(2,1)}, bf16[1024,1408]{1,0:T(8,128)(2,1)}, bf16[1024,1408]{1,0:T(8,128)(2,1)}) custom-call(bf16[1024,2048]{1,0:T(8,128)(2,1)} %get-tuple-element.162.refs_4_.refs_0_.refs_2_, bf16[2048,1408]{1,0:T(8,128)(2,1)} %refs_4_.7, ...), custom_call_target="tpu_custom_call" | custom-call | flops 179999997952 | bytes 1000000 | tf_op jit(solution)/shard_map/ffn_fwd/pallas_call | solution.py:838
  216.4 17.8 %ffn_fwd.5 = (bf16[128,2048]{1,0:T(8,128)(2,1)}, bf16[128,2048]{1,0:T(8,128)(2,1)}, bf16[256,2048]{1,0:T(8,128)(2,1)}, bf16[256,2048]{1,0:T(8,128)(2,1)}, bf16[2...) custom-call(bf16[1024,2048]{1,0:T(8,128)(2,1)} %get-tuple-element.16, ...), custom_call_target="tpu_custom_call", output_to_operand_aliasing={{5}: (4, {}), {6}: (5, {}), {7}: (6, {}), {3}: (7, {}), {4}... | custom-call | flops 179999997952 | bytes 1000000 | tf_op jit(solution)/shard_map/ffn_fwd/pallas_call | solution.py:838
  254.2 14.5 %norm_two.2 = (bf16[2,1024,2048]{2,1,0:T(8,128)(2,1)}, f32[2,2048]{1,0:T(2,128)}, bf16[1024,2048]{1,0:T(8,128)(2,1)}) custom-call(s32[4]{0:T(128)} %add_add_fusion.1.refs_0_, s32[8]{0:T(128)} %stack.54.refs_1_.refs_0_, f32[1]{0:T(128)} %get-tuple-element.293.refs_2_, bf16[256,2048]{1,0:T(8,128)(2,1)} %resid_two.2.refs_9_.refs_3_, ...), custom_call_target="tpu_custom_call" | custom-call | flops 149999992832 | bytes 1000000 | tf_op jit(solution)/shard_map/norm_two/pallas_call | solution.py:838
  268.7 19.1 %ffn_bwd.3 = (bf16[256,2048]{1,0:T(8,128)(2,1)}, bf16[256,2048]{1,0:T(8,128)(2,1)}, bf16[1024,1408]{1,0:T(8,128)(2,1)}, bf16[1024,1408]{1,0:T(8,128)(2,1)}) custom-call(bf16[1024,2048]{1,0:T(8,128)(2,1)} %get-tuple-element.185.refs_0_.refs_5_.refs_2_, bf16[1024,1408]{1,0:T(8,128)(2,1)} %get-tuple-element.186.refs_1_, ...), custom_call_target="tpu_custom_call" | custom-call | flops 179999997952 | bytes 1000000 | tf_op jit(solution)/shard_map/ffn_bwd/pallas_call | solution.py:838
  294.9 19.3 %ffn_bwd.4 = (bf16[128,2048]{1,0:T(8,128)(2,1)}, bf16[128,2048]{1,0:T(8,128)(2,1)}, bf16[256,2048]{1,0:T(8,128)(2,1)}, bf16[1024,1408]{1,0:T(8,128)(2,1)}, bf16[1024,1408]{1,0:T(8,128)(2,1)}) custom-call(bf16[1024,2048]{1,0:T(8,128)(2,1)} %get-tuple-element.185.refs_0_.refs_5_.refs_2_, ...), custom_call_target="tpu_custom_call", output_to_operand_aliasing={{3}: (6, {}), {4}: (7, {})} | custom-call | flops 179999997952 | bytes 1000000 | tf_op jit(solution)/shard_map/ffn_bwd/pallas_call | solution.py:838
  330.4 19.3 %collective-permute-done.25.refs_0_.refs_4_ = bf16[256,2048]{1,0:T(8,128)(2,1)S(1)} collective-permute-done((bf16[256,2048]{1,0:T(8,128)(2,1)}, bf16[256,2048]{1,0:T(8,128)(2,1)S(1)}, u32[]{:S(2)}, u32[]{:S(2)}) %collective-permute-start.25) | collective-permute-done | bytes 1048608 | tf_op jit(solution)/shard_map/ppermute | solution.py:551
  373.5 14.4 %norm_two.3 = (bf16[2,1024,2048]{2,1,0:T(8,128)(2,1)}, f32[2,2048]{1,0:T(2,128)}, bf16[1024,2048]{1,0:T(8,128)(2,1)}) custom-call(s32[4]{0:T(128)} %add_add_fusion.refs_0_, s32[8]{0:T(128)} %stack.54.refs_1_.refs_0_, f32[1]{0:T(128)} %get-tuple-element.294.refs_2_, bf16[256,2048]{1,0:T(8,128)(2,1)} %resid_two.3.refs_4_.refs_3_, ...), custom_call_target="tpu_custom_call", output_to_operand_aliasing={{0}: (11, {})} | custom-call | flops 149999992832 | bytes 1000000 | tf_op jit(solution)/shard_map/norm_two/pallas_call | solution.py:838
  387.9 19.1 %grad_plain_columns.1.refs_2_ = bf16[1408,2048]{1,0:T(8,128)(2,1)} custom-call(bf16[1024,1408]{1,0:T(8,128)(2,1)} %get-tuple-element.209.refs_0_, bf16[1024,1408]{1,0:T(8,128)(2,1)} %get-tuple-element.210.refs_1_, bf16[1024,2048]{1,0:T(8,128)(2,1)} %get-tuple-element.185.refs_0_.refs_5_.refs_2_, ...), custom_call_target="tpu_custom_call" | custom-call | flops 190000005120 | bytes 1000000 | tf_op jit(solution)/shard_map/grad_plain_columns/pallas_call | solution.py:838
  413.2 32.7 %ffn_bwd.5 = (bf16[256,2048]{1,0:T(8,128)(2,1)}, bf16[256,2048]{1,0:T(8,128)(2,1)}, bf16[128,2048]{1,0:T(8,128)(2,1)}, bf16[128,2048]{1,0:T(8,128)(2,1)}, bf16[2...) custom-call(bf16[1024,2048]{1,0:T(8,128)(2,1)} %get-tuple-element.206.refs_3_.refs_0_.refs_5_, ...), custom_call_target="tpu_custom_call" | custom-call | flops 359999995904 | bytes 1000000 | tf_op jit(solution)/shard_map/ffn_bwd/pallas_call | solution.py:838
  447.1 20.6 %grad_rows.3 = (bf16[11,1024,128]{2,1,0:T(8,128)(2,1)}, bf16[11,1024,128]{2,1,0:T(8,128)(2,1)}) custom-call(s32[4]{0:T(128)} %add_add_fusion.refs_0_, bf16[1024,2048]{1,0:T(8,128)(2,1)} %get-tuple-element.158.refs_2_.refs_0_.refs_1_, bf16[1024,2048]{1,0:T(8,128)(2,1)} %get-tuple-element.162.refs_4_.refs_0_.refs_2_, ...), custom_call_target="tpu_custom_call" | custom-call | flops 210000003072 | bytes 1000000 | tf_op jit(solution)/shard_map/grad_rows/pallas_call | solution.py:838
  473.7 20.6 %grad_rows.4 = (bf16[11,1024,128]{2,1,0:T(8,128)(2,1)}, bf16[11,1024,128]{2,1,0:T(8,128)(2,1)}) custom-call(s32[4]{0:T(128)} %add_add_fusion.refs_0_, bf16[1024,2048]{1,0:T(8,128)(2,1)} %get-tuple-element.158.refs_2_.refs_0_.refs_1_, bf16[1024,2048]{1,0:T(8,128)(2,1)} %get-tuple-element.162.refs_4_.refs_0_.refs_2_, ...), custom_call_target="tpu_custom_call" | custom-call | flops 210000003072 | bytes 1000000 | tf_op jit(solution)/shard_map/grad_rows/pallas_call | solution.py:838
  507.0 23.9 %attn_bwd.2.refs_2_.refs_1_.refs_3_ = bf16[1024,1536]{1,0:T(8,128)(2,1)} custom-call(s32[4]{0:T(128)} %add_add_fusion.1.refs_0_, bf16[1024,1536]{1,0:T(8,128)(2,1)} %get-tuple-element.148.refs_2_.refs_1_, bf16[256,2048]{1,0:T(8,128)(2,1)} %get-tuple-element.204.refs_12_.refs_2_.refs_3_, bf16[256,2048]{1,0:T(8,128)(2,1)} %collective-permute-done.33.refs_0_.refs_3_.refs_4_, ...), custom_call_target="tpu_custom_call" | custom-call | flops 240000008192 | bytes 1000000 | tf_op jit(solution)/shard_map/attn_bwd/pallas_call | solution.py:838
  550.9 20.8 %collective-permute-done.47.refs_5_ = bf16[5632,128]{1,0:T(8,128)(2,1)} collective-permute-done((bf16[5632,128]{1,0:T(8,128)(2,1)}, bf16[5632,128]{1,0:T(8,128)(2,1)}, u32[]{:S(2)}, u32[]{:S(2)}) %collective-permute-start.47) | collective-permute-done | bytes 1441824 | tf_op jit(solution)/shard_map/ppermute | solution.py:1953
  579.6 23.9 %attn_bwd.3.refs_8_.refs_4_.refs_1_.refs_2_ = bf16[1024,1536]{1,0:T(8,128)(2,1)} custom-call(s32[4]{0:T(128)} %add_add_fusion.refs_0_, bf16[1024,1536]{1,0:T(8,128)(2,1)} %get-tuple-element.152.refs_4_.refs_1_, bf16[256,2048]{1,0:T(8,128)(2,1)} %get-tuple-element.227.refs_3_.refs_2_.refs_8_, ...), custom_call_target="tpu_custom_call" | custom-call | flops 240000008192 | bytes 1000000 | tf_op jit(solution)/shard_map/attn_bwd/pallas_call | solution.py:838
  629.9 21.0 %grad_rows.5 = (bf16[12,1024,128]{2,1,0:T(8,128)(2,1)}, bf16[12,1024,128]{2,1,0:T(8,128)(2,1)}) custom-call(s32[4]{0:T(128)} %add_add_fusion.refs_0_, bf16[2,1024,2048]{2,1,0:T(8,128)(2,1)} %refs_2_.11, bf16[2,1024,2048]{2,1,0:T(8,128)(2,1)} %refs_2_.11, bf16[1024,1536]{1,0:T(8,128)(2,1)} %attn_bwd.2.refs_2_.refs_1_.refs_3_, ...), custom_call_target="tpu_custom_call" | custom-call | flops 210000003072 | bytes 1000000 | tf_op jit(solution)/shard_map/grad_rows/pallas_call | solution.py:838
  696.5 15.1 %collective-permute-done.59.refs_5_.refs_8_ = bf16[5632,128]{1,0:T(8,128)(2,1)} collective-permute-done((bf16[5632,128]{1,0:T(8,128)(2,1)S(1)}, bf16[5632,128]{1,0:T(8,128)(2,1)}, u32[]{:S(2)}, u32[]{:S(2)}) %collective-permute-start.59) | collective-permute-done | bytes 1441824 | tf_op jit(solution)/shard_map/ppermute | solution.py:1953
  737.6 16.1 %collective-permute-done.65.refs_5_.refs_8_ = bf16[6144,128]{1,0:T(8,128)(2,1)S(1)} collective-permute-done((bf16[6144,128]{1,0:T(8,128)(2,1)}, bf16[6144,128]{1,0:T(8,128)(2,1)S(1)}, u32[]{:S(2)}, u32[]{:S(2)}) %collective-permute-start.65) | collective-permute-done | bytes 1572896 | tf_op jit(solution)/shard_map/ppermute | solution.py:1953
  775.1 23.2 %collective-permute-done.73.refs_5_.refs_8_ = bf16[6144,128]{1,0:T(8,128)(2,1)S(1)} collective-permute-done((bf16[6144,128]{1,0:T(8,128)(2,1)}, bf16[6144,128]{1,0:T(8,128)(2,1)S(1)}, u32[]{:S(2)}, u32[]{:S(2)}) %collective-permute-start.73) | collective-permute-done | bytes 1572896 | tf_op jit(solution)/shard_map/ppermute | solution.py:1953
  879.1 16.1 %collective-permute-done.81.refs_3_ = bf16[6144,128]{1,0:T(8,128)(2,1)} collective-permute-done((bf16[6144,128]{1,0:T(8,128)(2,1)}, bf16[6144,128]{1,0:T(8,128)(2,1)}, u32[]{:S(2)}, u32[]{:S(2)}) %collective-permute-start.81) | collective-permute-done | bytes 1572896 | tf_op jit(solution)/shard_map/ppermute | solution.py:1953
  (286 shorter events, 437.5 us)
Async XLA Ops:
  252.6 37.7 %collective-permute-start.21 = (bf16[256,2048]{1,0:T(8,128)(2,1)}, bf16[256,2048]{1,0:T(8,128)(2,1)}, u32[]{:S(2)}, u32[]{:S(2)}) collective-permute-start(bf16[256,2048]{1,0:T(8,128)(2,1)} %get-tuple-element.181), channel_id=1, source_target_pairs={{0,1},{1,0},{2,3},{3,2},{4,5},{5,4},{6,7},{7,6},{8,9},{9,8},{10,11... | collective-permute-start | bytes 3145736 | tf_op jit(solution)/shard_map/ppermute | solution.py:551
  367.9 39.8 %collective-permute-start.33 = (bf16[256,2048]{1,0:T(8,128)(2,1)}, bf16[256,2048]{1,0:T(8,128)(2,1)}, u32[]{:S(2)}, u32[]{:S(2)}) collective-permute-start(bf16[256,2048]{1,0:T(8,128)(2,1)} %get-tuple-element.204.refs_12_.refs_2_.refs_3_), channel_id=1, source_target_pairs={{0,1},{1,0},{2,3},{3,2},{4,5},{5,4},{6,7},{7,6},{8,9},{9,8},{10,11... | collective-permute-start | bytes 3145736 | tf_op jit(solution)/shard_map/ppermute | solution.py:551
  369.1 38.6 %collective-permute-start.34 = (bf16[256,2048]{1,0:T(8,128)(2,1)}, bf16[256,2048]{1,0:T(8,128)(2,1)}, u32[]{:S(2)}, u32[]{:S(2)}) collective-permute-start(bf16[256,2048]{1,0:T(8,128)(2,1)} %get-tuple-element.204.refs_12_.refs_2_.refs_3_), channel_id=1, source_target_pairs={{0,2},{1,3},{2,0},{3,1},{4,6},{5,7},{6,4},{7,5},{8,10},{9,11},{10,... | collective-permute-start | bytes 3145736 | tf_op jit(solution)/shard_map/ppermute | solution.py:551
  409.9 220.0 %all-reduce.2.cloned.1.call-start = ((), (), s32[]{:S(2)}) async-start(), calls=%async_computation | async-start | bytes 11534336 | tf_op jit(solution)/shard_map/psum | solution.py:2186
  410.6 490.9 %all-gather.4.cloned.1.call-start = ((), (), s32[]{:S(2)}) async-start(), calls=%async_computation.1 | async-start | bytes 1081344 | tf_op jit(solution)/shard_map/all_gather | solution.py:2239
  506.9 64.8 %collective-permute-start.47 = (bf16[5632,128]{1,0:T(8,128)(2,1)}, bf16[5632,128]{1,0:T(8,128)(2,1)}, u32[]{:S(2)}, u32[]{:S(2)}) collective-permute-start(bf16[5632,128]{1,0:T(8,128)(2,1)} %line_step.10.refs_13_), channel_id=1, source_target_pairs={{0,8},{24,16},{8,0},{16,24},{1,9},{25,17},{9,1},{17,25},{2,10},{26... | collective-permute-start | bytes 4325384 | tf_op jit(solution)/shard_map/ppermute | solution.py:1953
  549.7 72.8 %collective-permute-start.52 = (bf16[256,2048]{1,0:T(8,128)(2,1)}, bf16[256,2048]{1,0:T(8,128)(2,1)}, u32[]{:S(2)}, u32[]{:S(2)}) collective-permute-start(bf16[256,2048]{1,0:T(8,128)(2,1)} %get-tuple-element.233.refs_6_), channel_id=1, source_target_pairs={{0,1},{1,0},{2,3},{3,2},{4,5},{5,4},{6,7},{7,6},{8,9},{9,8},{10,11... | collective-permute-start | bytes 3145736 | tf_op jit(solution)/shard_map/ppermute | solution.py:551
  549.9 72.6 %collective-permute-start.53 = (bf16[256,2048]{1,0:T(8,128)(2,1)}, bf16[256,2048]{1,0:T(8,128)(2,1)}, u32[]{:S(2)}, u32[]{:S(2)}) collective-permute-start(bf16[256,2048]{1,0:T(8,128)(2,1)} %get-tuple-element.240), channel_id=1, source_target_pairs={{0,2},{1,3},{2,0},{3,1},{4,6},{5,7},{6,4},{7,5},{8,10},{9,11},{10,... | collective-permute-start | bytes 3145736 | tf_op jit(solution)/shard_map/ppermute | solution.py:551
  618.7 38.2 %collective-permute-start.50 = (bf16[5632,128]{1,0:T(8,128)(2,1)}, bf16[5632,128]{1,0:T(8,128)(2,1)}, u32[]{:S(2)}, u32[]{:S(2)}) collective-permute-start(bf16[5632,128]{1,0:T(8,128)(2,1)} %get-tuple-element.237.refs_4_.refs_9_), channel_id=1, source_target_pairs={{0,8},{24,16},{8,0},{16,24},{1,9},{25,17},{9,1},{17,25},{2,10},{26... | collective-permute-start | bytes 4325384 | tf_op jit(solution)/shard_map/ppermute | solution.py:1953
  684.3 40.0 %collective-permute-start.56 = (bf16[256,2048]{1,0:T(8,128)(2,1)}, bf16[256,2048]{1,0:T(8,128)(2,1)}, u32[]{:S(2)}, u32[]{:S(2)}) collective-permute-start(bf16[256,2048]{1,0:T(8,128)(2,1)} %get-tuple-element.249.refs_13_), channel_id=1, source_target_pairs={{0,1},{1,0},{2,3},{3,2},{4,5},{5,4},{6,7},{7,6},{8,9},{9,8},{10,11... | collective-permute-start | bytes 3145736 | tf_op jit(solution)/shard_map/ppermute | solution.py:551
  684.9 39.4 %collective-permute-start.57 = (bf16[256,2048]{1,0:T(8,128)(2,1)}, bf16[256,2048]{1,0:T(8,128)(2,1)}, u32[]{:S(2)}, u32[]{:S(2)}) collective-permute-start(bf16[256,2048]{1,0:T(8,128)(2,1)} %get-tuple-element.250), channel_id=1, source_target_pairs={{0,2},{1,3},{2,0},{3,1},{4,6},{5,7},{6,4},{7,5},{8,10},{9,11},{10,... | collective-permute-start | bytes 3145736 | tf_op jit(solution)/shard_map/ppermute | solution.py:551
  724.3 39.5 %collective-permute-start.67 = (bf16[4096,128]{1,0:T(8,128)(2,1)}, bf16[4096,128]{1,0:T(8,128)(2,1)}, u32[]{:S(2)}, u32[]{:S(2)}) collective-permute-start(bf16[4096,128]{1,0:T(8,128)(2,1)} %bitcast.51), channel_id=1, source_target_pairs={{0,4},{4,0},{1,5},{5,1},{2,6},{6,2},{3,7},{7,3},{8,12},{12,8},{9,1... | collective-permute-start | bytes 3145736 | tf_op jit(solution)/shard_map/ppermute | solution.py:2221
  727.3 40.6 %collective-permute-start.63 = (bf16[128,2048]{1,0:T(8,128)(2,1)}, bf16[128,2048]{1,0:T(8,128)(2,1)}, u32[]{:S(2)}, u32[]{:S(2)}) collective-permute-start(bf16[128,2048]{1,0:T(8,128)(2,1)} %get-tuple-element.258.refs_1_), channel_id=1, source_target_pairs={{0,1},{1,0},{2,3},{3,2},{4,5},{5,4},{6,7},{7,6},{8,9},{9,8},{10,11... | collective-permute-start | bytes 1572872 | tf_op jit(solution)/shard_map/ppermute | solution.py:551
  727.9 41.0 %collective-permute-start.64 = (bf16[128,2048]{1,0:T(8,128)(2,1)}, bf16[128,2048]{1,0:T(8,128)(2,1)}, u32[]{:S(2)}, u32[]{:S(2)}) collective-permute-start(bf16[128,2048]{1,0:T(8,128)(2,1)} %get-tuple-element.259), channel_id=1, source_target_pairs={{0,2},{1,3},{2,0},{3,1},{4,6},{5,7},{6,4},{7,5},{8,10},{9,11},{10,... | collective-permute-start | bytes 1572872 | tf_op jit(solution)/shard_map/ppermute | solution.py:551
  737.6 37.5 %collective-permute-start.72 = (bf16[11264,128]{1,0:T(8,128)(2,1)}, bf16[11264,128]{1,0:T(8,128)(2,1)}, u32[]{:S(2)}, u32[]{:S(2)}) collective-permute-start(bf16[11264,128]{1,0:T(8,128)(2,1)} %get-tuple-element.265), channel_id=1, source_target_pairs={{0,4},{4,0},{1,5},{5,1},{2,6},{6,2},{3,7},{7,3},{8,12},{12,8},{9,1... | collective-permute-start | bytes 8650760 | tf_op jit(solution)/shard_map/ppermute | solution.py:2163
  760.8 37.5 %collective-permute-start.73 = (bf16[6144,128]{1,0:T(8,128)(2,1)}, bf16[6144,128]{1,0:T(8,128)(2,1)S(1)}, u32[]{:S(2)}, u32[]{:S(2)}) collective-permute-start(bf16[6144,128]{1,0:T(8,128)(2,1)} %get-tuple-element.262.refs_2_.refs_9_), channel_id=1, source_target_pairs={{0,8},{24,16},{8,0},{16,24},{1,9},{25,17},{9,1},{17,25},{2,10},{26... | collective-permute-start | bytes 4718600 | tf_op jit(solution)/shard_map/ppermute | solution.py:1953
  767.9 51.3 %collective-permute-start.70 = (bf16[128,2048]{1,0:T(8,128)(2,1)}, bf16[128,2048]{1,0:T(8,128)(2,1)}, u32[]{:S(2)}, u32[]{:S(2)}) collective-permute-start(bf16[128,2048]{1,0:T(8,128)(2,1)} %get-tuple-element.263.refs_6_), channel_id=1, source_target_pairs={{0,2},{1,3},{2,0},{3,1},{4,6},{5,7},{6,4},{7,5},{8,10},{9,11},{10,... | collective-permute-start | bytes 1572872 | tf_op jit(solution)/shard_map/ppermute | solution.py:551
  773.4 53.0 %collective-permute-start.68 = (bf16[256,2048]{1,0:T(8,128)(2,1)}, bf16[256,2048]{1,0:T(8,128)(2,1)}, u32[]{:S(2)}, u32[]{:S(2)}) collective-permute-start(bf16[256,2048]{1,0:T(8,128)(2,1)} %input_grad.3.refs_11_.refs_1_), channel_id=1, source_target_pairs={{0,1},{1,0},{2,3},{3,2},{4,5},{5,4},{6,7},{7,6},{8,9},{9,8},{10,11... | collective-permute-start | bytes 3145736 | tf_op jit(solution)/shard_map/ppermute | solution.py:551
  775.1 51.3 %collective-permute-start.69 = (bf16[256,2048]{1,0:T(8,128)(2,1)}, bf16[256,2048]{1,0:T(8,128)(2,1)}, u32[]{:S(2)}, u32[]{:S(2)}) collective-permute-start(bf16[256,2048]{1,0:T(8,128)(2,1)} %input_grad.3.refs_11_.refs_1_), channel_id=1, source_target_pairs={{0,2},{1,3},{2,0},{3,1},{4,6},{5,7},{6,4},{7,5},{8,10},{9,11},{10,... | collective-permute-start | bytes 3145736 | tf_op jit(solution)/shard_map/ppermute | solution.py:551
  805.2 37.9 %collective-permute-start.78 = (bf16[6144,128]{1,0:T(8,128)(2,1)}, bf16[6144,128]{1,0:T(8,128)(2,1)}, u32[]{:S(2)}, u32[]{:S(2)}) collective-permute-start(bf16[6144,128]{1,0:T(8,128)(2,1)} %get-tuple-element.269.refs_3_.refs_7_), channel_id=1, source_target_pairs={{0,8},{24,16},{8,0},{16,24},{1,9},{25,17},{9,1},{17,25},{2,10},{26... | collective-permute-start | bytes 4718600 | tf_op jit(solution)/shard_map/ppermute | solution.py:1953
  821.1 42.9 %collective-permute-start.77 = (bf16[11264,128]{1,0:T(8,128)(2,1)}, bf16[11264,128]{1,0:T(8,128)(2,1)}, u32[]{:S(2)}, u32[]{:S(2)}) collective-permute-start(bf16[11264,128]{1,0:T(8,128)(2,1)} %get-tuple-element.272), channel_id=1, source_target_pairs={{0,4},{4,0},{1,5},{5,1},{2,6},{6,2},{3,7},{7,3},{8,12},{12,8},{9,1... | collective-permute-start | bytes 8650760 | tf_op jit(solution)/shard_map/ppermute | solution.py:2163
  828.6 45.1 %collective-permute-start.75 = (bf16[128,2048]{1,0:T(8,128)(2,1)}, bf16[128,2048]{1,0:T(8,128)(2,1)}, u32[]{:S(2)}, u32[]{:S(2)}) collective-permute-start(bf16[128,2048]{1,0:T(8,128)(2,1)} %get-tuple-element.270.refs_8_), channel_id=1, source_target_pairs={{0,2},{1,3},{2,0},{3,1},{4,6},{5,7},{6,4},{7,5},{8,10},{9,11},{10,... | collective-permute-start | bytes 1572872 | tf_op jit(solution)/shard_map/ppermute | solution.py:551
  829.5 44.2 %collective-permute-start.76 = (bf16[128,2048]{1,0:T(8,128)(2,1)}, bf16[128,2048]{1,0:T(8,128)(2,1)}, u32[]{:S(2)}, u32[]{:S(2)}) collective-permute-start(bf16[128,2048]{1,0:T(8,128)(2,1)} %get-tuple-element.271), channel_id=1, source_target_pairs={{0,1},{1,0},{2,3},{3,2},{4,5},{5,4},{6,7},{7,6},{8,9},{9,8},{10,11... | collective-permute-start | bytes 1572872 | tf_op jit(solution)/shard_map/ppermute | solution.py:551
  848.0 47.2 %collective-permute-start.81 = (bf16[6144,128]{1,0:T(8,128)(2,1)}, bf16[6144,128]{1,0:T(8,128)(2,1)}, u32[]{:S(2)}, u32[]{:S(2)}) collective-permute-start(bf16[6144,128]{1,0:T(8,128)(2,1)} %get-tuple-element.274.refs_3_.refs_4_), channel_id=1, source_target_pairs={{0,8},{24,16},{8,0},{16,24},{1,9},{25,17},{9,1},{17,25},{2,10},{26... | collective-permute-start | bytes 4718600 | tf_op jit(solution)/shard_map/ppermute | solution.py:1953
  (88 other events, 1781.3 us)
Sparse Core Ops, SparseCore 0:
  413.6 158.1 all-reduce.1
Sparse Core Ops, SparseCore 1:
  503.2 99.7 all-gather.3
